TPU v7x, 256 devices: a whole 4x4x8 slice. The times are simulated.
256 devices in a mesh: lon: 16 (over y_hi, z), lat: 4 (over x), mem: 4 (over y_lo, core).
Axes of the slice: x: 4, y: 4 (y_hi: 2, y_lo: 2; y = y_hi * 2 + y_lo), z: 8, core: 2. Of those that a mesh axis runs over, the one named last changes fastest.
Arguments:
- tracer: float32 [128, 8, 32, 2048], P('mem', None, 'lat', 'lon'), parts along dimension 0, may hold values from -3 to 3
- courant: float32 [2, 8, 32, 2048], P(None, None, 'lat', 'lon'), may hold values from -0.45 to 0.45
- mixing: float32 [7, 32, 2048], P(None, 'lat', 'lon'), may hold values from 0.1 to 10
- forcing: float32 [5, 196608], P(None, ('lon', 'lat')), may hold values from 0 to 1
- plant_type: int32 [196608], P(('lon', 'lat')), may hold values from 0 to 15
- land_params: float32 [3, 128, 16], P(None, 'mem'), parts along dimension 1, may hold values from 0 to 1
- send_slot: int32 [196608], P(('lon', 'lat')), may hold values from -1 to 4095, as said below
- recv_cell: int32 [4096, 64], P(('lon', 'lat')), may hold values from 0 to 1024, as said below
Outputs:
- tracer_next: float32 [128, 8, 32, 2048], P('mem', None, 'lat', 'lon'), parts along dimension 0
- surface_flux: float32 [128, 32, 2048], P('mem', 'lat', 'lon'), parts along dimension 0
There are 4 independent parts, one for each index of `mem`. A program takes and returns all parts, laid end to end along the dimension named above; an argument that names none is the same for every part. Nothing has to cross between parts.
Inputs may be any that keep to these rules, and one draw needn't show every extreme that they name: `send_slot`: -1 marks an empty column slot; otherwise the value is tile * 64 + place. Each device holds 1536 or more live columns and some device holds 3072. No two columns of one device share a tile and place, at most 64 columns of one device go to one tile, and that many are reached. A quarter of the tiles receive no columns. `recv_cell`: row t * 64 + d, place k gives the local cell (row * 128 + column) of tile t for the column that device d sends to that place, or 1024 where it sends none; it agrees with send_slot.
All inputs are finite; a program needn't handle non-finite values.
Results may differ from a plain program's by a relative error of at most 0.0003.
Values sent between devices are 32-bit elements; how exact they have to be, the bound alone decides.
No kernel may reach another device: no remote copies, remote signals or barrier semaphores. Data moves between devices by JAX's collectives and lax.ppermute only.
A program may use at most 64 MiB of HBM per device.

v0:
```python
import jax
import jax.numpy as jnp
from jax import lax
from jax.sharding import PartitionSpec as P

FLUX_SCALE = 0.02
GAS_CONSTANT = 8.314


def with_halo(cells, sides, width, closed):
    for axis, dim in sides:
        count = lax.axis_size(axis)
        ends = count if closed else count - 1
        head = lax.slice_in_dim(cells, 0, width, axis=dim)
        tail = lax.slice_in_dim(cells, cells.shape[dim] - width, cells.shape[dim], axis=dim)
        cells = jnp.concatenate(
            [
                lax.ppermute(tail, axis, [(i, (i + 1) % count) for i in range(ends)]),
                cells,
                lax.ppermute(head, axis, [((i + 1) % count, i) for i in range(ends)]),
            ],
            axis=dim,
        )
    return cells


def arrhenius(energy, leaf_temp):
    return jnp.exp(energy * (leaf_temp - 25.0) / (298.15 * GAS_CONSTANT * (leaf_temp + 273.15)))


def column_exchange(drivers, param_rows, bottom_tracer):
    light = 2000.0 * drivers[0]
    leaf_temp = 35.0 * drivers[1]
    water_factor = 0.2 + 0.8 * drivers[2]
    leaf_area = 0.5 + 5.5 * drivers[3]
    area_share = 0.05 + 0.55 * drivers[4]
    carbox_ref = 30.0 + 70.0 * param_rows[0]
    transport_ratio = 1.4 + 0.8 * param_rows[1]
    respiration_share = 0.005 + 0.025 * param_rows[2]
    carbon_leaf = 0.7 * (400.0 + 100.0 * bottom_tracer)
    carboxylation = carbox_ref * arrhenius(65330.0, leaf_temp) * water_factor
    transport_max = transport_ratio * carbox_ref * arrhenius(43540.0, leaf_temp)
    michaelis_carbon = 404.9 * arrhenius(79430.0, leaf_temp)
    michaelis_oxygen = 278.4 * arrhenius(36380.0, leaf_temp)
    compensation = 42.75 * arrhenius(37830.0, leaf_temp)
    absorbed = 0.425 * light
    total_rate = absorbed + transport_max
    electron_rate = (
        total_rate - jnp.sqrt(total_rate * total_rate - 2.8 * absorbed * transport_max)
    ) / 1.4
    rubisco_rate = (
        carboxylation
        * (carbon_leaf - compensation)
        / (carbon_leaf + michaelis_carbon * (1.0 + 210.0 / michaelis_oxygen))
    )
    light_rate = (
        electron_rate * (carbon_leaf - compensation) / (4.0 * carbon_leaf + 8.0 * compensation)
    )
    gross_rate = jnp.minimum(rubisco_rate, light_rate)
    canopy_scale = (1.0 - jnp.exp(-0.5 * leaf_area)) / 0.5
    return (
        -FLUX_SCALE * area_share * canopy_scale * (gross_rate - respiration_share * carboxylation)
    )


def member_params(land_params, plant_type):
    type_count = land_params.shape[2]
    members = land_params.shape[1]
    type_onehot = (
        lax.broadcasted_iota(jnp.int32, (type_count, plant_type.shape[0]), 0) == plant_type[None, :]
    ).astype(jnp.float32)
    param_table = land_params.reshape(3 * members, type_count)
    picked = jnp.dot(
        param_table,
        type_onehot,
        precision=lax.Precision.HIGHEST,
        preferred_element_type=jnp.float32,
    )
    return picked.reshape(3, members, plant_type.shape[0])


def select_columns(values, index):
    span = values.shape[1]
    return jnp.take(values, jnp.minimum(index, span - 1), axis=1)


def place_columns(values, index, span):
    return jnp.zeros((values.shape[0], span), jnp.float32).at[:, index].add(values, mode="drop")


def window(array_in, start_at, count, dimension):
    return lax.slice_in_dim(array_in, start_at, start_at + count, axis=dimension)


def flux_divergence(padded, courant_pad, dimension):
    extent = padded.shape[dimension] - 6
    edge_values = 7.0 / 12.0 * (
        window(padded, 1, extent + 3, dimension) + window(padded, 2, extent + 3, dimension)
    ) - 1.0 / 12.0 * (
        window(padded, 0, extent + 3, dimension) + window(padded, 3, extent + 3, dimension)
    )
    left_low = window(edge_values, 0, extent + 1, dimension)
    left_high = window(edge_values, 1, extent + 1, dimension)
    right_high = window(edge_values, 2, extent + 1, dimension)
    left_mean = window(padded, 2, extent + 1, dimension)
    right_mean = window(padded, 3, extent + 1, dimension)
    face_courant = window(courant_pad, 2, extent + 1, dimension)
    slope_left = left_high - left_low
    curve_left = 6.0 * (left_mean - 0.5 * (left_low + left_high))
    slope_right = right_high - left_high
    curve_right = 6.0 * (right_mean - 0.5 * (left_high + right_high))
    from_left = left_high - 0.5 * face_courant * (
        slope_left - (1.0 - 2.0 / 3.0 * face_courant) * curve_left
    )
    from_right = left_high - 0.5 * face_courant * (
        slope_right + (1.0 + 2.0 / 3.0 * face_courant) * curve_right
    )
    fluxes = face_courant * jnp.where(face_courant > 0, from_left, from_right)
    return window(fluxes, 1, extent, dimension) - window(fluxes, 0, extent, dimension)


def implicit_mixing(rhs_field, coefficient):
    layers = rhs_field.shape[-3]
    ratios = []
    sweep_values = []
    for layer_index in range(layers):
        weight_below = (
            coefficient[layer_index - 1] if layer_index > 0 else jnp.zeros_like(coefficient[0])
        )
        weight_above = (
            coefficient[layer_index] if layer_index < layers - 1 else jnp.zeros_like(coefficient[0])
        )
        pivot_value = 1.0 + weight_below + weight_above
        carried = rhs_field[..., layer_index, :, :]
        if layer_index > 0:
            pivot_value = pivot_value - weight_below * ratios[-1]
            carried = carried + weight_below * sweep_values[-1]
        ratios.append(weight_above / pivot_value)
        sweep_values.append(carried / pivot_value)
    solved = [sweep_values[-1]]
    for layer_index in range(layers - 2, -1, -1):
        solved.insert(0, sweep_values[layer_index] + ratios[layer_index] * solved[0])
    return jnp.stack(solved, axis=-3)


def per_device(tracer, courant, mixing, forcing, plant_type, land_params, send_slot, recv_cell):
    members, levels, row_count, column_count = tracer.shape
    row_ids = lax.axis_index("lat") * row_count + lax.broadcasted_iota(
        jnp.int32, (1, 1, row_count, 1), 2
    )
    north_edge = row_ids == row_count * lax.axis_size("lat") - 1
    wind_east = courant[0:1]
    wind_north = jnp.where(north_edge, 0.0, courant[1:2])
    stacked = jnp.concatenate([tracer, wind_east, wind_north], axis=0)
    east_west = with_halo(stacked, (("lon", 3),), 3, True)
    north_south = with_halo(stacked, (("lat", 2),), 3, False)
    advected = (
        tracer
        - flux_divergence(east_west[:members], east_west[members : members + 1], 3)
        - flux_divergence(north_south[:members], north_south[members + 1 : members + 2], 2)
    )
    tile_count = lax.axis_size("lon") * lax.axis_size("lat")
    slot_count = recv_cell.shape[1]
    place_count = tile_count * slot_count
    cell_count = row_count * column_count
    bottom = tracer[:, 0].reshape(members, cell_count)
    recv_flat = recv_cell.reshape(place_count)
    send_place = jnp.where(send_slot >= 0, send_slot, place_count)
    picked = select_columns(bottom, recv_flat)
    at_land = lax.all_to_all(picked, ("lon", "lat"), split_axis=1, concat_axis=1, tiled=True)
    bottom_tracer = select_columns(at_land, send_place)
    column_flux = column_exchange(forcing, member_params(land_params, plant_type), bottom_tracer)
    outgoing = place_columns(column_flux, send_place, place_count)
    incoming = lax.all_to_all(outgoing, ("lon", "lat"), split_axis=1, concat_axis=1, tiled=True)
    surface = place_columns(incoming, recv_flat, cell_count)
    surface = surface.reshape(members, row_count, column_count)
    forced = advected.at[:, 0].add(surface)
    tracer_next = implicit_mixing(forced, mixing)
    return (tracer_next, surface)


def solution(mesh):
    in_specs = (
        P("mem", None, "lat", "lon"),
        P(None, None, "lat", "lon"),
        P(None, "lat", "lon"),
        P(None, ("lon", "lat")),
        P(("lon", "lat")),
        P(None, "mem", None),
        P(("lon", "lat")),
        P(("lon", "lat"), None),
    )
    out_specs = (P("mem", None, "lat", "lon"), P("mem", "lat", "lon"))
    return jax.shard_map(
        per_device, mesh=mesh, in_specs=in_specs, out_specs=out_specs, check_vma=False
    )
```

profile of v0, /device:TPU:2, one launch (start us, length us, event | category | flops | bytes accessed | tf_op | source)
XLA Modules:
  0.0 187.5 jit_solution(18000289044353384233)
XLA Ops:
  0.6 0.8 fusion.74
  1.4 1.4 copy.117
  3.1 1.4 fusion.72
  4.5 2.6 %copy.101 = f32[34,8,8,3]{0,2,3,1:T(8,128)} copy(f32[34,8,8,3]{3,1,2,0:T(8,128)} %get-tuple-element.57) | data formatting | bytes 52224 | tf_op jit(solution)/shard_map/slice | solution.py:15
  7.1 1.9 %collective-permute-start = (f32[34,8,8,3]{0,2,3,1:T(8,128)}, f32[34,8,8,3]{0,2,3,1:T(8,128)}, u32[]{:S(2)}, u32[]{:S(2)}) collective-permute-start(f32[34,8,8,3]{0,2,3,1:T(8,128)} %copy.101), channel_id=1, source_target_pairs={{0,16},{16,32},{32,48},{48,64},{64,80},{80,96},{96,112},{112,128},... | collective-permute-start | bytes 78344 | tf_op jit(solution)/shard_map/ppermute | solution.py:18
  9.0 1.4 copy.107
  10.4 6.6 %collective-permute-start.1 = (f32[34,8,8,3]{0,2,3,1:T(8,128)}, f32[34,8,8,3]{0,2,3,1:T(8,128)S(1)}, u32[]{:S(2)}, u32[]{:S(2)}) collective-permute-start(f32[34,8,8,3]{0,2,3,1:T(8,128)} %copy.107), channel_id=1, source_target_pairs={{16,0},{32,16},{48,32},{64,48},{80,64},{96,80},{112,96},{128,112},... | collective-permute-start | bytes 78344 | tf_op jit(solution)/shard_map/ppermute | solution.py:20
  17.0 1.0 fusion.73
  18.0 3.4 %collective-permute-start.2 = (f32[34,8,3,128]{3,1,2,0:T(8,128)}, f32[34,8,3,128]{3,1,2,0:T(8,128)}, u32[]{:S(2)}, u32[]{:S(2)}) collective-permute-start(f32[34,8,3,128]{3,1,2,0:T(8,128)} %get-tuple-element.61), channel_id=1, source_target_pairs={{0,4},{4,8},{8,12},{1,5},{5,9},{9,13},{2,6},{6,10},{10,14},{3,7},{... | collective-permute-start | bytes 1253384 | tf_op jit(solution)/shard_map/ppermute | solution.py:18
  21.4 3.2 %collective-permute-start.3 = (f32[34,8,3,128]{3,1,2,0:T(8,128)}, f32[34,8,3,128]{3,1,2,0:T(8,128)}, u32[]{:S(2)}, u32[]{:S(2)}) collective-permute-start(f32[34,8,3,128]{3,1,2,0:T(8,128)} %get-tuple-element.62), channel_id=1, source_target_pairs={{4,0},{8,4},{12,8},{5,1},{9,5},{13,9},{6,2},{10,6},{14,10},{7,3},{... | collective-permute-start | bytes 1253384 | tf_op jit(solution)/shard_map/ppermute | solution.py:20
  24.7 0.6 compare_select_fusion
  25.3 0.2 copy.119
  25.5 14.2 %gather_fusion = f32[4096,32]{1,0:T(8,128)} fusion(f32[32,1024]{0,1:T(8,128)S(1)} %bitcast.106, s32[4096]{0:T(1024)S(1)} %broadcast_clamp_fusion), kind=kCustom, calls=%fused_computation | custom fusion | bytes 1064960 | tf_op jit(solution)/shard_map/jit(_take)/gather | solution.py:84
  39.7 2.2 %copy.120 = f32[32,64,64]{2,0,1:T(8,128)S(1)} copy(f32[32,64,64]{0,2,1:T(8,128)} %bitcast.114) | data formatting | bytes 1048576 | tf_op jit(solution)/shard_map/jit(_take)/gather | solution.py:84
  42.1 1.4 reshape.185
  43.6 9.3 %all-to-all-start = ((f32[64,1,2048]{2,1,0:T(1,128)}), f32[64,1,2048]{2,1,0:T(1,128)}, u32[]{:S(2)}, u32[]{:S(2)}) async-start(f32[64,1,2048]{2,1,0:T(1,128)} %reshape.185), calls=%async_computation | async-start | bytes 1048576 | tf_op jit(solution)/shard_map/all_to_all | solution.py:170
  52.9 0.6 fusion.54
  53.6 0.8 multiply_multiply_fusion
  54.5 0.6 fusion.58
  55.2 0.6 slice_bitcast_fusion
  55.8 0.6 fusion.60
  56.4 0.6 fusion.61
  57.0 0.6 fusion.62
  57.7 1.7 convolution_bitcast_fusion
  59.3 0.6 subtract_bitcast_fusion
  59.9 2.0 %copy.102 = f32[34,8,8,3]{3,1,2,0:T(8,128)S(1)} copy(f32[34,8,8,3]{0,2,3,1:T(8,128)} %collective-permute-done) | data formatting | bytes 52224 | tf_op jit(solution)/shard_map/ppermute | solution.py:18
  62.0 1.1 copy.109
  63.1 0.8 maximum_maximum_fusion
  63.9 0.9 pad_maximum_fusion
  65.0 1.2 fusion.11
  66.1 3.1 %fusion.5 = f32[32,8,8,129]{3,1,2,0:T(8,128)} fusion(f32[34,8,8,131]{3,1,2,0:T(8,128)S(1)} %get-tuple-element.56, f32[34,8,8,131]{3,1,2,0:T(8,128)S(1)} %get-tuple-element.55, f32[32,8,8,131]{3,1,2,0:T(8,128)S(1)} %fusion.11, f32[8,8,129]{2,0,1:T(8,128)S(1)} %get-tuple-element.74, f32[8,8,129]{2,0,1:T(8,128)S(1)} %get-tuple-element.73, ...), kind=kLoop, calls=%fused_computation.14 | loop fusion | flops 4755456 | bytes 6480960 | tf_op jit(solution)/shard_map/mul | solution.py:118
  69.2 1.3 compare_bitcast_fusion.1
  70.5 2.6 %pad_maximum_fusion.2 = f32[34,8,14,128]{3,1,2,0:T(8,128)} fusion(f32[34,8,3,128]{3,1,2,0:T(8,128)} %collective-permute-done.3, f32[1,8,8,128]{3,1,2,0:T(8,128)S(1)} %copy_select_fusion, f32[1,8,8,128]{3,1,2,0:T(8,128)S(1)} %copy.136, f32[32,8,8,128]{3,1,2,0:T(8,128)S(1)} %copy.117, f32[34,8,3,128]{3,1,2,0:T(8,128)} %collective-permute-done.2), kind=kLoop, calls=%fused_computation.25 | loop fusion | flops 1949696 | bytes 3899392 | tf_op jit(solution)/shard_map/concatenate | solution.py:16
  73.1 3.0 %maximum_maximum_fusion.1 = (f32[34,8,11,128]{3,1,2,0:T(8,128)}, f32[34,8,11,128]{3,1,2,0:T(8,128)}) fusion(f32[1,8,8,128]{3,1,2,0:T(8,128)S(1)} %copy_select_fusion, f32[1,8,8,128]{3,1,2,0:T(8,128)S(1)} %copy.136, f32[32,8,8,128]{3,1,2,0:T(8,128)S(1)} %copy.117, f32[34,8,3,128]{3,1,2,0:T(8,128)} %collective-permute-done.2, ...), kind=kLoop, calls=%fused_computation.26 | loop fusion | flops 2297856 | bytes 5013504 | tf_op jit(solution)/shard_map/concatenate | solution.py:16
  76.1 0.6 multiply_bitcast_fusion.5
  76.7 0.6 broadcast.543
  77.3 3.0 %reduce.2 = f32[64,2048]{1,0:T(8,128)S(1)} reduce(f32[64,1,2048]{2,1,0:T(1,128)} %all-to-all-done, f32[]{:T(128)} %broadcast.543), dimensions={1}, to_apply=%all_to_all.14.reduce_sub_computation | reduce | bytes 1048580 | tf_op jit(solution)/shard_map/all_to_all | solution.py:170
  80.3 0.4 reshape.186
  80.7 0.6 copy.121
  81.5 10.9 %gather_fusion.1 = f32[3072,32]{1,0:T(8,128)} fusion(f32[32,4096]{0,1:T(8,128)S(1)} %bitcast.107, s32[3072]{0:T(1024)S(1)} %copy-done.18), kind=kCustom, calls=%fused_computation.1 | custom fusion | bytes 798720 | tf_op jit(solution)/shard_map/jit(_take)/gather | solution.py:84
  92.4 1.8 copy.122
  94.3 0.6 fusion.34
  94.8 0.5 copy.123
  95.3 18.7 %scatter_custom_fusion = f32[32,4096]{0,1:T(8,128)} fusion(s32[3072]{0:T(1024)} %get-tuple-element.96, f32[3072,32]{1,0:T(8,128)S(1)} %copy.123, f32[]{:T(128)} %constant.55.clone.1), kind=kCustom, calls=%fused_computation.50 | custom fusion | flops 98304 | bytes 524800 | tf_op jit(solution)/shard_map/scatter-add | solution.py:88
  114.0 3.3 %copy.124 = f32[32,64,64]{2,0,1:T(8,128)} copy(f32[32,64,64]{0,2,1:T(8,128)} %bitcast.108) | data formatting | bytes 1048576 | tf_op jit(solution)/shard_map/all_to_all | solution.py:174
  117.3 2.8 %reshape.187 = f32[64,1,2048]{2,1,0:T(1,128)} reshape(f32[64,32,64]{2,1,0:T(8,128)} %bitcast.112) | data formatting | bytes 1048576
  120.1 13.0 %all-to-all-start.1 = ((f32[64,1,2048]{2,1,0:T(1,128)}), f32[64,1,2048]{2,1,0:T(1,128)}, u32[]{:S(2)}, u32[]{:S(2)}) async-start(f32[64,1,2048]{2,1,0:T(1,128)} %reshape.187), calls=%async_computation.1 | async-start | bytes 1048576 | tf_op jit(solution)/shard_map/all_to_all | solution.py:174
  133.2 1.8 fusion.14
  135.1 0.7 fusion.21
  135.8 0.8 copy-done.3
  136.6 0.3 copy-done.4
  136.9 0.6 fusion.26
  137.5 12.2 %all-to-all-done.1 = f32[64,1,2048]{2,1,0:T(1,128)} async-done(((f32[64,1,2048]{2,1,0:T(1,128)}), f32[64,1,2048]{2,1,0:T(1,128)}, u32[]{:S(2)}, u32[]{:S(2)}) %all-to-all-start.1) | async-done | bytes 524320 | tf_op jit(solution)/shard_map/all_to_all | solution.py:174
  149.7 3.0 %reduce.3 = f32[64,2048]{1,0:T(8,128)S(1)} reduce(f32[64,1,2048]{2,1,0:T(1,128)} %all-to-all-done.1, f32[]{:T(128)} %broadcast.543), dimensions={1}, to_apply=%all_to_all.17.reduce_sub_computation | reduce | bytes 1048580 | tf_op jit(solution)/shard_map/all_to_all | solution.py:174
  152.6 0.4 reshape.188
  153.1 0.6 copy.125
  153.7 0.4 reshape.172
  154.2 2.0 %copy.126 = f32[4096,32]{1,0:T(8,128)} copy(f32[4096,32]{0,1:T(8,128)S(1)} %bitcast.115) | data formatting | bytes 1048576 | tf_op jit(solution)/shard_map/all_to_all | solution.py:174
  156.1 23.0 %scatter_custom_fusion.1 = f32[32,1024]{0,1:T(8,128)S(1)} fusion(s32[4096]{0:T(1024)} %bitcast.133, f32[4096,32]{1,0:T(8,128)} %copy.126, f32[]{:T(128)} %constant.55.clone.1), kind=kCustom, calls=%fused_computation.70 | custom fusion | flops 131072 | bytes 131584 | tf_op jit(solution)/shard_map/scatter-add | solution.py:88
  179.5 1.1 fusion.43
  180.7 2.1 %multiply_add_fusion = (f32[32,1,8,128]{3,1,2,0:T(1,128)S(1)}, f32[32,1,8,128]{3,1,2,0:T(1,128)S(1)}, f32[32,1,8,128]{3,1,2,0:T(1,128)S(1)}, f32[32,1,8,128]{3,1...) fusion(f32[32,1,8,128]{3,1,2,0:T(1,128)S(1)} %get-tuple-element, ...), kind=kLoop, calls=%fused_computation.89 | loop fusion | flops 557056 | bytes 2134016 | tf_op jit(solution)/shard_map/add | solution.py:142
  182.8 2.7 %stack.2 = f32[32,8,8,128]{3,1,2,0:T(8,128)S(1)} concatenate(f32[32,1,8,128]{3,1,2,0:T(1,128)S(1)} %get-tuple-element.24, f32[32,1,8,128]{3,1,2,0:T(1,128)S(1)} %get-tuple-element.25, f32[32,1,8,128]{3,1,2,0:T(1,128)S(1)} %get-tuple-element.26, f32[32,1,8,128]{3,1,2,0:T(1,128)S(1)} %get-tuple-element.27, f32[32,1,8,128]{3,1,2,0:T(1,128)S(1)} %get-tuple-element.28, ...), dimensions={1} | concatenate | bytes 2097152 | tf_op jit(solution)/shard_map/stack | solution.py:143
  185.5 1.2 copy.128
  186.7 0.8 copy.129
  (110 shorter events, 1.2 us)
Async XLA Ops:
  4.5 20.1 %copy-start.9 = (s32[64,64]{1,0:T(8,128)S(1)}, s32[64,64]{1,0:T(8,128)}, u32[]{:S(2)}) copy-start(s32[64,64]{1,0:T(8,128)} %param.17) | copy-start | bytes 49156
  7.1 18.2 %slice-start = ((f32[32,8,8,128]{3,2,1,0:T(8,128)}), f32[32,1,8,128]{3,2,1,0:T(8,128)S(1)}, s32[]{:S(2)}) async-start(f32[32,8,8,128]{3,2,1,0:T(8,128)} %param.10), calls=%async_computation.2 | async-start | bytes 262144 | tf_op jit(solution)/shard_map/slice | solution.py:166
  7.1 52.8 %collective-permute-start = (f32[34,8,8,3]{0,2,3,1:T(8,128)}, f32[34,8,8,3]{0,2,3,1:T(8,128)}, u32[]{:S(2)}, u32[]{:S(2)}) collective-permute-start(f32[34,8,8,3]{0,2,3,1:T(8,128)} %copy.101), channel_id=1, source_target_pairs={{0,16},{16,32},{32,48},{48,64},{64,80},{80,96},{96,112},{112,128},... | collective-permute-start | bytes 78344 | tf_op jit(solution)/shard_map/ppermute | solution.py:18
  10.4 51.5 %collective-permute-start.1 = (f32[34,8,8,3]{0,2,3,1:T(8,128)}, f32[34,8,8,3]{0,2,3,1:T(8,128)S(1)}, u32[]{:S(2)}, u32[]{:S(2)}) collective-permute-start(f32[34,8,8,3]{0,2,3,1:T(8,128)} %copy.107), channel_id=1, source_target_pairs={{16,0},{32,16},{48,32},{64,48},{80,64},{96,80},{112,96},{128,112},... | collective-permute-start | bytes 78344 | tf_op jit(solution)/shard_map/ppermute | solution.py:20
  18.0 51.2 %collective-permute-start.2 = (f32[34,8,3,128]{3,1,2,0:T(8,128)}, f32[34,8,3,128]{3,1,2,0:T(8,128)}, u32[]{:S(2)}, u32[]{:S(2)}) collective-permute-start(f32[34,8,3,128]{3,1,2,0:T(8,128)} %get-tuple-element.61), channel_id=1, source_target_pairs={{0,4},{4,8},{8,12},{1,5},{5,9},{9,13},{2,6},{6,10},{10,14},{3,7},{... | collective-permute-start | bytes 1253384 | tf_op jit(solution)/shard_map/ppermute | solution.py:18
  21.4 49.1 %collective-permute-start.3 = (f32[34,8,3,128]{3,1,2,0:T(8,128)}, f32[34,8,3,128]{3,1,2,0:T(8,128)}, u32[]{:S(2)}, u32[]{:S(2)}) collective-permute-start(f32[34,8,3,128]{3,1,2,0:T(8,128)} %get-tuple-element.62), channel_id=1, source_target_pairs={{4,0},{8,4},{12,8},{5,1},{9,5},{13,9},{6,2},{10,6},{14,10},{7,3},{... | collective-permute-start | bytes 1253384 | tf_op jit(solution)/shard_map/ppermute | solution.py:20
  41.9 11.0 %copy-start.17 = (s32[3072]{0:T(1024)S(1)}, s32[3072]{0:T(1024)}, u32[]{:S(2)}) copy-start(s32[3072]{0:T(1024)} %param.16) | copy-start | bytes 36868
  42.1 11.5 %copy-start.19 = (f32[5,3072]{1,0:T(8,128)S(1)}, f32[5,3072]{1,0:T(8,128)}, u32[]{:S(2)}) copy-start(f32[5,3072]{1,0:T(8,128)} %param.13) | copy-start | bytes 184324
  42.1 12.3 %copy-start.31 = (f32[3,32,16]{1,2,0:T(8,128)S(1)}, f32[3,32,16]{1,2,0:T(8,128)}, u32[]{:S(2)}) copy-start(f32[3,32,16]{1,2,0:T(8,128)} %param.15) | copy-start | bytes 18436
  42.1 12.4 %copy-start.6 = (f32[7,8,128]{2,1,0:T(8,128)S(1)}, f32[7,8,128]{2,1,0:T(8,128)}, u32[]{:S(2)}) copy-start(f32[7,8,128]{2,1,0:T(8,128)} %param.12) | copy-start | bytes 86020
  42.1 15.5 %copy-start.44 = (s32[3072]{0:T(1024)S(1)}, s32[3072]{0:T(1024)}, u32[]{:S(2)}) copy-start(s32[3072]{0:T(1024)} %param.14) | copy-start | bytes 36868
  43.6 33.1 %all-to-all-start = ((f32[64,1,2048]{2,1,0:T(1,128)}), f32[64,1,2048]{2,1,0:T(1,128)}, u32[]{:S(2)}, u32[]{:S(2)}) async-start(f32[64,1,2048]{2,1,0:T(1,128)} %reshape.185), calls=%async_computation | async-start | bytes 1048576 | tf_op jit(solution)/shard_map/all_to_all | solution.py:170
  55.2 0.6 copy-start.26
  55.8 0.6 copy-start.28
  56.4 7.5 %copy-start.20 = (f32[1,8,128]{2,1,0:T(8,128)}, f32[1,8,128]{2,1,0:T(8,128)S(1)}, u32[]{:S(2)}) copy-start(f32[1,8,128]{2,1,0:T(8,128)S(1)} %get-tuple-element.37) | copy-start | bytes 12292
  57.0 6.9 %copy-start.22 = (f32[1,8,128]{2,1,0:T(8,128)}, f32[1,8,128]{2,1,0:T(8,128)S(1)}, u32[]{:S(2)}) copy-start(f32[1,8,128]{2,1,0:T(8,128)S(1)} %get-tuple-element.39) | copy-start | bytes 12292
  57.7 4.3 %copy-start.24 = (f32[1,8,128]{2,1,0:T(8,128)}, f32[1,8,128]{2,1,0:T(8,128)S(1)}, u32[]{:S(2)}) copy-start(f32[1,8,128]{2,1,0:T(8,128)S(1)} %get-tuple-element.41) | copy-start | bytes 12292
  80.7 0.7 copy-start.18
  81.4 12.8 %copy-start.5 = (f32[96,3072]{1,0:T(8,128)S(1)}, f32[96,3072]{1,0:T(8,128)}, u32[]{:S(2)}) copy-start(f32[96,3072]{1,0:T(8,128)} %convolution_bitcast_fusion) | copy-start | bytes 3538948
  81.4 12.8 %copy-start.10 = (f32[1,3072]{1,0:T(1,128)S(1)}, f32[1,3072]{1,0:T(1,128)}, u32[]{:S(2)}) copy-start(f32[1,3072]{1,0:T(1,128)} %get-tuple-element.64) | copy-start | bytes 36868
  81.4 12.8 %copy-start.11 = (f32[1,3072]{1,0:T(1,128)S(1)}, f32[1,3072]{1,0:T(1,128)}, u32[]{:S(2)}) copy-start(f32[1,3072]{1,0:T(1,128)} %get-tuple-element.65) | copy-start | bytes 36868
  81.4 12.8 %copy-start.12 = (f32[1,3072]{1,0:T(1,128)S(1)}, f32[1,3072]{1,0:T(1,128)}, u32[]{:S(2)}) copy-start(f32[1,3072]{1,0:T(1,128)} %get-tuple-element.66) | copy-start | bytes 36868
  81.4 12.8 %copy-start.13 = (f32[1,3072]{1,0:T(1,128)S(1)}, f32[1,3072]{1,0:T(1,128)}, u32[]{:S(2)}) copy-start(f32[1,3072]{1,0:T(1,128)} %get-tuple-element.68) | copy-start | bytes 36868
  81.4 12.8 %copy-start.14 = (f32[1,3072]{1,0:T(1,128)S(1)}, f32[1,3072]{1,0:T(1,128)}, u32[]{:S(2)}) copy-start(f32[1,3072]{1,0:T(1,128)} %get-tuple-element.69) | copy-start | bytes 36868
  81.4 12.8 %copy-start.15 = (f32[1,3072]{1,0:T(1,128)S(1)}, f32[1,3072]{1,0:T(1,128)}, u32[]{:S(2)}) copy-start(f32[1,3072]{1,0:T(1,128)} %get-tuple-element.70) | copy-start | bytes 36868
  81.4 12.8 %copy-start.16 = (f32[1,3072]{1,0:T(1,128)S(1)}, f32[1,3072]{1,0:T(1,128)}, u32[]{:S(2)}) copy-start(f32[1,3072]{1,0:T(1,128)} %get-tuple-element.71) | copy-start | bytes 36868
  114.0 19.1 %copy-start.1 = (f32[34,8,11,128]{3,1,2,0:T(8,128)S(1)}, f32[34,8,11,128]{3,1,2,0:T(8,128)}, u32[]{:S(2)}) copy-start(f32[34,8,11,128]{3,1,2,0:T(8,128)} %get-tuple-element.59) | copy-start | bytes 4595716
  117.3 15.8 %copy-start = (f32[34,8,14,128]{3,1,2,0:T(8,128)S(1)}, f32[34,8,14,128]{3,1,2,0:T(8,128)}, u32[]{:S(2)}) copy-start(f32[34,8,14,128]{3,1,2,0:T(8,128)} %pad_maximum_fusion.2) | copy-start | bytes 5849092
  120.1 29.5 %all-to-all-start.1 = ((f32[64,1,2048]{2,1,0:T(1,128)}), f32[64,1,2048]{2,1,0:T(1,128)}, u32[]{:S(2)}, u32[]{:S(2)}) async-start(f32[64,1,2048]{2,1,0:T(1,128)} %reshape.187), calls=%async_computation.1 | async-start | bytes 1048576 | tf_op jit(solution)/shard_map/all_to_all | solution.py:174
  133.1 1.9 copy-start.2
  133.1 1.9 copy-start.7
  133.2 1.9 copy-start.8
  133.2 1.9 copy-start.30
  135.0 1.6 copy-start.3
  135.1 1.8 copy-start.4
  154.0 25.3 %copy-start.21 = (f32[1,8,128]{2,1,0:T(8,128)S(1)}, f32[1,8,128]{2,1,0:T(8,128)}, u32[]{:S(2)}) copy-start(f32[1,8,128]{2,1,0:T(8,128)} %copy-done.20) | copy-start | bytes 12292
  154.0 25.4 %copy-start.23 = (f32[1,8,128]{2,1,0:T(8,128)S(1)}, f32[1,8,128]{2,1,0:T(8,128)}, u32[]{:S(2)}) copy-start(f32[1,8,128]{2,1,0:T(8,128)} %copy-done.22) | copy-start | bytes 12292
  154.0 25.4 %copy-start.25 = (f32[1,8,128]{2,1,0:T(8,128)S(1)}, f32[1,8,128]{2,1,0:T(8,128)}, u32[]{:S(2)}) copy-start(f32[1,8,128]{2,1,0:T(8,128)} %copy-done.24) | copy-start | bytes 12292
  154.1 25.4 %copy-start.27 = (f32[1,8,128]{2,1,0:T(8,128)S(1)}, f32[1,8,128]{2,1,0:T(8,128)}, u32[]{:S(2)}) copy-start(f32[1,8,128]{2,1,0:T(8,128)} %copy-done.26) | copy-start | bytes 12292
  154.1 25.4 %copy-start.29 = (f32[1,8,128]{2,1,0:T(8,128)S(1)}, f32[1,8,128]{2,1,0:T(8,128)}, u32[]{:S(2)}) copy-start(f32[1,8,128]{2,1,0:T(8,128)} %copy-done.28) | copy-start | bytes 12292
  154.1 25.4 %copy-start.36 = (f32[8,128]{1,0:T(8,128)S(1)}, f32[8,128]{1,0:T(8,128)}, u32[]{:S(2)}) copy-start(f32[8,128]{1,0:T(8,128)} %get-tuple-element.81) | copy-start | bytes 12292
  154.1 25.4 %copy-start.37 = (f32[8,128]{1,0:T(8,128)S(1)}, f32[8,128]{1,0:T(8,128)}, u32[]{:S(2)}) copy-start(f32[8,128]{1,0:T(8,128)} %get-tuple-element.84) | copy-start | bytes 12292
  154.1 25.4 %copy-start.38 = (f32[8,128]{1,0:T(8,128)S(1)}, f32[8,128]{1,0:T(8,128)}, u32[]{:S(2)}) copy-start(f32[8,128]{1,0:T(8,128)} %get-tuple-element.85) | copy-start | bytes 12292
  154.1 25.4 %copy-start.39 = (f32[8,128]{1,0:T(8,128)S(1)}, f32[8,128]{1,0:T(8,128)}, u32[]{:S(2)}) copy-start(f32[8,128]{1,0:T(8,128)} %get-tuple-element.86) | copy-start | bytes 12292
  154.1 25.4 %copy-start.40 = (f32[8,128]{1,0:T(8,128)S(1)}, f32[8,128]{1,0:T(8,128)}, u32[]{:S(2)}) copy-start(f32[8,128]{1,0:T(8,128)} %get-tuple-element.88) | copy-start | bytes 12292
  154.1 25.4 %copy-start.41 = (f32[8,128]{1,0:T(8,128)S(1)}, f32[8,128]{1,0:T(8,128)}, u32[]{:S(2)}) copy-start(f32[8,128]{1,0:T(8,128)} %get-tuple-element.90) | copy-start | bytes 12292
  154.1 25.4 %copy-start.42 = (f32[8,128]{1,0:T(8,128)S(1)}, f32[8,128]{1,0:T(8,128)}, u32[]{:S(2)}) copy-start(f32[8,128]{1,0:T(8,128)} %get-tuple-element.91) | copy-start | bytes 12292
  154.1 25.4 %copy-start.43 = (f32[8,128]{1,0:T(8,128)S(1)}, f32[8,128]{1,0:T(8,128)}, u32[]{:S(2)}) copy-start(f32[8,128]{1,0:T(8,128)} %get-tuple-element.92) | copy-start | bytes 12292
  156.1 24.5 %copy-start.32 = (f32[8,128]{1,0:T(8,128)S(1)}, f32[8,128]{1,0:T(8,128)}, u32[]{:S(2)}) copy-start(f32[8,128]{1,0:T(8,128)} %get-tuple-element.32) | copy-start | bytes 12292
  156.1 24.5 %copy-start.33 = (f32[8,128]{1,0:T(8,128)S(1)}, f32[8,128]{1,0:T(8,128)}, u32[]{:S(2)}) copy-start(f32[8,128]{1,0:T(8,128)} %get-tuple-element.36) | copy-start | bytes 12292
  156.1 24.5 %copy-start.34 = (f32[8,128]{1,0:T(8,128)S(1)}, f32[8,128]{1,0:T(8,128)}, u32[]{:S(2)}) copy-start(f32[8,128]{1,0:T(8,128)} %get-tuple-element.38) | copy-start | bytes 12292
  156.1 24.5 %copy-start.35 = (f32[8,128]{1,0:T(8,128)S(1)}, f32[8,128]{1,0:T(8,128)}, u32[]{:S(2)}) copy-start(f32[8,128]{1,0:T(8,128)} %get-tuple-element.40) | copy-start | bytes 12292
where the time goes:
time: 190 us; the launch traced here: 188 us
  other arithmetic  74.3 us (39%)
  local copies, waits for them, and re-layouts  60.5 us (32%)
  starting transfers between devices  37.4 us (20%)
  waiting for transfers between devices  12.2 us (6%)
    scatter-add x2, other arithmetic, place_columns(): jnp.zeros((values.shape[0], span), jnp.float32).at[:, index]  41.7 us
    gather x4, local copies, waits for them, and re-layouts, select_columns(): return jnp.take(values, jnp.minimum(index, span - 1), axis=1)  29.1 us
    all_to_all x1, starting transfers between devices, per_device(): lax.all_to_all(outgoing, ('lon', 'lat'), split_axis=1, concat_axis=1, til...  13 us
    all_to_all x1, waiting for transfers between devices, per_device(): lax.all_to_all(outgoing, ('lon', 'lat'), split_axis=1, concat_axis=1, til...  12.2 us
    unnamed x99, local copies, waits for them, and re-layouts  9.9 us
    ppermute x2, starting transfers between devices, with_halo(): lax.ppermute(head, axis, [((i + 1) % count, i) for i in range(ends)])  9.76 us
    all_to_all x1, starting transfers between devices, per_device(): lax.all_to_all(picked, ('lon', 'lat'), split_axis=1, concat_axis=1, tiled...  9.32 us
    concatenate x4, other arithmetic, with_halo(): jnp.concatenate([lax.ppermute(tail, axis, [(i, (i + 1) % count) for i in...  7.25 us
  transfers between devices with their start and end apart: 6, of which 1 were waited for; matrix products, arithmetic and copies ran while one was open for 26% of the time, Pallas kernels for 0%

commit v1 on v0

v1 whole, which is shorter than its diff:
```python
import functools

import jax
import jax.numpy as jnp
from jax import lax
from jax.experimental import pallas as pl
from jax.experimental.pallas import tpu as pltpu
from jax.sharding import PartitionSpec as P

FLUX_SCALE = 0.02
GAS_CONSTANT = 8.314
LANES = 128
ROWS = 8
VMEM_BYTES = 40 * 2**20


def nt_dot(left, right):
    return lax.dot_general(
        left, right, (((1,), (1,)), ((), ())), preferred_element_type=jnp.float32
    )


def bf16_parts(values, count):
    parts = []
    rest = values
    for _ in range(count):
        part = rest.astype(jnp.bfloat16)
        rest = rest - part.astype(jnp.float32)
        parts.append(part)
    return parts


def column_kernel(forcing_ref, type_ref, slot_ref, out_ref):
    columns = slot_ref.shape[1]
    tiles = out_ref.shape[0]
    places = 64
    slot = slot_ref[...]
    tile = jnp.right_shift(slot, 6)
    place = jnp.bitwise_and(slot, places - 1)
    light = forcing_ref[0:1, :]
    leaf_temp = forcing_ref[1:2, :]
    water = forcing_ref[2:3, :]
    leaf_area = 0.5 + 5.5 * forcing_ref[3:4, :]
    area_share = 0.05 + 0.55 * forcing_ref[4:5, :]
    canopy_scale = (1.0 - jnp.exp(-0.5 * leaf_area)) / 0.5
    flux_scale = -FLUX_SCALE * area_share * canopy_scale
    plant = type_ref[...].astype(jnp.float32)

    tile_onehot = (
        lax.broadcasted_iota(jnp.int32, (tiles, columns), 0) == tile
    ).astype(jnp.float32).astype(jnp.bfloat16)
    place_ids = lax.broadcasted_iota(jnp.int32, (LANES, columns), 0)
    first_half = (place_ids == place).astype(jnp.float32).astype(jnp.bfloat16)
    second_half = (place_ids == place + places).astype(jnp.float32).astype(jnp.bfloat16)

    def spread(values, count):
        return [
            tile_onehot * jnp.broadcast_to(part, (tiles, columns))
            for part in bf16_parts(values, count)
        ]

    first = jnp.concatenate(spread(light, 3) + spread(water, 3) + spread(plant, 1), axis=0)
    second = jnp.concatenate(spread(leaf_temp, 3) + spread(flux_scale, 3), axis=0)
    from_first = nt_dot(first, first_half)
    from_second = nt_dot(second, second_half)

    def part_sum(values, start, count):
        total = values[start * tiles : (start + 1) * tiles]
        for step in range(1, count):
            total = total + values[(start + step) * tiles : (start + step + 1) * tiles]
        return total

    out_ref[:, 0, 0:LANES] = part_sum(from_first, 0, 3) + part_sum(from_second, 0, 3)
    out_ref[:, 0, LANES : 2 * LANES] = part_sum(from_first, 3, 3) + part_sum(from_second, 3, 3)
    out_ref[:, 0, 2 * LANES : 3 * LANES] = part_sum(from_first, 6, 1)


def pack_columns(forcing, plant_type, send_slot, tiles):
    columns = send_slot.shape[0]
    return pl.pallas_call(
        column_kernel,
        out_shape=jax.ShapeDtypeStruct((tiles, 1, 3 * LANES), jnp.float32),
        compiler_params=pltpu.CompilerParams(vmem_limit_bytes=VMEM_BYTES),
        cost_estimate=pl.CostEstimate(flops=2 * 448 * columns * 256, bytes_accessed=300000, transcendentals=columns),
        name="pack_columns",
    )(forcing, plant_type.reshape(1, columns), send_slot.reshape(1, columns))


def halo_kernel(tracer_ref, courant_ref, low_ref, high_ref, side_ref):
    blocks = tracer_ref.shape[0] // ROWS
    levels = courant_ref.shape[0] // (2 * ROWS)
    for step in range(3):
        low_ref[step * blocks : (step + 1) * blocks, :] = tracer_ref[
            pl.ds(step, blocks, stride=ROWS), :
        ]
        high_ref[step * blocks : (step + 1) * blocks, :] = tracer_ref[
            pl.ds(ROWS - 3 + step, blocks, stride=ROWS), :
        ]
    high_ref[3 * blocks : 3 * blocks + levels, :] = courant_ref[
        pl.ds(levels * ROWS + ROWS - 1, levels, stride=ROWS), :
    ]
    slot_of_lane = lax.broadcasted_iota(jnp.int32, (ROWS, LANES), 1) // 8

    def merge(read, count):
        total = jnp.zeros((ROWS, LANES), jnp.float32)
        for slot in range(count):
            moved = pltpu.roll(read(slot), 3 + 8 * slot, 1)
            total = jnp.where(slot_of_lane == slot, moved, total)
        return total

    def step(group, carry):
        def read(slot):
            start = pl.multiple_of((group * 16 + slot) * ROWS, ROWS)
            return tracer_ref[pl.ds(start, ROWS), :]

        side_ref[pl.ds(pl.multiple_of(group * ROWS, ROWS), ROWS), :] = merge(read, 16)
        return carry

    lax.fori_loop(0, blocks // 16, step, 0)
    side_ref[blocks // 2 : blocks // 2 + ROWS, :] = merge(
        lambda slot: courant_ref[slot * ROWS : (slot + 1) * ROWS, :], levels
    )


def pack_halos(tracer_rows, courant_rows):
    blocks = tracer_rows.shape[0] // ROWS
    levels = courant_rows.shape[0] // (2 * ROWS)
    return pl.pallas_call(
        halo_kernel,
        out_shape=(
            jax.ShapeDtypeStruct((3 * blocks, LANES), jnp.float32),
            jax.ShapeDtypeStruct((3 * blocks + levels, LANES), jnp.float32),
            jax.ShapeDtypeStruct((blocks // 2 + ROWS, LANES), jnp.float32),
        ),
        compiler_params=pltpu.CompilerParams(vmem_limit_bytes=VMEM_BYTES),
        cost_estimate=pl.CostEstimate(flops=1000000, bytes_accessed=2000000, transcendentals=0),
        name="pack_halos",
    )(tracer_rows, courant_rows)


def face_weights(face_courant):
    half = 0.5 * face_courant
    upwind = face_courant > 0
    shrink_left = 1.0 - 2.0 / 3.0 * face_courant
    shrink_right = 1.0 + 2.0 / 3.0 * face_courant
    curve = half * jnp.where(upwind, shrink_left, shrink_right)
    middle = face_courant * jnp.where(upwind, 1.0 - half - 3.0 * curve, 1.0 + half + 3.0 * curve)
    left_edge = face_courant * jnp.where(upwind, half - 3.0 * curve, 0.0)
    right_edge = face_courant * jnp.where(upwind, 0.0, 3.0 * curve - half)
    left_cell = face_courant * jnp.where(upwind, 6.0 * curve, 0.0)
    right_cell = face_courant * jnp.where(upwind, 0.0, -6.0 * curve)
    near, far = 7.0 / 12.0, 1.0 / 12.0
    return [
        -far * left_edge,
        near * left_edge - far * middle,
        near * (middle + left_edge) - far * right_edge + left_cell,
        near * (middle + right_edge) - far * left_edge + right_cell,
        near * right_edge - far * middle,
        -far * right_edge,
    ]


def divergence_weights(face_after, face_before):
    after = face_weights(face_after)
    before = face_weights(face_before)
    taps = []
    for offset in range(7):
        if offset == 0:
            taps.append(-before[0])
        elif offset == 6:
            taps.append(after[5])
        else:
            taps.append(after[offset - 1] - before[offset])
    return taps


def advect_kernel(
    lat_ref, tracer_ref, courant_ref, mixing_ref, south_ref, north_ref, west_ref, east_ref,
    out_ref, response_ref, rows_ref, side_ref, weight_ref, pivot_ref,
):
    levels = mixing_ref.shape[0] + 1
    members = tracer_ref.shape[0]
    blocks = members * levels
    lat = lat_ref[0]
    first = lat == 0
    last = lat == lat_ref[1] - 1
    zero = jnp.zeros((blocks, LANES), jnp.float32)
    for step in range(3):
        span = slice(step * blocks, (step + 1) * blocks)
        rows_ref[pl.ds(ROWS - 3 + step, blocks, stride=ROWS), :] = jnp.where(
            first, zero, south_ref[span, :]
        )
        rows_ref[pl.ds(step, blocks, stride=ROWS), :] = jnp.where(last, zero, north_ref[span, :])
    lane = lax.broadcasted_iota(jnp.int32, (ROWS, LANES), 1)
    row = lax.broadcasted_iota(jnp.int32, (ROWS, LANES), 0)
    from_west = lane % 8 < 3
    for group in range(blocks // 16):
        span = slice(group * ROWS, (group + 1) * ROWS)
        side_ref[span, :] = jnp.where(from_west, west_ref[span, :], east_ref[span, :])

    side_courant = west_ref[blocks // 2 : blocks // 2 + ROWS, :]
    for level in range(levels):
        east_face = courant_ref[0, level]
        west_cell = pltpu.roll(side_courant, LANES - 3 - 8 * level, 1)
        west_face = pltpu.roll(jnp.where(lane == LANES - 1, west_cell, east_face), 1, 1)
        north_face = courant_ref[1, level]
        below = jnp.where(first, 0.0, south_ref[3 * blocks + level : 3 * blocks + level + 1, :])
        south_face = jnp.where(row == 0, below, pltpu.roll(north_face, 1, 0))
        north_face = jnp.where(jnp.logical_and(last, row == ROWS - 1), 0.0, north_face)
        along_lon = divergence_weights(east_face, west_face)
        along_lat = divergence_weights(north_face, south_face)
        weight_ref[level, 0] = 1.0 - along_lon[3] - along_lat[3]
        for place, offset in enumerate((0, 1, 2, 4, 5, 6)):
            weight_ref[level, 1 + place] = -along_lon[offset]
            weight_ref[level, 7 + place] = -along_lat[offset]

    ratio = None
    response = []
    for level in range(levels):
        pivot = jnp.ones((ROWS, LANES), jnp.float32)
        if level > 0:
            pivot = pivot + mixing_ref[level - 1]
        if level < levels - 1:
            pivot = pivot + mixing_ref[level]
        if level > 0:
            pivot = pivot - mixing_ref[level - 1] * ratio
        inverse = 1.0 / pivot
        carried = inverse
        if level > 0:
            carried = mixing_ref[level - 1] * inverse
            response.append(carried * response[-1])
        else:
            response.append(inverse)
        pivot_ref[level, 0] = inverse
        pivot_ref[level, 1] = carried
        if level < levels - 1:
            ratio = mixing_ref[level] * inverse
            pivot_ref[level, 2] = ratio
    for level in range(levels - 1, -1, -1):
        if level < levels - 1:
            response[level] = response[level] + pivot_ref[level, 2] * response[level + 1]
        response_ref[level] = response[level]

    together = 4

    def member_step(index, carry):
        start = index * together
        swept = [None] * together
        for level in range(levels):
            for step in range(together):
                member = start + step
                inside = (step % 2) * levels + level
                group = index * (together * levels // 16) + step * levels // 16
                cells = tracer_ref[member, level]
                side = side_ref[pl.ds(pl.multiple_of(group * ROWS, ROWS), ROWS), :]
                side = pltpu.roll(side, LANES - 3 - 8 * inside, 1)
                edge = rows_ref[
                    pl.ds(pl.multiple_of((member * levels + level) * ROWS, ROWS), ROWS), :
                ]
                total = weight_ref[level, 0] * cells
                for place, shift in enumerate((3, 2, 1)):
                    padded = jnp.where(lane >= LANES - shift, side, cells)
                    total = total + weight_ref[level, 1 + place] * pltpu.roll(padded, shift, 1)
                for place, shift in enumerate((1, 2, 3)):
                    padded = jnp.where(lane < shift, side, cells)
                    total = total + weight_ref[level, 4 + place] * pltpu.roll(
                        padded, LANES - shift, 1
                    )
                for place, shift in enumerate((3, 2, 1)):
                    padded = jnp.where(row >= ROWS - shift, edge, cells)
                    total = total + weight_ref[level, 7 + place] * pltpu.roll(padded, shift, 0)
                for place, shift in enumerate((1, 2, 3)):
                    padded = jnp.where(row < shift, edge, cells)
                    total = total + weight_ref[level, 10 + place] * pltpu.roll(
                        padded, ROWS - shift, 0
                    )
                total = total * pivot_ref[level, 0]
                if level > 0:
                    total = total + pivot_ref[level, 1] * swept[step]
                swept[step] = total
                out_ref[member, level] = total
        for level in range(levels - 2, -1, -1):
            for step in range(together):
                member = start + step
                swept[step] = out_ref[member, level] + pivot_ref[level, 2] * swept[step]
                out_ref[member, level] = swept[step]
        return carry

    lax.fori_loop(0, members // together, member_step, 0)


def advect_and_mix(lat_place, tracer, courant, mixing, south, north, west, east):
    members, levels, rows, lanes = tracer.shape
    blocks = members * levels
    vmem = pl.BlockSpec(memory_space=pltpu.VMEM)
    return pl.pallas_call(
        advect_kernel,
        out_shape=(
            jax.ShapeDtypeStruct(tracer.shape, jnp.float32),
            jax.ShapeDtypeStruct((levels, rows, lanes), jnp.float32),
        ),
        in_specs=[pl.BlockSpec(memory_space=pltpu.SMEM)] + [vmem] * 7,
        out_specs=(vmem, vmem),
        scratch_shapes=[
            pltpu.VMEM((blocks * ROWS, LANES), jnp.float32),
            pltpu.VMEM((blocks // 2, LANES), jnp.float32),
            pltpu.VMEM((levels, 13, ROWS, LANES), jnp.float32),
            pltpu.VMEM((levels, 3, ROWS, LANES), jnp.float32),
        ],
        compiler_params=pltpu.CompilerParams(vmem_limit_bytes=VMEM_BYTES),
        cost_estimate=pl.CostEstimate(flops=12000000, bytes_accessed=4000000, transcendentals=0),
        name="advect_and_mix",
    )(lat_place, tracer, courant, mixing, south, north, west, east)


def arrhenius(energy, leaf_temp):
    return jnp.exp(energy * (leaf_temp - 25.0) / (298.15 * GAS_CONSTANT * (leaf_temp + 273.15)))


def flux_kernel(
    received_ref, cell_ref, params_ref, bottom_ref, partial_ref, response_ref,
    out_ref, surface_ref, table_ref, bottom_rows_ref, column_ref, index_ref, left_ref, right_ref,
):
    members = params_ref.shape[1]
    types = params_ref.shape[2]
    sources, places = cell_ref.shape
    groups = sources // 2
    levels = response_ref.shape[0]

    carbox = 30.0 + 70.0 * params_ref[0]
    table_ref[0, :, 0:types] = carbox
    table_ref[1, :, 0:types] = (1.4 + 0.8 * params_ref[1]) * carbox
    table_ref[2, :, 0:types] = (0.005 + 0.025 * params_ref[2]) * carbox
    for row in range(ROWS):
        bottom_rows_ref[row] = 0.7 * (400.0 + 100.0 * bottom_ref[:, 0, row, :])

    half = lax.broadcasted_iota(jnp.int32, (groups, LANES), 1) < places

    def pair(values):
        low, high = values[0:groups], values[groups : 2 * groups]
        return (
            jnp.where(half, low, pltpu.roll(high, places, 1)),
            jnp.where(half, pltpu.roll(low, places, 1), high),
        )

    light, leaf_temp = pair(received_ref[:, 0, 0:LANES])
    water, flux_scale = pair(received_ref[:, 0, LANES : 2 * LANES])
    plant, _ = pair(received_ref[:, 0, 2 * LANES : 3 * LANES])
    leaf_temp = 35.0 * leaf_temp
    column_ref[0] = 0.425 * (2000.0 * light)
    column_ref[1] = arrhenius(65330.0, leaf_temp) * (0.2 + 0.8 * water)
    column_ref[2] = arrhenius(43540.0, leaf_temp)
    michaelis_carbon = 404.9 * arrhenius(79430.0, leaf_temp)
    michaelis_oxygen = 278.4 * arrhenius(36380.0, leaf_temp)
    column_ref[3] = michaelis_carbon * (1.0 + 210.0 / michaelis_oxygen)
    column_ref[4] = 42.75 * arrhenius(37830.0, leaf_temp)
    column_ref[5] = flux_scale
    index_ref[0] = plant.astype(jnp.int32)
    cells = cell_ref[...]
    cells = jnp.concatenate([cells[0:groups], cells[groups : 2 * groups]], axis=1)
    index_ref[1] = jnp.right_shift(cells, 7)
    index_ref[2] = jnp.bitwise_and(cells, LANES - 1)

    lane_ids = lax.broadcasted_iota(jnp.int32, (LANES, LANES), 0)

    def group_step(group, carry):
        def spread(ref, quantity):
            return jnp.broadcast_to(ref[quantity, pl.ds(group, 1), :], (members, LANES))

        plant_index = spread(index_ref, 0)
        row_index = spread(index_ref, 1)
        lane_index = spread(index_ref, 2)

        def pick(table, index):
            return jnp.take_along_axis(table, index, axis=1, mode="promise_in_bounds")

        carbon_leaf = pick(bottom_rows_ref[0], lane_index)
        for row in range(1, ROWS):
            carbon_leaf = jnp.where(
                row_index == row, pick(bottom_rows_ref[row], lane_index), carbon_leaf
            )
        absorbed = spread(column_ref, 0)
        warm = spread(column_ref, 1)
        carboxylation = pick(table_ref[0], plant_index) * warm
        transport_max = pick(table_ref[1], plant_index) * spread(column_ref, 2)
        respiration = pick(table_ref[2], plant_index) * warm
        compensation = spread(column_ref, 4)
        total_rate = absorbed + transport_max
        electron_rate = (
            total_rate - jnp.sqrt(total_rate * total_rate - 2.8 * absorbed * transport_max)
        ) / 1.4
        excess = carbon_leaf - compensation
        rubisco_rate = carboxylation * excess / (carbon_leaf + spread(column_ref, 3))
        light_rate = electron_rate * excess / (4.0 * carbon_leaf + 8.0 * compensation)
        flux = spread(column_ref, 5) * (jnp.minimum(rubisco_rate, light_rate) - respiration)
        high, low = bf16_parts(flux, 2)
        span = pl.ds(pl.multiple_of(group * LANES, LANES), LANES)
        zero = jnp.zeros((members, LANES), jnp.bfloat16)
        for row in range(ROWS):
            here = (row_index == row).astype(jnp.float32).astype(jnp.bfloat16)
            left_ref[pl.ds(row * 2 * members, members), span] = high * here
            left_ref[pl.ds(row * 2 * members + members, members), span] = low * here
        lane_row = index_ref[2, pl.ds(group, 1), :]
        right_ref[:, span] = (lane_ids == lane_row).astype(jnp.float32).astype(jnp.bfloat16)
        return carry

    lax.fori_loop(0, groups, group_step, 0)
    summed = nt_dot(left_ref[...], right_ref[...])
    for row in range(ROWS):
        start = row * 2 * members
        surface_ref[:, row, :] = (
            summed[start : start + members] + summed[start + members : start + 2 * members]
        )

    def member_step(member, carry):
        surface = surface_ref[member]
        for level in range(levels):
            out_ref[member, level] = partial_ref[member, level] + response_ref[level] * surface
        return carry

    lax.fori_loop(0, members, member_step, 0, unroll=2)


def fluxes(received, recv_cell, land_params, tracer, partial, response):
    members, levels, rows, lanes = tracer.shape
    tiles = received.shape[0]
    place_count = recv_cell.shape[0] * recv_cell.shape[1]

    def whole(array):
        return pl.BlockSpec(array.shape, lambda step: (0,) * array.ndim)

    return pl.pallas_call(
        flux_kernel,
        out_shape=(
            jax.ShapeDtypeStruct(tracer.shape, jnp.float32),
            jax.ShapeDtypeStruct((members, rows, lanes), jnp.float32),
        ),
        in_specs=[
            whole(received),
            whole(recv_cell),
            whole(land_params),
            pl.BlockSpec((members, 1, rows, lanes), lambda step: (0, 0, 0, 0)),
            whole(partial),
            whole(response),
        ],
        out_specs=(
            pl.BlockSpec(tracer.shape, lambda step: (0, 0, 0, 0)),
            pl.BlockSpec((members, rows, lanes), lambda step: (0, 0, 0)),
        ),
        grid=(1,),
        scratch_shapes=[
            pltpu.VMEM((3, members, LANES), jnp.float32),
            pltpu.VMEM((ROWS, members, LANES), jnp.float32),
            pltpu.VMEM((6, tiles // 2, LANES), jnp.float32),
            pltpu.VMEM((3, tiles // 2, LANES), jnp.int32),
            pltpu.VMEM((2 * ROWS * members, place_count), jnp.bfloat16),
            pltpu.VMEM((LANES, place_count), jnp.bfloat16),
        ],
        compiler_params=pltpu.CompilerParams(vmem_limit_bytes=VMEM_BYTES),
        cost_estimate=pl.CostEstimate(flops=600000000, bytes_accessed=3000000, transcendentals=400000),
        name="fluxes",
    )(received, recv_cell, land_params, tracer, partial, response)


def per_device(tracer, courant, mixing, forcing, plant_type, land_params, send_slot, recv_cell):
    members, levels, row_count, column_count = tracer.shape
    lon_count, lat_count = lax.axis_size("lon"), lax.axis_size("lat")
    low, high, side = pack_halos(
        tracer.reshape(members * levels * row_count, column_count),
        courant.reshape(2 * levels * row_count, column_count),
    )
    north = lax.ppermute(low, "lat", [((i + 1) % lat_count, i) for i in range(lat_count)])
    south = lax.ppermute(high, "lat", [(i, (i + 1) % lat_count) for i in range(lat_count)])
    west = lax.ppermute(side, "lon", [(i, (i + 1) % lon_count) for i in range(lon_count)])
    east = lax.ppermute(side, "lon", [((i + 1) % lon_count, i) for i in range(lon_count)])
    outgoing = pack_columns(forcing, plant_type, send_slot, lon_count * lat_count)
    received = lax.all_to_all(outgoing, ("lon", "lat"), split_axis=0, concat_axis=0, tiled=True)
    lat_place = jnp.stack([lax.axis_index("lat"), jnp.int32(lat_count)]).astype(jnp.int32)
    partial, response = advect_and_mix(
        lat_place, tracer, courant, mixing, south, north, west, east
    )
    return fluxes(received, recv_cell, land_params, tracer, partial, response)


def solution(mesh):
    in_specs = (
        P("mem", None, "lat", "lon"),
        P(None, None, "lat", "lon"),
        P(None, "lat", "lon"),
        P(None, ("lon", "lat")),
        P(("lon", "lat")),
        P(None, "mem", None),
        P(("lon", "lat")),
        P(("lon", "lat"), None),
    )
    out_specs = (P("mem", None, "lat", "lon"), P("mem", "lat", "lon"))
    return jax.shard_map(
        per_device, mesh=mesh, in_specs=in_specs, out_specs=out_specs, check_vma=False
    )
```

time: 190 us -> 53.9 us (0.28); the launches traced: 188 us -> 53.6 us
  other arithmetic: 74.3 us -> 0.08 us
  local copies, waits for them, and re-layouts: 60.5 us -> 2.17 us
  Pallas kernels: 0 us -> 20.5 us
  starting transfers between devices: 37.4 us -> 22.3 us
  waiting for transfers between devices: 12.2 us -> 7.77 us
    scatter-add x2 -> x0, other arithmetic: 41.7 us -> none  [place_columns(): jnp.zeros((values.shape[0], span), jnp.float32).at[:, index]]
    gather x4 -> x0, local copies, waits for them, and re-layouts: 29.1 us -> none  [select_columns(): return jnp.take(values, jnp.minimum(index, span - 1), axis=1)]
    pallas_call x0 -> x4, Pallas kernels: none -> 20.5 us  [the longest x1 8.81 us: advect_and_mix(): pl.pallas_call(advect_kernel, out_shape=(jax.ShapeDtypeStruct(tracer.shap...]
    all_to_all x2 -> x1, waiting for transfers between devices: 12.2 us -> 0.01 us  [per_device(): lax.all_to_all(outgoing, ('lon', 'lat'), split_axis=0, concat_axis=0, til...]
    mul x12 -> x0, other arithmetic: 8.94 us -> none  [the longest x2 3.81 us: flux_divergence(): fluxes = face_courant * jnp.where(face_courant > 0, from_left, from_right)]
    all_to_all x2 -> x1, starting transfers between devices: 22.3 us -> 14.4 us  [per_device(): lax.all_to_all(outgoing, ('lon', 'lat'), split_axis=0, concat_axis=0, til...]
    ppermute x4, waiting for transfers between devices: 0.01 us -> 7.77 us  [the longest x1 5.98 us: per_device(): lax.ppermute(side, 'lon', [(i, (i + 1) % lon_count) for i in range(lon_co...]
    unnamed x99 -> x21, local copies, waits for them, and re-layouts: 9.9 us -> 2.17 us
  transfers between devices with their start and end apart: 6 -> 5, of which waited for: 1 -> 2; matrix products, arithmetic and copies ran while one was open for 26% -> 0% of each run, Pallas kernels for 0% -> 21%
where the time goes in v1:
time: 53.9 us; the launch traced here: 53.6 us
  starting transfers between devices  22.3 us (41%)
  Pallas kernels  20.5 us (38%)
  waiting for transfers between devices  7.77 us (14%)
  local copies, waits for them, and re-layouts  2.17 us (4%)
  between operations  0.72 us (1%)
    all_to_all x1, starting transfers between devices, per_device(): lax.all_to_all(outgoing, ('lon', 'lat'), split_axis=0, concat_axis=0, til...  14.4 us
    pallas_call x1, Pallas kernels, advect_and_mix(): pl.pallas_call(advect_kernel, out_shape=(jax.ShapeDtypeStruct(tracer.shap...  8.81 us
    pallas_call x1, Pallas kernels, fluxes(): pl.pallas_call(flux_kernel, out_shape=(jax.ShapeDtypeStruct(tracer.shape,...  8.02 us
    ppermute x1, waiting for transfers between devices, per_device(): lax.ppermute(side, 'lon', [(i, (i + 1) % lon_count) for i in range(lon_co...  5.98 us
    ppermute x1, starting transfers between devices, per_device(): lax.ppermute(side, 'lon', [((i + 1) % lon_count, i) for i in range(lon_co...  5.45 us
    pallas_call x1, Pallas kernels, pack_columns(): pl.pallas_call(column_kernel, out_shape=jax.ShapeDtypeStruct((tiles, 1, 3...  2.18 us
    unnamed x21, local copies, waits for them, and re-layouts  2.17 us
    ppermute x1, waiting for transfers between devices, per_device(): lax.ppermute(side, 'lon', [((i + 1) % lon_count, i) for i in range(lon_co...  1.78 us
  transfers between devices with their start and end apart: 5, of which 2 were waited for; matrix products, arithmetic and copies ran while one was open for 0% of the time, Pallas kernels for 21%

profile of v1, /device:TPU:2, one launch (start us, length us, event | category | flops | bytes accessed | tf_op | source)
XLA Modules:
  0.0 53.6 jit_solution(18419971946985854516)
XLA Ops:
  0.6 0.0 copy-start
  0.6 1.2 %copy-done = f32[32,8,8,128]{3,2,1,0:T(8,128)S(1)} copy-done((f32[32,8,8,128]{3,2,1,0:T(8,128)S(1)}, f32[32,8,8,128]{3,2,1,0:T(8,128)}, u32[]{:S(2)}) %copy-start) | copy-done | bytes 1048600
  1.9 0.0 copy-start.2
  1.9 0.8 %copy-done.2 = f32[2,8,8,128]{3,2,1,0:T(8,128)S(1)} copy-done((f32[2,8,8,128]{3,2,1,0:T(8,128)S(1)}, f32[2,8,8,128]{3,2,1,0:T(8,128)}, u32[]{:S(2)}) %copy-start.2) | copy-done | bytes 65560
  2.7 0.0 copy-start.6
  2.7 0.0 copy-start.7
  2.7 0.0 copy-start.8
  2.7 1.5 %pack_halos.1 = (f32[768,128]{1,0:T(8,128)S(1)}, f32[776,128]{1,0:T(8,128)S(1)}, f32[136,128]{1,0:T(8,128)S(1)}) custom-call(f32[2048,128]{1,0:T(8,128)S(1)} %bitcast.5, f32[128,128]{1,0:T(8,128)S(1)} %bitcast.6), custom_call_target="tpu_custom_call" | custom-call | flops 1000000 | bytes 2000000 | tf_op jit(solution)/shard_map/pack_halos/pallas_call | solution.py:128
  4.2 1.6 %collective-permute-start = (f32[776,128]{1,0:T(8,128)S(1)}, f32[776,128]{1,0:T(8,128)S(1)}, u32[]{:S(2)}, u32[]{:S(2)}) collective-permute-start(f32[776,128]{1,0:T(8,128)S(1)} %get-tuple-element.7), channel_id=1, source_target_pairs={{0,4},{4,8},{8,12},{12,0},{1,5},{5,9},{9,13},{13,1},{2,6},{6,10},{... | collective-permute-start | bytes 1191944 | tf_op jit(solution)/shard_map/ppermute | solution.py:473
  5.8 0.9 %collective-permute-start.1 = (f32[768,128]{1,0:T(8,128)S(1)}, f32[768,128]{1,0:T(8,128)S(1)}, u32[]{:S(2)}, u32[]{:S(2)}) collective-permute-start(f32[768,128]{1,0:T(8,128)S(1)} %get-tuple-element.8), channel_id=1, source_target_pairs={{4,0},{8,4},{12,8},{0,12},{5,1},{9,5},{13,9},{1,13},{6,2},{10,6},{... | collective-permute-start | bytes 1179656 | tf_op jit(solution)/shard_map/ppermute | solution.py:472
  6.7 0.0 copy-done.6
  6.7 0.0 copy-done.7
  6.7 0.0 copy-done.8
  6.7 0.0 copy-start.1
  6.7 2.2 %pack_columns.1 = f32[64,1,384]{2,1,0:T(1,128)} custom-call(f32[5,3072]{1,0:T(8,128)S(1)} %copy-done.6, s32[1,3072]{1,0:T(1,128)S(1)} %bitcast.7, s32[1,3072]{1,0:T(1,128)S(1)} %bitcast.8), custom_call_target="tpu_custom_call" | custom-call | flops 704643072 | bytes 300000 | tf_op jit(solution)/shard_map/pack_columns/pallas_call | solution.py:80
  8.9 0.0 copy-start.9
  8.9 0.0 copy-start.5
  8.9 14.4 %all-to-all-start = ((f32[64,1,384]{2,1,0:T(1,128)}), f32[64,1,384]{2,1,0:T(1,128)S(1)}, u32[]{:S(2)}, u32[]{:S(2)}) async-start(f32[64,1,384]{2,1,0:T(1,128)} %pack_columns.1), calls=%async_computation | async-start | bytes 196608 | tf_op jit(solution)/shard_map/all_to_all | solution.py:477
  23.3 0.0 copy-start.3
  23.3 5.5 %collective-permute-start.3 = (f32[136,128]{1,0:T(8,128)S(1)}, f32[136,128]{1,0:T(8,128)S(1)}, u32[]{:S(2)}, u32[]{:S(2)}) collective-permute-start(f32[136,128]{1,0:T(8,128)S(1)} %get-tuple-element.9), channel_id=1, source_target_pairs={{16,0},{32,16},{48,32},{64,48},{80,64},{96,80},{112,96},{128,112},... | collective-permute-start | bytes 208904 | tf_op jit(solution)/shard_map/ppermute | solution.py:475
  28.8 0.0 collective-permute-start.2
  28.8 0.0 copy-done.9
  28.8 0.1 copy.10.params_ref
  28.9 0.1 pad_add_fusion.lat_ref
  28.9 0.0 copy-start.4
  28.9 1.8 %collective-permute-done.3.east_ref = f32[136,128]{1,0:T(8,128)S(1)} collective-permute-done((f32[136,128]{1,0:T(8,128)S(1)}, f32[136,128]{1,0:T(8,128)S(1)}, u32[]{:S(2)}, u32[]{:S(2)}) %collective-permute-start.3) | collective-permute-done | bytes 69664 | tf_op jit(solution)/shard_map/ppermute | solution.py:475
  30.7 6.0 %collective-permute-done.2.west_ref = f32[136,128]{1,0:T(8,128)S(1)} collective-permute-done((f32[136,128]{1,0:T(8,128)S(1)}, f32[136,128]{1,0:T(8,128)S(1)}, u32[]{:S(2)}, u32[]{:S(2)}) %collective-permute-start.2) | collective-permute-done | bytes 69664 | tf_op jit(solution)/shard_map/ppermute | solution.py:474
  36.7 0.0 collective-permute-done.1.north_ref
  36.7 0.0 collective-permute-done.south_ref
  36.7 0.0 copy-done.1
  36.7 0.0 copy-done.5
  36.7 0.0 copy-done.3
  36.7 8.8 %advect_and_mix.1 = (f32[32,8,8,128]{3,2,1,0:T(8,128)S(1)}, f32[8,8,128]{2,1,0:T(8,128)S(1)}) custom-call(s32[2]{0:T(128)S(1)} %pad_add_fusion.lat_ref, f32[32,8,8,128]{3,2,1,0:T(8,128)S(1)} %copy-done.1, f32[2,8,8,128]{3,2,1,0:T(8,128)S(1)} %copy-done.3, f32[7,8,128]{2,1,0:T(8,128)S(1)} %copy-done.5, f32[776,128]{1,0:T(8,128)S(1)} %collective-permute-done.south_ref, ...), custom_call_target="tpu_custom_call" | custom-call | flops 12000000 | bytes 4000000 | tf_op jit(solution)/shard_map/advect_and_mix/pallas_call | solution.py:296
  45.6 0.0 all-to-all-done.received_ref
  45.6 0.0 copy-done.4
  45.6 8.0 %fluxes.1 = (f32[32,8,8,128]{3,2,1,0:T(8,128)}, f32[32,8,128]{2,1,0:T(8,128)}) custom-call(f32[64,1,384]{2,1,0:T(1,128)S(1)} %all-to-all-done.received_ref, s32[64,64]{1,0:T(8,128)S(1)} %copy-done.4, f32[3,32,16]{2,1,0:T(8,128)S(1)} %copy.10.params_ref, f32[32,8,8,128]{3,2,1,0:T(8,128)S(1)} %copy-done.1, ...), custom_call_target="tpu_custom_call" | custom-call | flops 600000000 | bytes 3000000 | tf_op jit(solution)/shard_map/fluxes/pallas_call | solution.py:432
Async XLA Ops:
  0.6 1.2 %copy-start = (f32[32,8,8,128]{3,2,1,0:T(8,128)S(1)}, f32[32,8,8,128]{3,2,1,0:T(8,128)}, u32[]{:S(2)}) copy-start(f32[32,8,8,128]{3,2,1,0:T(8,128)} %bottom_ref.1) | copy-start | bytes 3145732
  1.9 0.8 %copy-start.2 = (f32[2,8,8,128]{3,2,1,0:T(8,128)S(1)}, f32[2,8,8,128]{3,2,1,0:T(8,128)}, u32[]{:S(2)}) copy-start(f32[2,8,8,128]{3,2,1,0:T(8,128)} %courant_ref.1) | copy-start | bytes 196612
  2.7 4.0 %copy-start.6 = (f32[5,3072]{1,0:T(8,128)S(1)}, f32[5,3072]{1,0:T(8,128)}, u32[]{:S(2)}) copy-start(f32[5,3072]{1,0:T(8,128)} %forcing_ref.1) | copy-start | bytes 184324
  2.7 4.0 %copy-start.7 = (s32[3072]{0:T(1024)S(1)}, s32[3072]{0:T(1024)}, u32[]{:S(2)}) copy-start(s32[3072]{0:T(1024)} %param.12) | copy-start | bytes 36868
  2.7 4.0 %copy-start.8 = (s32[3072]{0:T(1024)S(1)}, s32[3072]{0:T(1024)}, u32[]{:S(2)}) copy-start(s32[3072]{0:T(1024)} %param.14) | copy-start | bytes 36868
  4.2 32.5 %collective-permute-start = (f32[776,128]{1,0:T(8,128)S(1)}, f32[776,128]{1,0:T(8,128)S(1)}, u32[]{:S(2)}, u32[]{:S(2)}) collective-permute-start(f32[776,128]{1,0:T(8,128)S(1)} %get-tuple-element.7), channel_id=1, source_target_pairs={{0,4},{4,8},{8,12},{12,0},{1,5},{5,9},{9,13},{13,1},{2,6},{6,10},{... | collective-permute-start | bytes 1191944 | tf_op jit(solution)/shard_map/ppermute | solution.py:473
  5.8 30.9 %collective-permute-start.1 = (f32[768,128]{1,0:T(8,128)S(1)}, f32[768,128]{1,0:T(8,128)S(1)}, u32[]{:S(2)}, u32[]{:S(2)}) collective-permute-start(f32[768,128]{1,0:T(8,128)S(1)} %get-tuple-element.8), channel_id=1, source_target_pairs={{4,0},{8,4},{12,8},{0,12},{5,1},{9,5},{13,9},{1,13},{6,2},{10,6},{... | collective-permute-start | bytes 1179656 | tf_op jit(solution)/shard_map/ppermute | solution.py:472
  6.7 30.0 %copy-start.1 = (f32[32,8,8,128]{3,2,1,0:T(8,128)S(1)}, f32[32,8,8,128]{3,2,1,0:T(8,128)}, u32[]{:S(2)}) copy-start(f32[32,8,8,128]{3,2,1,0:T(8,128)} %bottom_ref.1) | copy-start | bytes 3145732
  8.9 19.9 %copy-start.9 = (f32[3,32,16]{1,2,0:T(8,128)S(1)}, f32[3,32,16]{1,2,0:T(8,128)}, u32[]{:S(2)}) copy-start(f32[3,32,16]{1,2,0:T(8,128)} %param.13) | copy-start | bytes 18436
  8.9 27.9 %copy-start.5 = (f32[7,8,128]{2,1,0:T(8,128)S(1)}, f32[7,8,128]{2,1,0:T(8,128)}, u32[]{:S(2)}) copy-start(f32[7,8,128]{2,1,0:T(8,128)} %mixing_ref.1) | copy-start | bytes 86020
  8.9 36.7 %all-to-all-start = ((f32[64,1,384]{2,1,0:T(1,128)}), f32[64,1,384]{2,1,0:T(1,128)S(1)}, u32[]{:S(2)}, u32[]{:S(2)}) async-start(f32[64,1,384]{2,1,0:T(1,128)} %pack_columns.1), calls=%async_computation | async-start | bytes 196608 | tf_op jit(solution)/shard_map/all_to_all | solution.py:477
  23.3 13.4 %copy-start.3 = (f32[2,8,8,128]{3,2,1,0:T(8,128)S(1)}, f32[2,8,8,128]{3,2,1,0:T(8,128)}, u32[]{:S(2)}) copy-start(f32[2,8,8,128]{3,2,1,0:T(8,128)} %courant_ref.1) | copy-start | bytes 196612
  23.3 7.4 %collective-permute-start.3 = (f32[136,128]{1,0:T(8,128)S(1)}, f32[136,128]{1,0:T(8,128)S(1)}, u32[]{:S(2)}, u32[]{:S(2)}) collective-permute-start(f32[136,128]{1,0:T(8,128)S(1)} %get-tuple-element.9), channel_id=1, source_target_pairs={{16,0},{32,16},{48,32},{64,48},{80,64},{96,80},{112,96},{128,112},... | collective-permute-start | bytes 208904 | tf_op jit(solution)/shard_map/ppermute | solution.py:475
  28.8 7.9 %collective-permute-start.2 = (f32[136,128]{1,0:T(8,128)S(1)}, f32[136,128]{1,0:T(8,128)S(1)}, u32[]{:S(2)}, u32[]{:S(2)}) collective-permute-start(f32[136,128]{1,0:T(8,128)S(1)} %get-tuple-element.9), channel_id=1, source_target_pairs={{0,16},{16,32},{32,48},{48,64},{64,80},{80,96},{96,112},{112,128},... | collective-permute-start | bytes 208904 | tf_op jit(solution)/shard_map/ppermute | solution.py:474
  28.9 16.6 %copy-start.4 = (s32[64,64]{1,0:T(8,128)S(1)}, s32[64,64]{1,0:T(8,128)}, u32[]{:S(2)}) copy-start(s32[64,64]{1,0:T(8,128)} %cell_ref.1) | copy-start | bytes 49156

commit v2 on v1

v2 whole, which is shorter than its diff:
```python
import functools

import jax
import jax.numpy as jnp
from jax import lax
from jax.experimental import pallas as pl
from jax.experimental.pallas import tpu as pltpu
from jax.sharding import PartitionSpec as P

FLUX_SCALE = 0.02
GAS_CONSTANT = 8.314
LANES = 128
ROWS = 8
VMEM_BYTES = 40 * 2**20
PACK_VMEM_BYTES = 58 * 2**20
PARTS = 2
ADVECT_BYTES = 4000000


def nt_dot(left, right):
    return lax.dot_general(
        left, right, (((1,), (1,)), ((), ())), preferred_element_type=jnp.float32
    )


def bf16_parts(values, count):
    parts = []
    rest = values
    for _ in range(count):
        part = rest.astype(jnp.bfloat16)
        rest = rest - part.astype(jnp.float32)
        parts.append(part)
    return parts


def pack_kernel(
    tracer_hbm, courant_hbm, forcing_hbm, type_hbm, slot_hbm,
    payload_ref, low_ref, high_ref, westward_ref, eastward_ref,
    cells_ref, faces_ref, forcing_ref, type_ref, slot_ref, copy_sems,
):
    moves = (
        (slot_hbm, slot_ref),
        (forcing_hbm, forcing_ref),
        (type_hbm, type_ref),
        (tracer_hbm, cells_ref),
        (courant_hbm, faces_ref),
    )
    copies = [
        pltpu.make_async_copy(source, target, copy_sems.at[place])
        for place, (source, target) in enumerate(moves)
    ]
    for copy in copies:
        copy.start()
    for copy in copies[0:3]:
        copy.wait()

    columns = slot_ref.shape[1]
    slot = slot_ref[...]
    lon_tile = jnp.right_shift(slot, 8).astype(jnp.float32).astype(jnp.bfloat16)
    place = jnp.bitwise_and(slot, 255).astype(jnp.float32).astype(jnp.bfloat16)
    one, zero = jnp.bfloat16(1.0), jnp.bfloat16(0.0)

    def ids(count):
        return (
            lax.broadcasted_iota(jnp.int32, (count, columns), 0)
            .astype(jnp.float32)
            .astype(jnp.bfloat16)
        )

    tile_mask = ids(16) == lon_tile
    place_onehot = jnp.where(ids(256) == place, one, zero)
    leaf_area = 0.5 + 5.5 * forcing_ref[3:4, :]
    area_share = 0.05 + 0.55 * forcing_ref[4:5, :]
    canopy_scale = (1.0 - jnp.exp(-0.5 * leaf_area)) / 0.5
    values = [
        (forcing_ref[0:1, :], PARTS),
        (forcing_ref[1:2, :], PARTS),
        (forcing_ref[2:3, :], PARTS),
        (-FLUX_SCALE * area_share * canopy_scale, PARTS),
        (type_ref[...].astype(jnp.float32), 1),
    ]
    rows = []
    for value, count in values:
        for part in bf16_parts(value, count):
            rows.append(jnp.where(tile_mask, jnp.broadcast_to(part, (16, columns)), zero))
    moved = nt_dot(jnp.concatenate(rows, axis=0), place_onehot)
    placed = []
    start = 0
    for value, count in values:
        total = moved[start : start + 16]
        for step in range(1, count):
            total = total + moved[start + 16 * step : start + 16 * (step + 1)]
        placed.append(total)
        start += 16 * count
    low_half = lax.broadcasted_iota(jnp.int32, (16, LANES), 1) < 64
    for tile in range(4):
        span = slice((tile // 2) * LANES, (tile // 2 + 1) * LANES)
        for pair in range(3):
            left = placed[2 * pair][:, span]
            right = placed[min(2 * pair + 1, 4)][:, span]
            if tile % 2 == 0:
                joined = jnp.where(low_half, left, pltpu.roll(right, 64, 1))
            else:
                joined = jnp.where(low_half, pltpu.roll(left, 64, 1), right)
            payload_ref[tile * 16 : (tile + 1) * 16, 0, pair * LANES : (pair + 1) * LANES] = joined

    for copy in copies[3:5]:
        copy.wait()
    blocks = cells_ref.shape[0] // ROWS
    levels = faces_ref.shape[0] // (2 * ROWS)
    for step in range(3):
        low_ref[step * blocks : (step + 1) * blocks, :] = cells_ref[
            pl.ds(step, blocks, stride=ROWS), :
        ]
        high_ref[step * blocks : (step + 1) * blocks, :] = cells_ref[
            pl.ds(ROWS - 3 + step, blocks, stride=ROWS), :
        ]
    high_ref[3 * blocks : 3 * blocks + levels, :] = faces_ref[
        pl.ds(levels * ROWS + ROWS - 1, levels, stride=ROWS), :
    ]
    squares = cells_ref.shape[0] // LANES
    for square in range(squares):
        turned = cells_ref[square * LANES : (square + 1) * LANES, :].T
        westward_ref[3 * square : 3 * square + 3, :] = turned[0:3]
        eastward_ref[3 * square : 3 * square + 3, :] = turned[LANES - 3 : LANES]
    turned = faces_ref[...].T
    westward_ref[3 * squares : 3 * squares + ROWS, :] = turned[LANES - ROWS : LANES]
    eastward_ref[3 * squares : 3 * squares + ROWS, :] = turned[LANES - ROWS : LANES]


def pack(tracer_rows, courant_rows, forcing, plant_type, send_slot, tiles):
    columns = send_slot.shape[0]
    blocks = tracer_rows.shape[0] // ROWS
    levels = courant_rows.shape[0] // (2 * ROWS)
    side_rows = 3 * (tracer_rows.shape[0] // LANES) + ROWS
    vmem = pl.BlockSpec(memory_space=pltpu.VMEM)
    hbm = pl.BlockSpec(memory_space=pltpu.HBM)
    return pl.pallas_call(
        pack_kernel,
        out_shape=(
            jax.ShapeDtypeStruct((tiles, 1, 3 * LANES), jnp.float32),
            jax.ShapeDtypeStruct((3 * blocks, LANES), jnp.float32),
            jax.ShapeDtypeStruct((3 * blocks + levels, LANES), jnp.float32),
            jax.ShapeDtypeStruct((side_rows, LANES), jnp.float32),
            jax.ShapeDtypeStruct((side_rows, LANES), jnp.float32),
        ),
        in_specs=[hbm] * 5,
        out_specs=(vmem,) * 5,
        scratch_shapes=[
            pltpu.VMEM(tracer_rows.shape, jnp.float32),
            pltpu.VMEM(courant_rows.shape, jnp.float32),
            pltpu.VMEM(forcing.shape, jnp.float32),
            pltpu.VMEM((1, columns), jnp.int32),
            pltpu.VMEM((1, columns), jnp.int32),
            pltpu.SemaphoreType.DMA((5,)),
        ],
        compiler_params=pltpu.CompilerParams(vmem_limit_bytes=PACK_VMEM_BYTES),
        cost_estimate=pl.CostEstimate(
            flops=300000000, bytes_accessed=2500000, transcendentals=columns
        ),
        name="pack",
    )(
        tracer_rows, courant_rows, forcing,
        plant_type.reshape(1, columns), send_slot.reshape(1, columns),
    )


def face_weights(face_courant):
    half = 0.5 * face_courant
    upwind = face_courant > 0
    shrink_left = 1.0 - 2.0 / 3.0 * face_courant
    shrink_right = 1.0 + 2.0 / 3.0 * face_courant
    curve = half * jnp.where(upwind, shrink_left, shrink_right)
    middle = face_courant * jnp.where(upwind, 1.0 - half - 3.0 * curve, 1.0 + half + 3.0 * curve)
    left_edge = face_courant * jnp.where(upwind, half - 3.0 * curve, 0.0)
    right_edge = face_courant * jnp.where(upwind, 0.0, 3.0 * curve - half)
    left_cell = face_courant * jnp.where(upwind, 6.0 * curve, 0.0)
    right_cell = face_courant * jnp.where(upwind, 0.0, -6.0 * curve)
    near, far = 7.0 / 12.0, 1.0 / 12.0
    return [
        -far * left_edge,
        near * left_edge - far * middle,
        near * (middle + left_edge) - far * right_edge + left_cell,
        near * (middle + right_edge) - far * left_edge + right_cell,
        near * right_edge - far * middle,
        -far * right_edge,
    ]


def divergence_weights(face_after, face_before):
    after = face_weights(face_after)
    before = face_weights(face_before)
    taps = []
    for offset in range(7):
        if offset == 0:
            taps.append(-before[0])
        elif offset == 6:
            taps.append(after[5])
        else:
            taps.append(after[offset - 1] - before[offset])
    return taps


TURNED_ROWS = LANES + 16
PADDED_ROWS = 2 * ROWS


def advect_kernel(
    lat_ref, tracer_ref, courant_ref, mixing_ref, south_ref, north_ref, west_ref, east_ref,
    out_ref, response_ref,
    turned_ref, turned_sum_ref, turned_courant_ref, lon_ref, rows_ref, weight_ref, pivot_ref,
):
    levels = mixing_ref.shape[0] + 1
    members = out_ref.shape[0]
    blocks = members * levels
    squares = blocks * ROWS // LANES
    first = lat_ref[0] == 0
    last = lat_ref[0] == lat_ref[1] - 1

    for square in range(squares):
        base = square * TURNED_ROWS
        turned_ref[base + 5 : base + 8, :] = west_ref[3 * square : 3 * square + 3, :]
        turned_ref[base + 8 + LANES : base + 11 + LANES, :] = east_ref[
            3 * square : 3 * square + 3, :
        ]
        turned_ref[base + 8 : base + 8 + LANES, :] = tracer_ref[
            square * LANES : (square + 1) * LANES, :
        ].T
    half = levels * ROWS
    turned_faces = courant_ref[...].T
    low_half = lax.broadcasted_iota(jnp.int32, (LANES, LANES), 1) < half
    turned_faces = jnp.where(low_half, turned_faces, pltpu.roll(turned_faces, half, 1))
    turned_courant_ref[8 : 8 + LANES, :] = turned_faces
    side_face = west_ref[3 * squares : 3 * squares + ROWS, :]
    side_face = jnp.where(low_half[0:ROWS], side_face, pltpu.roll(side_face, half, 1))
    turned_courant_ref[0:8, :] = side_face

    def lon_step(tile, carry):
        start = pl.multiple_of(tile * ROWS, ROWS)
        taps = divergence_weights(
            turned_courant_ref[pl.ds(start + 8, ROWS), :],
            turned_courant_ref[pl.ds(start + 7, ROWS), :],
        )
        for square in range(squares):
            base = square * TURNED_ROWS + start + 5
            total = taps[0] * turned_ref[pl.ds(base, ROWS), :]
            for offset in range(1, 7):
                total = total + taps[offset] * turned_ref[pl.ds(base + offset, ROWS), :]
            turned_sum_ref[pl.ds(square * LANES + start, ROWS), :] = total
        return carry

    lax.fori_loop(0, LANES // ROWS, lon_step, 0)
    for square in range(squares):
        span = slice(square * LANES, (square + 1) * LANES)
        lon_ref[span, :] = turned_sum_ref[span, :].T

    zero = jnp.zeros((blocks, LANES), jnp.float32)
    for step in range(3):
        span = slice(step * blocks, (step + 1) * blocks)
        rows_ref[pl.ds(5 + step, blocks, stride=PADDED_ROWS), :] = jnp.where(
            first, zero, south_ref[span, :]
        )
        rows_ref[pl.ds(PADDED_ROWS + step, blocks, stride=PADDED_ROWS), :] = jnp.where(
            last, zero, north_ref[span, :]
        )
    for block in range(blocks):
        rows_ref[block * PADDED_ROWS + 8 : block * PADDED_ROWS + 16, :] = tracer_ref[
            block * ROWS : (block + 1) * ROWS, :
        ]
    row = lax.broadcasted_iota(jnp.int32, (ROWS, LANES), 0)
    for level in range(levels):
        north_face = courant_ref[half + level * ROWS : half + (level + 1) * ROWS, :]
        below = jnp.where(first, 0.0, south_ref[3 * blocks + level : 3 * blocks + level + 1, :])
        south_face = jnp.where(row == 0, below, pltpu.roll(north_face, 1, 0))
        north_face = jnp.where(jnp.logical_and(last, row == ROWS - 1), 0.0, north_face)
        taps = divergence_weights(north_face, south_face)
        for offset in range(7):
            weight_ref[level, offset] = 1.0 - taps[3] if offset == 3 else -taps[offset]

    ratio = None
    response = []
    for level in range(levels):
        pivot = jnp.ones((ROWS, LANES), jnp.float32)
        if level > 0:
            pivot = pivot + mixing_ref[level - 1]
        if level < levels - 1:
            pivot = pivot + mixing_ref[level]
        if level > 0:
            pivot = pivot - mixing_ref[level - 1] * ratio
        inverse = 1.0 / pivot
        carried = inverse
        if level > 0:
            carried = mixing_ref[level - 1] * inverse
            response.append(carried * response[-1])
        else:
            response.append(inverse)
        pivot_ref[level, 0] = inverse
        pivot_ref[level, 1] = carried
        if level < levels - 1:
            ratio = mixing_ref[level] * inverse
            pivot_ref[level, 2] = ratio
    for level in range(levels - 1, -1, -1):
        if level < levels - 1:
            response[level] = response[level] + pivot_ref[level, 2] * response[level + 1]
        response_ref[level] = response[level]

    together = 4

    def member_step(index, carry):
        swept = [None] * together
        stored = [[None] * levels for _ in range(together)]
        for level in range(levels):
            for step in range(together):
                block = (index * together + step) * levels + level
                base = pl.multiple_of(block * PADDED_ROWS, PADDED_ROWS)
                total = -lon_ref[pl.ds(pl.multiple_of(block * ROWS, ROWS), ROWS), :]
                for offset in range(7):
                    total = (
                        total
                        + weight_ref[level, offset] * rows_ref[pl.ds(base + 5 + offset, ROWS), :]
                    )
                total = total * pivot_ref[level, 0]
                if level > 0:
                    total = total + pivot_ref[level, 1] * swept[step]
                swept[step] = total
                stored[step][level] = total
        for level in range(levels - 1, -1, -1):
            for step in range(together):
                if level < levels - 1:
                    swept[step] = stored[step][level] + pivot_ref[level, 2] * swept[step]
                out_ref[index * together + step, level] = swept[step]
        return carry

    lax.fori_loop(0, members // together, member_step, 0)


def advect_and_mix(lat_place, tracer_rows, courant_rows, mixing, south, north, west, east):
    levels, rows, lanes = mixing.shape[0] + 1, mixing.shape[1], mixing.shape[2]
    blocks = tracer_rows.shape[0] // rows
    members = blocks // levels
    squares = tracer_rows.shape[0] // lanes
    vmem = pl.BlockSpec(memory_space=pltpu.VMEM)
    return pl.pallas_call(
        advect_kernel,
        out_shape=(
            jax.ShapeDtypeStruct((members, levels, rows, lanes), jnp.float32),
            jax.ShapeDtypeStruct((levels, rows, lanes), jnp.float32),
        ),
        in_specs=[pl.BlockSpec(memory_space=pltpu.SMEM)] + [vmem] * 7,
        out_specs=(vmem, vmem),
        scratch_shapes=[
            pltpu.VMEM((squares * TURNED_ROWS, LANES), jnp.float32),
            pltpu.VMEM((squares * LANES, LANES), jnp.float32),
            pltpu.VMEM((LANES + 8, LANES), jnp.float32),
            pltpu.VMEM((squares * LANES, LANES), jnp.float32),
            pltpu.VMEM(((blocks + 1) * PADDED_ROWS, LANES), jnp.float32),
            pltpu.VMEM((levels, 7, ROWS, LANES), jnp.float32),
            pltpu.VMEM((levels, 3, ROWS, LANES), jnp.float32),
        ],
        compiler_params=pltpu.CompilerParams(vmem_limit_bytes=VMEM_BYTES),
        cost_estimate=pl.CostEstimate(flops=12000000, bytes_accessed=ADVECT_BYTES, transcendentals=0),
        name="advect_and_mix",
    )(lat_place, tracer_rows, courant_rows, mixing, south, north, west, east)


def arrhenius(energy, leaf_temp):
    return jnp.exp(energy * (leaf_temp - 25.0) / (298.15 * GAS_CONSTANT * (leaf_temp + 273.15)))


CHUNK = 4


def flux_kernel(
    received_ref, cell_ref, params_ref, bottom_ref, partial_ref, response_ref,
    out_ref, surface_ref,
    column_ref, left_ref, right_ref, result_ref, copy_sems,
):
    members = params_ref.shape[1]
    types = params_ref.shape[2]
    sources, places = cell_ref.shape
    groups = sources // 2
    levels = response_ref.shape[0]
    quarters = ROWS // 2
    one, zero = jnp.bfloat16(1.0), jnp.bfloat16(0.0)

    carbox = 30.0 + 70.0 * params_ref[0]
    tables = jnp.concatenate(
        [carbox, (1.4 + 0.8 * params_ref[1]) * carbox, (0.005 + 0.025 * params_ref[2]) * carbox],
        axis=0,
    )
    table_parts = jnp.concatenate(bf16_parts(tables, 2), axis=1)
    bottom = jnp.concatenate(
        [
            jnp.concatenate(
                [bottom_ref[:, 0, 2 * quarter, :], bottom_ref[:, 0, 2 * quarter + 1, :]], axis=1
            )
            for quarter in range(quarters)
        ],
        axis=0,
    )
    bottom_parts = jnp.concatenate(bf16_parts(bottom, 2), axis=0)

    half = lax.broadcasted_iota(jnp.int32, (groups, LANES), 1) < places

    def pair(values):
        low, high = values[0:groups], values[groups : 2 * groups]
        return (
            jnp.where(half, low, pltpu.roll(high, places, 1)),
            jnp.where(half, pltpu.roll(low, places, 1), high),
        )

    light, leaf_temp = pair(received_ref[:, 0, 0:LANES])
    water, flux_scale = pair(received_ref[:, 0, LANES : 2 * LANES])
    plant, _ = pair(received_ref[:, 0, 2 * LANES : 3 * LANES])
    leaf_temp = 35.0 * leaf_temp
    absorbed = 0.425 * (2000.0 * light)
    michaelis_carbon = 404.9 * arrhenius(79430.0, leaf_temp)
    michaelis_oxygen = 278.4 * arrhenius(36380.0, leaf_temp)
    compensation = 42.75 * arrhenius(37830.0, leaf_temp)
    column_ref[0] = absorbed
    column_ref[1] = arrhenius(65330.0, leaf_temp) * (0.2 + 0.8 * water)
    column_ref[2] = arrhenius(43540.0, leaf_temp)
    column_ref[3] = michaelis_carbon * (1.0 + 210.0 / michaelis_oxygen)
    column_ref[4] = compensation
    column_ref[5] = flux_scale
    column_ref[6] = 2.8 * absorbed
    column_ref[7] = (1.4 * 8.0) * compensation
    column_ref[8] = plant
    cells = jnp.concatenate(
        [cell_ref[pl.ds(tile, sources // 4, stride=4), :] for tile in range(4)], axis=0
    )
    cells = jnp.concatenate([cells[0:groups], cells[groups : 2 * groups]], axis=1)
    column_ref[9] = jnp.right_shift(cells, 8).astype(jnp.float32)
    column_ref[10] = jnp.bitwise_and(cells, 255).astype(jnp.float32)

    def ids(count, mask):
        return (
            jnp.bitwise_and(lax.broadcasted_iota(jnp.int32, (count, LANES), 0), mask)
            .astype(jnp.float32)
            .astype(jnp.bfloat16)
        )

    cell_ids = ids(256, 255)
    type_ids = ids(2 * types, types - 1)

    for chunk in range(groups // CHUNK):
        rows = range(chunk * CHUNK, (chunk + 1) * CHUNK)
        span = slice(chunk * CHUNK * LANES, (chunk + 1) * CHUNK * LANES)

        def spread(quantity, count=members):
            return jnp.concatenate(
                [
                    jnp.broadcast_to(column_ref[quantity, row : row + 1, :], (count, LANES))
                    for row in rows
                ],
                axis=1,
            )

        def onehot(row_ids, quantity):
            return jnp.concatenate(
                [
                    jnp.where(
                        row_ids == column_ref[quantity, row : row + 1, :].astype(jnp.bfloat16),
                        one,
                        zero,
                    )
                    for row in rows
                ],
                axis=1,
            )

        cell_onehot = onehot(cell_ids, 10)
        right_ref[:, span] = cell_onehot
        near = jnp.dot(bottom_parts, cell_onehot, preferred_element_type=jnp.float32)
        near = near[0 : quarters * members] + near[quarters * members : 2 * quarters * members]
        quarter_index = spread(9)
        picked = near[0:members]
        for quarter in range(1, quarters):
            picked = jnp.where(
                quarter_index == quarter, near[quarter * members : (quarter + 1) * members], picked
            )
        params = jnp.dot(
            table_parts, onehot(type_ids, 8), preferred_element_type=jnp.float32
        )
        carbon_leaf = 280.0 + 70.0 * picked
        warm = spread(1)
        carboxylation = params[0:members] * warm
        transport_max = params[members : 2 * members] * spread(2)
        respiration = params[2 * members : 3 * members] * warm
        total_rate = spread(0) + transport_max
        square = total_rate * total_rate - spread(6) * transport_max
        electron_rate = total_rate - square * lax.rsqrt(square)
        excess = carbon_leaf - spread(4)
        rubisco_base = carbon_leaf + spread(3)
        light_base = (1.4 * 4.0) * carbon_leaf + spread(7)
        shared = excess / (rubisco_base * light_base)
        rubisco_rate = carboxylation * light_base * shared
        light_rate = electron_rate * rubisco_base * shared
        flux = spread(5) * (jnp.minimum(rubisco_rate, light_rate) - respiration)
        high, low = bf16_parts(flux, 2)
        quarter_index = quarter_index.astype(jnp.bfloat16)
        for quarter in range(quarters):
            here = quarter_index == jnp.bfloat16(quarter)
            start = quarter * 2 * members
            left_ref[start : start + members, span] = jnp.where(here, high, zero)
            left_ref[start + members : start + 2 * members, span] = jnp.where(here, low, zero)

    summed = nt_dot(left_ref[...], right_ref[...])
    for quarter in range(quarters):
        start = quarter * 2 * members
        total = summed[start : start + members] + summed[start + members : start + 2 * members]
        surface_ref[:, 2 * quarter, :] = total[:, 0:LANES]
        surface_ref[:, 2 * quarter + 1, :] = total[:, LANES : 2 * LANES]

    copies = []
    quarter = members // 4
    for part in range(4):

        def member_step(member, carry):
            surface = surface_ref[member]
            for level in range(levels):
                result_ref[member, level] = (
                    partial_ref[member, level] + response_ref[level] * surface
                )
            return carry

        lax.fori_loop(part * quarter, (part + 1) * quarter, member_step, 0, unroll=4)
        span = pl.ds(part * quarter, quarter)
        copy = pltpu.make_async_copy(result_ref.at[span], out_ref.at[span], copy_sems.at[part])
        copy.start()
        copies.append(copy)
    for copy in copies:
        copy.wait()


def fluxes(received, recv_cell, land_params, tracer, partial, response):
    members, levels, rows, lanes = tracer.shape
    tiles = received.shape[0]
    place_count = recv_cell.shape[0] * recv_cell.shape[1]

    def whole(array):
        return pl.BlockSpec(array.shape, lambda step: (0,) * array.ndim)

    return pl.pallas_call(
        flux_kernel,
        out_shape=(
            jax.ShapeDtypeStruct(tracer.shape, jnp.float32),
            jax.ShapeDtypeStruct((members, rows, lanes), jnp.float32),
        ),
        in_specs=[
            whole(received),
            whole(recv_cell),
            whole(land_params),
            pl.BlockSpec((members, 1, rows, lanes), lambda step: (0, 0, 0, 0)),
            whole(partial),
            whole(response),
        ],
        out_specs=(
            pl.BlockSpec(memory_space=pltpu.HBM),
            pl.BlockSpec((members, rows, lanes), lambda step: (0, 0, 0)),
        ),
        grid=(1,),
        scratch_shapes=[
            pltpu.VMEM((11, tiles // 2, LANES), jnp.float32),
            pltpu.VMEM((ROWS * members, place_count), jnp.bfloat16),
            pltpu.VMEM((256, place_count), jnp.bfloat16),
            pltpu.VMEM(tracer.shape, jnp.float32),
            pltpu.SemaphoreType.DMA((4,)),
        ],
        compiler_params=pltpu.CompilerParams(vmem_limit_bytes=VMEM_BYTES),
        cost_estimate=pl.CostEstimate(flops=600000000, bytes_accessed=3000000, transcendentals=400000),
        name="fluxes",
    )(received, recv_cell, land_params, tracer, partial, response)


def per_device(tracer, courant, mixing, forcing, plant_type, land_params, send_slot, recv_cell):
    members, levels, row_count, column_count = tracer.shape
    lon_count, lat_count = lax.axis_size("lon"), lax.axis_size("lat")
    tracer_rows = tracer.reshape(members * levels * row_count, column_count)
    courant_rows = courant.reshape(2 * levels * row_count, column_count)
    outgoing, low, high, westward, eastward = pack(
        tracer_rows, courant_rows, forcing, plant_type, send_slot, lon_count * lat_count
    )
    north = lax.ppermute(low, "lat", [((i + 1) % lat_count, i) for i in range(lat_count)])
    south = lax.ppermute(high, "lat", [(i, (i + 1) % lat_count) for i in range(lat_count)])
    west = lax.ppermute(eastward, "lon", [(i, (i + 1) % lon_count) for i in range(lon_count)])
    east = lax.ppermute(westward, "lon", [((i + 1) % lon_count, i) for i in range(lon_count)])
    received = lax.all_to_all(outgoing, ("lat", "lon"), split_axis=0, concat_axis=0, tiled=True)
    lat_place = jnp.stack([lax.axis_index("lat"), jnp.int32(lat_count)]).astype(jnp.int32)
    partial, response = advect_and_mix(
        lat_place, tracer_rows, courant_rows, mixing, south, north, west, east
    )
    return fluxes(received, recv_cell, land_params, tracer, partial, response)


def solution(mesh):
    in_specs = (
        P("mem", None, "lat", "lon"),
        P(None, None, "lat", "lon"),
        P(None, "lat", "lon"),
        P(None, ("lon", "lat")),
        P(("lon", "lat")),
        P(None, "mem", None),
        P(("lon", "lat")),
        P(("lon", "lat"), None),
    )
    out_specs = (P("mem", None, "lat", "lon"), P("mem", "lat", "lon"))
    return jax.shard_map(
        per_device, mesh=mesh, in_specs=in_specs, out_specs=out_specs, check_vma=False
    )
```

time: 53.9 us -> 36.4 us (0.68)
  Pallas kernels: 20.5 us -> 10.5 us
  waiting for transfers between devices: 7.77 us -> 2.03 us
  local copies, waits for them, and re-layouts: 2.17 us -> 0.1 us
    ppermute x2, waiting for transfers between devices: 7.76 us -> 2.02 us  [the longest x1 2.02 us: per_device(): lax.ppermute(eastward, 'lon', [(i, (i + 1) % lon_count) for i in range(lo...]
    pallas_call x3 -> x2, Pallas kernels: 12.5 us -> 6.97 us  [the longest x1 3.93 us: advect_and_mix(): pl.pallas_call(advect_kernel, out_shape=(jax.ShapeDtypeStruct((members, l...]
    pallas_call x1, Pallas kernels: 8.02 us -> 3.57 us  [fluxes(): pl.pallas_call(flux_kernel, out_shape=(jax.ShapeDtypeStruct(tracer.shape,...]
    unnamed x21 -> x15, local copies, waits for them, and re-layouts: 2.17 us -> 0.1 us
  transfers between devices with their start and end apart: 5 -> 5, of which waited for: 2 -> 1; matrix products, arithmetic and copies ran while one was open for 0% -> 0% of each run, Pallas kernels for 21% -> 11%
where the time goes in v2:
time: 36.4 us; the launch traced here: 36.1 us
  starting transfers between devices  22.6 us (62%)
  Pallas kernels  10.5 us (29%)
  waiting for transfers between devices  2.03 us (6%)
  between operations  0.73 us (2%)
    all_to_all x1, starting transfers between devices, per_device(): lax.all_to_all(outgoing, ('lat', 'lon'), split_axis=0, concat_axis=0, til...  14.5 us
    ppermute x1, starting transfers between devices, per_device(): lax.ppermute(westward, 'lon', [((i + 1) % lon_count, i) for i in range(lo...  4.18 us
    pallas_call x1, Pallas kernels, advect_and_mix(): pl.pallas_call(advect_kernel, out_shape=(jax.ShapeDtypeStruct((members, l...  3.93 us
    pallas_call x1, Pallas kernels, fluxes(): pl.pallas_call(flux_kernel, out_shape=(jax.ShapeDtypeStruct(tracer.shape,...  3.57 us
    pallas_call x1, Pallas kernels, pack(): pl.pallas_call(pack_kernel, out_shape=(jax.ShapeDtypeStruct((tiles, 1, 3...  3.04 us
    ppermute x1, waiting for transfers between devices, per_device(): lax.ppermute(eastward, 'lon', [(i, (i + 1) % lon_count) for i in range(lo...  2.02 us
    ppermute x1, starting transfers between devices, per_device(): lax.ppermute(high, 'lat', [(i, (i + 1) % lat_count) for i in range(lat_co...  1.57 us
    ppermute x1, starting transfers between devices, per_device(): lax.ppermute(eastward, 'lon', [(i, (i + 1) % lon_count) for i in range(lo...  1.54 us
  transfers between devices with their start and end apart: 5, of which 1 were waited for; matrix products, arithmetic and copies ran while one was open for 0% of the time, Pallas kernels for 11%

profile of v2, /device:TPU:2, one launch (start us, length us, event | category | flops | bytes accessed | tf_op | source)
XLA Modules:
  0.0 36.1 jit_solution(16686109734006331210)
XLA Ops:
  0.6 0.0 copy-start
  0.6 3.0 %pack.1 = (f32[64,1,384]{2,1,0:T(1,128)}, f32[768,128]{1,0:T(8,128)}, f32[776,128]{1,0:T(8,128)}, f32[56,128]{1,0:T(8,128)}, f32[56,128]{1,0:T(8,128)}) custom-call(f32[2048,128]{1,0:T(8,128)} %bitcast.5, f32[128,128]{1,0:T(8,128)} %bitcast.7, f32[5,3072]{1,0:T(8,128)} %forcing_hbm.1, s32[1,3072]{1,0:T(1,128)} %bitcast.9, s32[1,3072]{1,0:T(1,128)} %bitcast.10), custom_call_target="tpu_custom_call" | custom-call | flops 300000000 | bytes 2500000 | tf_op jit(solution)/shard_map/pack/pallas_call | solution.py:138
  3.7 1.6 %collective-permute-start = (f32[776,128]{1,0:T(8,128)}, f32[776,128]{1,0:T(8,128)S(1)}, u32[]{:S(2)}, u32[]{:S(2)}) collective-permute-start(f32[776,128]{1,0:T(8,128)} %get-tuple-element.10), channel_id=1, source_target_pairs={{0,4},{4,8},{8,12},{12,0},{1,5},{5,9},{9,13},{13,1},{2,6},{6,10},{... | collective-permute-start | bytes 1191944 | tf_op jit(solution)/shard_map/ppermute | solution.py:585
  5.3 0.9 %collective-permute-start.1 = (f32[768,128]{1,0:T(8,128)}, f32[768,128]{1,0:T(8,128)S(1)}, u32[]{:S(2)}, u32[]{:S(2)}) collective-permute-start(f32[768,128]{1,0:T(8,128)} %get-tuple-element.11), channel_id=1, source_target_pairs={{4,0},{8,4},{12,8},{0,12},{5,1},{9,5},{13,9},{1,13},{6,2},{10,6},{... | collective-permute-start | bytes 1179656 | tf_op jit(solution)/shard_map/ppermute | solution.py:584
  6.1 0.0 copy-start.6
  6.1 0.0 copy-start.5
  6.1 0.0 copy-start.4
  6.1 0.0 copy-start.3
  6.1 14.5 %all-to-all-start = ((f32[64,1,384]{2,1,0:T(1,128)}), f32[64,1,384]{2,1,0:T(1,128)S(1)}, u32[]{:S(2)}, u32[]{:S(2)}) async-start(f32[64,1,384]{2,1,0:T(1,128)} %get-tuple-element.9), calls=%async_computation | async-start | bytes 196608 | tf_op jit(solution)/shard_map/all_to_all | solution.py:588
  20.6 0.0 copy-start.1
  20.6 0.0 copy-done.6
  20.6 1.5 %collective-permute-start.2 = (f32[56,128]{1,0:T(8,128)S(1)}, f32[56,128]{1,0:T(8,128)S(1)}, u32[]{:S(2)}, u32[]{:S(2)}) collective-permute-start(f32[56,128]{1,0:T(8,128)S(1)} %copy-done.6), channel_id=1, source_target_pairs={{0,16},{16,32},{32,48},{48,64},{64,80},{80,96},{96,112},{112,128},... | collective-permute-start | bytes 86024 | tf_op jit(solution)/shard_map/ppermute | solution.py:586
  22.2 0.0 copy-done.5
  22.2 4.2 %collective-permute-start.3 = (f32[56,128]{1,0:T(8,128)S(1)}, f32[56,128]{1,0:T(8,128)S(1)}, u32[]{:S(2)}, u32[]{:S(2)}) collective-permute-start(f32[56,128]{1,0:T(8,128)S(1)} %copy-done.5), channel_id=1, source_target_pairs={{16,0},{32,16},{48,32},{64,48},{80,64},{96,80},{112,96},{128,112},... | collective-permute-start | bytes 86024 | tf_op jit(solution)/shard_map/ppermute | solution.py:587
  26.4 0.1 pad_add_fusion.lat_ref
  26.4 0.0 copy-done.4
  26.4 0.1 copy.10.params_ref
  26.5 0.0 copy-start.2
  26.5 2.0 %collective-permute-done.2.west_ref = f32[56,128]{1,0:T(8,128)S(1)} collective-permute-done((f32[56,128]{1,0:T(8,128)S(1)}, f32[56,128]{1,0:T(8,128)S(1)}, u32[]{:S(2)}, u32[]{:S(2)}) %collective-permute-start.2) | collective-permute-done | bytes 28704 | tf_op jit(solution)/shard_map/ppermute | solution.py:586
  28.5 0.0 collective-permute-done.3.east_ref
  28.5 0.0 collective-permute-done.1.north_ref
  28.5 0.0 collective-permute-done.south_ref
  28.5 0.0 copy-done
  28.6 0.0 copy-done.3
  28.6 0.0 copy-done.1
  28.6 3.9 %advect_and_mix.1 = (f32[32,8,8,128]{3,2,1,0:T(8,128)S(1)}, f32[8,8,128]{2,1,0:T(8,128)S(1)}) custom-call(s32[2]{0:T(128)S(1)} %pad_add_fusion.lat_ref, f32[2048,128]{1,0:T(8,128)S(1)} %bitcast.6, f32[128,128]{1,0:T(8,128)S(1)} %bitcast.8, f32[7,8,128]{2,1,0:T(8,128)S(1)} %copy-done.3, f32[776,128]{1,0:T(8,128)S(1)} %collective-permute-done.south_ref, ...), custom_call_target="tpu_custom_call" | custom-call | flops 12000000 | bytes 4000000 | tf_op jit(solution)/shard_map/advect_and_mix/pallas_call | solution.py:343
  32.5 0.0 all-to-all-done.received_ref
  32.5 0.0 copy-done.2
  32.5 3.6 %fluxes.1 = (f32[32,8,8,128]{3,2,1,0:T(8,128)}, f32[32,8,128]{2,1,0:T(8,128)}) custom-call(f32[64,1,384]{2,1,0:T(1,128)S(1)} %all-to-all-done.received_ref, s32[64,64]{1,0:T(8,128)S(1)} %copy-done.2, f32[3,32,16]{2,1,0:T(8,128)S(1)} %copy.10.params_ref, f32[32,8,8,128]{3,2,1,0:T(8,128)S(1)} %copy-done, f32[32,8,8,128]{3,2,1,0:T(8,128)S(1)} %get-tuple-element.14.partial_ref, ...), custom_call_target="tpu_custom_call" | custom-call | flops 600000000 | bytes 3000000 | tf_op jit(solution)/shard_map/fluxes/pallas_call | solution.py:544
Async XLA Ops:
  0.6 27.9 %copy-start = (f32[32,8,8,128]{3,2,1,0:T(8,128)S(1)}, f32[32,8,8,128]{3,2,1,0:T(8,128)}, u32[]{:S(2)}) copy-start(f32[32,8,8,128]{3,2,1,0:T(8,128)} %bottom_ref.1) | copy-start | bytes 3145732
  3.7 24.8 %collective-permute-start = (f32[776,128]{1,0:T(8,128)}, f32[776,128]{1,0:T(8,128)S(1)}, u32[]{:S(2)}, u32[]{:S(2)}) collective-permute-start(f32[776,128]{1,0:T(8,128)} %get-tuple-element.10), channel_id=1, source_target_pairs={{0,4},{4,8},{8,12},{12,0},{1,5},{5,9},{9,13},{13,1},{2,6},{6,10},{... | collective-permute-start | bytes 1191944 | tf_op jit(solution)/shard_map/ppermute | solution.py:585
  5.3 23.3 %collective-permute-start.1 = (f32[768,128]{1,0:T(8,128)}, f32[768,128]{1,0:T(8,128)S(1)}, u32[]{:S(2)}, u32[]{:S(2)}) collective-permute-start(f32[768,128]{1,0:T(8,128)} %get-tuple-element.11), channel_id=1, source_target_pairs={{4,0},{8,4},{12,8},{0,12},{5,1},{9,5},{13,9},{1,13},{6,2},{10,6},{... | collective-permute-start | bytes 1179656 | tf_op jit(solution)/shard_map/ppermute | solution.py:584
  6.1 14.5 %copy-start.6 = (f32[56,128]{1,0:T(8,128)S(1)}, f32[56,128]{1,0:T(8,128)}, u32[]{:S(2)}) copy-start(f32[56,128]{1,0:T(8,128)} %get-tuple-element.12) | copy-start | bytes 86020
  6.1 16.0 %copy-start.5 = (f32[56,128]{1,0:T(8,128)S(1)}, f32[56,128]{1,0:T(8,128)}, u32[]{:S(2)}) copy-start(f32[56,128]{1,0:T(8,128)} %get-tuple-element.13) | copy-start | bytes 86020
  6.1 20.3 %copy-start.4 = (f32[3,32,16]{1,2,0:T(8,128)S(1)}, f32[3,32,16]{1,2,0:T(8,128)}, u32[]{:S(2)}) copy-start(f32[3,32,16]{1,2,0:T(8,128)} %param.13) | copy-start | bytes 18436
  6.1 22.4 %copy-start.3 = (f32[7,8,128]{2,1,0:T(8,128)S(1)}, f32[7,8,128]{2,1,0:T(8,128)}, u32[]{:S(2)}) copy-start(f32[7,8,128]{2,1,0:T(8,128)} %mixing_ref.1) | copy-start | bytes 86020
  6.1 26.4 %all-to-all-start = ((f32[64,1,384]{2,1,0:T(1,128)}), f32[64,1,384]{2,1,0:T(1,128)S(1)}, u32[]{:S(2)}, u32[]{:S(2)}) async-start(f32[64,1,384]{2,1,0:T(1,128)} %get-tuple-element.9), calls=%async_computation | async-start | bytes 196608 | tf_op jit(solution)/shard_map/all_to_all | solution.py:588
  20.6 8.0 %copy-start.1 = (f32[2,8,8,128]{3,2,1,0:T(8,128)S(1)}, f32[2,8,8,128]{3,2,1,0:T(8,128)}, u32[]{:S(2)}) copy-start(f32[2,8,8,128]{3,2,1,0:T(8,128)} %param.9) | copy-start | bytes 196612
  20.6 7.9 %collective-permute-start.2 = (f32[56,128]{1,0:T(8,128)S(1)}, f32[56,128]{1,0:T(8,128)S(1)}, u32[]{:S(2)}, u32[]{:S(2)}) collective-permute-start(f32[56,128]{1,0:T(8,128)S(1)} %copy-done.6), channel_id=1, source_target_pairs={{0,16},{16,32},{32,48},{48,64},{64,80},{80,96},{96,112},{112,128},... | collective-permute-start | bytes 86024 | tf_op jit(solution)/shard_map/ppermute | solution.py:586
  22.2 6.4 %collective-permute-start.3 = (f32[56,128]{1,0:T(8,128)S(1)}, f32[56,128]{1,0:T(8,128)S(1)}, u32[]{:S(2)}, u32[]{:S(2)}) collective-permute-start(f32[56,128]{1,0:T(8,128)S(1)} %copy-done.5), channel_id=1, source_target_pairs={{16,0},{32,16},{48,32},{64,48},{80,64},{96,80},{112,96},{128,112},... | collective-permute-start | bytes 86024 | tf_op jit(solution)/shard_map/ppermute | solution.py:587
  26.5 6.0 %copy-start.2 = (s32[64,64]{1,0:T(8,128)S(1)}, s32[64,64]{1,0:T(8,128)}, u32[]{:S(2)}) copy-start(s32[64,64]{1,0:T(8,128)} %cell_ref.1) | copy-start | bytes 49156

commit v3 on v2

--- a/solution.py
+++ b/solution.py
@@ -12,9 +12,7 @@
 LANES = 128
 ROWS = 8
 VMEM_BYTES = 40 * 2**20
-PACK_VMEM_BYTES = 58 * 2**20
 PARTS = 2
-ADVECT_BYTES = 4000000
 
 
 def nt_dot(left, right):
@@ -154,15 +152,18 @@
             pltpu.VMEM((1, columns), jnp.int32),
             pltpu.SemaphoreType.DMA((5,)),
         ],
-        compiler_params=pltpu.CompilerParams(vmem_limit_bytes=PACK_VMEM_BYTES),
+        compiler_params=pltpu.CompilerParams(vmem_limit_bytes=VMEM_BYTES),
         cost_estimate=pl.CostEstimate(
             flops=300000000, bytes_accessed=2500000, transcendentals=columns
         ),
         name="pack",
-    )(
-        tracer_rows, courant_rows, forcing,
-        plant_type.reshape(1, columns), send_slot.reshape(1, columns),
-    )
+    )(*(
+        pltpu.with_memory_space_constraint(array, pltpu.HBM)
+        for array in (
+            tracer_rows, courant_rows, forcing,
+            plant_type.reshape(1, columns), send_slot.reshape(1, columns),
+        )
+    ))
 
 
 def face_weights(face_courant):
@@ -205,54 +206,17 @@
 PADDED_ROWS = 2 * ROWS
 
 
-def advect_kernel(
-    lat_ref, tracer_ref, courant_ref, mixing_ref, south_ref, north_ref, west_ref, east_ref,
-    out_ref, response_ref,
-    turned_ref, turned_sum_ref, turned_courant_ref, lon_ref, rows_ref, weight_ref, pivot_ref,
+def lat_kernel(
+    lat_ref, tracer_ref, courant_ref, mixing_ref, south_ref, north_ref,
+    sum_ref, response_ref, pivot_ref,
+    rows_ref, weight_ref,
 ):
     levels = mixing_ref.shape[0] + 1
-    members = out_ref.shape[0]
-    blocks = members * levels
-    squares = blocks * ROWS // LANES
+    blocks = tracer_ref.shape[0] // ROWS
+    members = blocks // levels
+    half = levels * ROWS
     first = lat_ref[0] == 0
     last = lat_ref[0] == lat_ref[1] - 1
-
-    for square in range(squares):
-        base = square * TURNED_ROWS
-        turned_ref[base + 5 : base + 8, :] = west_ref[3 * square : 3 * square + 3, :]
-        turned_ref[base + 8 + LANES : base + 11 + LANES, :] = east_ref[
-            3 * square : 3 * square + 3, :
-        ]
-        turned_ref[base + 8 : base + 8 + LANES, :] = tracer_ref[
-            square * LANES : (square + 1) * LANES, :
-        ].T
-    half = levels * ROWS
-    turned_faces = courant_ref[...].T
-    low_half = lax.broadcasted_iota(jnp.int32, (LANES, LANES), 1) < half
-    turned_faces = jnp.where(low_half, turned_faces, pltpu.roll(turned_faces, half, 1))
-    turned_courant_ref[8 : 8 + LANES, :] = turned_faces
-    side_face = west_ref[3 * squares : 3 * squares + ROWS, :]
-    side_face = jnp.where(low_half[0:ROWS], side_face, pltpu.roll(side_face, half, 1))
-    turned_courant_ref[0:8, :] = side_face
-
-    def lon_step(tile, carry):
-        start = pl.multiple_of(tile * ROWS, ROWS)
-        taps = divergence_weights(
-            turned_courant_ref[pl.ds(start + 8, ROWS), :],
-            turned_courant_ref[pl.ds(start + 7, ROWS), :],
-        )
-        for square in range(squares):
-            base = square * TURNED_ROWS + start + 5
-            total = taps[0] * turned_ref[pl.ds(base, ROWS), :]
-            for offset in range(1, 7):
-                total = total + taps[offset] * turned_ref[pl.ds(base + offset, ROWS), :]
-            turned_sum_ref[pl.ds(square * LANES + start, ROWS), :] = total
-        return carry
-
-    lax.fori_loop(0, LANES // ROWS, lon_step, 0)
-    for square in range(squares):
-        span = slice(square * LANES, (square + 1) * LANES)
-        lon_ref[span, :] = turned_sum_ref[span, :].T
 
     zero = jnp.zeros((blocks, LANES), jnp.float32)
     for step in range(3):
@@ -307,27 +271,86 @@
     together = 4
 
     def member_step(index, carry):
+        for level in range(levels):
+            taps = [weight_ref[level, offset] for offset in range(7)]
+            for step in range(together):
+                block = (index * together + step) * levels + level
+                base = pl.multiple_of(block * PADDED_ROWS, PADDED_ROWS) + 5
+                total = taps[0] * rows_ref[pl.ds(base, ROWS), :]
+                for offset in range(1, 7):
+                    total = total + taps[offset] * rows_ref[pl.ds(base + offset, ROWS), :]
+                sum_ref[pl.ds(pl.multiple_of(block * ROWS, ROWS), ROWS), :] = total
+        return carry
+
+    lax.fori_loop(0, members // together, member_step, 0)
+
+
+def lon_kernel(
+    tracer_ref, courant_ref, west_ref, east_ref, sum_ref, pivot_ref,
+    out_ref,
+    turned_ref, turned_sum_ref, turned_courant_ref, lon_ref,
+):
+    members, levels = out_ref.shape[0], out_ref.shape[1]
+    squares = tracer_ref.shape[0] // LANES
+
+    for square in range(squares):
+        base = square * TURNED_ROWS
+        turned_ref[base + 5 : base + 8, :] = west_ref[3 * square : 3 * square + 3, :]
+        turned_ref[base + 8 + LANES : base + 11 + LANES, :] = east_ref[
+            3 * square : 3 * square + 3, :
+        ]
+        turned_ref[base + 8 : base + 8 + LANES, :] = tracer_ref[
+            square * LANES : (square + 1) * LANES, :
+        ].T
+    half = levels * ROWS
+    turned_faces = courant_ref[...].T
+    low_half = lax.broadcasted_iota(jnp.int32, (LANES, LANES), 1) < half
+    turned_faces = jnp.where(low_half, turned_faces, pltpu.roll(turned_faces, half, 1))
+    turned_courant_ref[8 : 8 + LANES, :] = turned_faces
+    side_face = west_ref[3 * squares : 3 * squares + ROWS, :]
+    side_face = jnp.where(low_half[0:ROWS], side_face, pltpu.roll(side_face, half, 1))
+    turned_courant_ref[0:8, :] = side_face
+
+    def lon_step(tile, carry):
+        start = pl.multiple_of(tile * ROWS, ROWS)
+        taps = divergence_weights(
+            turned_courant_ref[pl.ds(start + 8, ROWS), :],
+            turned_courant_ref[pl.ds(start + 7, ROWS), :],
+        )
+        for square in range(squares):
+            base = square * TURNED_ROWS + start + 5
+            total = taps[0] * turned_ref[pl.ds(base, ROWS), :]
+            for offset in range(1, 7):
+                total = total + taps[offset] * turned_ref[pl.ds(base + offset, ROWS), :]
+            turned_sum_ref[pl.ds(square * LANES + start, ROWS), :] = total
+        return carry
+
+    lax.fori_loop(0, LANES // ROWS, lon_step, 0)
+    for square in range(squares):
+        span = slice(square * LANES, (square + 1) * LANES)
+        lon_ref[span, :] = turned_sum_ref[span, :].T
+
+    together = 4
+
+    def member_step(index, carry):
         swept = [None] * together
         stored = [[None] * levels for _ in range(together)]
         for level in range(levels):
+            inverse = pivot_ref[level, 0]
+            carried = pivot_ref[level, 1]
             for step in range(together):
                 block = (index * together + step) * levels + level
-                base = pl.multiple_of(block * PADDED_ROWS, PADDED_ROWS)
-                total = -lon_ref[pl.ds(pl.multiple_of(block * ROWS, ROWS), ROWS), :]
-                for offset in range(7):
-                    total = (
-                        total
-                        + weight_ref[level, offset] * rows_ref[pl.ds(base + 5 + offset, ROWS), :]
-                    )
-                total = total * pivot_ref[level, 0]
+                span = pl.ds(pl.multiple_of(block * ROWS, ROWS), ROWS)
+                total = (sum_ref[span, :] - lon_ref[span, :]) * inverse
                 if level > 0:
-                    total = total + pivot_ref[level, 1] * swept[step]
+                    total = total + carried * swept[step]
                 swept[step] = total
                 stored[step][level] = total
         for level in range(levels - 1, -1, -1):
+            ratio = pivot_ref[level, 2] if level < levels - 1 else None
             for step in range(together):
                 if level < levels - 1:
-                    swept[step] = stored[step][level] + pivot_ref[level, 2] * swept[step]
+                    swept[step] = stored[step][level] + ratio * swept[step]
                 out_ref[index * together + step, level] = swept[step]
         return carry
 
@@ -340,27 +363,41 @@
     members = blocks // levels
     squares = tracer_rows.shape[0] // lanes
     vmem = pl.BlockSpec(memory_space=pltpu.VMEM)
-    return pl.pallas_call(
-        advect_kernel,
+    params = pltpu.CompilerParams(vmem_limit_bytes=VMEM_BYTES)
+    cost = pl.CostEstimate(flops=6000000, bytes_accessed=4000000, transcendentals=0)
+    lat_sum, response, pivots = pl.pallas_call(
+        lat_kernel,
         out_shape=(
-            jax.ShapeDtypeStruct((members, levels, rows, lanes), jnp.float32),
+            jax.ShapeDtypeStruct(tracer_rows.shape, jnp.float32),
             jax.ShapeDtypeStruct((levels, rows, lanes), jnp.float32),
+            jax.ShapeDtypeStruct((levels, 3, rows, lanes), jnp.float32),
         ),
-        in_specs=[pl.BlockSpec(memory_space=pltpu.SMEM)] + [vmem] * 7,
-        out_specs=(vmem, vmem),
+        in_specs=[pl.BlockSpec(memory_space=pltpu.SMEM)] + [vmem] * 5,
+        out_specs=(vmem,) * 3,
+        scratch_shapes=[
+            pltpu.VMEM(((blocks + 1) * PADDED_ROWS, LANES), jnp.float32),
+            pltpu.VMEM((levels, 7, ROWS, LANES), jnp.float32),
+        ],
+        compiler_params=params,
+        cost_estimate=cost,
+        name="advect_lat",
+    )(lat_place, tracer_rows, courant_rows, mixing, south, north)
+    partial = pl.pallas_call(
+        lon_kernel,
+        out_shape=jax.ShapeDtypeStruct((members, levels, rows, lanes), jnp.float32),
+        in_specs=[vmem] * 6,
+        out_specs=vmem,
         scratch_shapes=[
             pltpu.VMEM((squares * TURNED_ROWS, LANES), jnp.float32),
             pltpu.VMEM((squares * LANES, LANES), jnp.float32),
             pltpu.VMEM((LANES + 8, LANES), jnp.float32),
             pltpu.VMEM((squares * LANES, LANES), jnp.float32),
-            pltpu.VMEM(((blocks + 1) * PADDED_ROWS, LANES), jnp.float32),
-            pltpu.VMEM((levels, 7, ROWS, LANES), jnp.float32),
-            pltpu.VMEM((levels, 3, ROWS, LANES), jnp.float32),
         ],
-        compiler_params=pltpu.CompilerParams(vmem_limit_bytes=VMEM_BYTES),
-        cost_estimate=pl.CostEstimate(flops=12000000, bytes_accessed=ADVECT_BYTES, transcendentals=0),
-        name="advect_and_mix",
-    )(lat_place, tracer_rows, courant_rows, mixing, south, north, west, east)
+        compiler_params=params,
+        cost_estimate=cost,
+        name="advect_lon_and_mix",
+    )(tracer_rows, courant_rows, west, east, lat_sum, pivots)
+    return partial, response
 
 
 def arrhenius(energy, leaf_temp):

time: 36.4 us -> 35.3 us (0.970)
  Pallas kernels: 10.5 us -> 9.79 us
  waiting for transfers between devices: 2.03 us -> 1.45 us
    ppermute x1, waiting for transfers between devices: 2.02 us -> 0.19 us  [per_device(): lax.ppermute(eastward, 'lon', [(i, (i + 1) % lon_count) for i in range(lo...]
    all_to_all x1, waiting for transfers between devices: 0.01 us -> 1.26 us  [per_device(): lax.all_to_all(outgoing, ('lat', 'lon'), split_axis=0, concat_axis=0, til...]
    pallas_call x1, Pallas kernels: 3.04 us -> 2.56 us  [pack(): pl.pallas_call(pack_kernel, out_shape=(jax.ShapeDtypeStruct((tiles, 1, 3...]
    pallas_call x1 -> x2, Pallas kernels: 3.93 us -> 3.67 us  [the longest x1 1.88 us: advect_and_mix(): pl.pallas_call(lon_kernel, out_shape=jax.ShapeDtypeStruct((members, level...]
  transfers between devices with their start and end apart: 5 -> 5, of which waited for: 1 -> 2; matrix products, arithmetic and copies ran while one was open for 0% -> 0% of each run, Pallas kernels for 11% -> 11%
where the time goes in v3:
time: 35.3 us; the launch traced here: 34.7 us
  starting transfers between devices  22.6 us (64%)
  Pallas kernels  9.79 us (28%)
  waiting for transfers between devices  1.45 us (4%)
  between operations  0.72 us (2%)
    all_to_all x1, starting transfers between devices, per_device(): lax.all_to_all(outgoing, ('lat', 'lon'), split_axis=0, concat_axis=0, til...  14.5 us
    ppermute x1, starting transfers between devices, per_device(): lax.ppermute(westward, 'lon', [((i + 1) % lon_count, i) for i in range(lo...  4.18 us
    pallas_call x1, Pallas kernels, fluxes(): pl.pallas_call(flux_kernel, out_shape=(jax.ShapeDtypeStruct(tracer.shape,...  3.56 us
    pallas_call x1, Pallas kernels, pack(): pl.pallas_call(pack_kernel, out_shape=(jax.ShapeDtypeStruct((tiles, 1, 3...  2.56 us
    pallas_call x1, Pallas kernels, advect_and_mix(): pl.pallas_call(lon_kernel, out_shape=jax.ShapeDtypeStruct((members, level...  1.88 us
    pallas_call x1, Pallas kernels, advect_and_mix(): pl.pallas_call(lat_kernel, out_shape=(jax.ShapeDtypeStruct(tracer_rows.sh...  1.79 us
    ppermute x1, starting transfers between devices, per_device(): lax.ppermute(high, 'lat', [(i, (i + 1) % lat_count) for i in range(lat_co...  1.57 us
    ppermute x1, starting transfers between devices, per_device(): lax.ppermute(eastward, 'lon', [(i, (i + 1) % lon_count) for i in range(lo...  1.54 us
  transfers between devices with their start and end apart: 5, of which 2 were waited for; matrix products, arithmetic and copies ran while one was open for 0% of the time, Pallas kernels for 11%

profile of v3, /device:TPU:2, one launch (start us, length us, event | category | flops | bytes accessed | tf_op | source)
XLA Modules:
  0.0 34.7 jit_solution(9018945494363873256)
XLA Ops:
  0.6 0.0 copy-start
  0.6 2.6 %pack.1 = (f32[64,1,384]{2,1,0:T(1,128)}, f32[768,128]{1,0:T(8,128)S(1)}, f32[776,128]{1,0:T(8,128)S(1)}, f32[56,128]{1,0:T(8,128)S(1)}, f32[56,128]{1,0:T(8,128)S(1)}) custom-call(f32[2048,128]{1,0:T(8,128)} %bitcast.5, f32[128,128]{1,0:T(8,128)} %bitcast.8, f32[5,3072]{1,0:T(8,128)} %forcing_hbm.1, s32[1,3072]{1,0:T(1,128)} %bitcast.11, s32[1,3072]{1,0:T(1,128)} %bitcast.12), custom_call_target="tpu_custom_call" | custom-call | flops 300000000 | bytes 2500000 | tf_op jit(solution)/shard_map/pack/pallas_call | solution.py:136
  3.2 1.6 %collective-permute-start.2 = (f32[776,128]{1,0:T(8,128)S(1)}, f32[776,128]{1,0:T(8,128)S(1)}, u32[]{:S(2)}, u32[]{:S(2)}) collective-permute-start(f32[776,128]{1,0:T(8,128)S(1)} %get-tuple-element.13), channel_id=1, source_target_pairs={{0,4},{4,8},{8,12},{12,0},{1,5},{5,9},{9,13},{13,1},{2,6},{6,10},{... | collective-permute-start | bytes 1191944 | tf_op jit(solution)/shard_map/ppermute | solution.py:622
  4.8 0.9 %collective-permute-start.3 = (f32[768,128]{1,0:T(8,128)S(1)}, f32[768,128]{1,0:T(8,128)S(1)}, u32[]{:S(2)}, u32[]{:S(2)}) collective-permute-start(f32[768,128]{1,0:T(8,128)S(1)} %get-tuple-element.14), channel_id=1, source_target_pairs={{4,0},{8,4},{12,8},{0,12},{5,1},{9,5},{13,9},{1,13},{6,2},{10,6},{... | collective-permute-start | bytes 1179656 | tf_op jit(solution)/shard_map/ppermute | solution.py:621
  5.6 0.0 copy-start.4
  5.6 0.0 copy-start.3
  5.7 14.5 %all-to-all-start = ((f32[64,1,384]{2,1,0:T(1,128)}), f32[64,1,384]{2,1,0:T(1,128)S(1)}, u32[]{:S(2)}, u32[]{:S(2)}) async-start(f32[64,1,384]{2,1,0:T(1,128)} %get-tuple-element.10), calls=%async_computation | async-start | bytes 196608 | tf_op jit(solution)/shard_map/all_to_all | solution.py:625
  20.1 0.0 copy-start.1
  20.1 1.5 %collective-permute-start = (f32[56,128]{1,0:T(8,128)S(1)}, f32[56,128]{1,0:T(8,128)S(1)}, u32[]{:S(2)}, u32[]{:S(2)}) collective-permute-start(f32[56,128]{1,0:T(8,128)S(1)} %get-tuple-element.11), channel_id=1, source_target_pairs={{0,16},{16,32},{32,48},{48,64},{64,80},{80,96},{96,112},{112,128},... | collective-permute-start | bytes 86024 | tf_op jit(solution)/shard_map/ppermute | solution.py:623
  21.7 4.2 %collective-permute-start.1 = (f32[56,128]{1,0:T(8,128)S(1)}, f32[56,128]{1,0:T(8,128)S(1)}, u32[]{:S(2)}, u32[]{:S(2)}) collective-permute-start(f32[56,128]{1,0:T(8,128)S(1)} %get-tuple-element.12), channel_id=1, source_target_pairs={{16,0},{32,16},{48,32},{64,48},{80,64},{96,80},{112,96},{128,112},... | collective-permute-start | bytes 86024 | tf_op jit(solution)/shard_map/ppermute | solution.py:624
  25.8 0.1 pad_add_fusion.lat_ref
  25.9 0.0 copy-done.4
  25.9 0.1 copy.10.params_ref
  26.0 0.0 collective-permute-done.3.north_ref
  26.0 0.0 collective-permute-done.2.south_ref
  26.0 0.0 copy-done
  26.0 0.0 copy-done.3
  26.0 0.0 copy-done.1
  26.0 1.8 %advect_lat.1 = (f32[2048,128]{1,0:T(8,128)S(1)}, f32[8,8,128]{2,1,0:T(8,128)S(1)}, f32[8,3,8,128]{3,2,1,0:T(8,128)S(1)}) custom-call(s32[2]{0:T(128)S(1)} %pad_add_fusion.lat_ref, f32[2048,128]{1,0:T(8,128)S(1)} %bitcast.6, f32[128,128]{1,0:T(8,128)S(1)} %bitcast.9, f32[7,8,128]{2,1,0:T(8,128)S(1)} %copy-done.3, ...), custom_call_target="tpu_custom_call" | custom-call | flops 6000000 | bytes 4000000 | tf_op jit(solution)/shard_map/advect_lat/pallas_call | solution.py:368
  27.8 0.2 collective-permute-done.west_ref
  28.0 0.0 collective-permute-done.1.east_ref
  28.0 0.0 copy-start.2
  28.0 1.9 %advect_lon_and_mix.1.partial_ref = f32[32,8,8,128]{3,2,1,0:T(8,128)S(1)} custom-call(f32[2048,128]{1,0:T(8,128)S(1)} %bitcast.7, f32[128,128]{1,0:T(8,128)S(1)} %bitcast.10, f32[56,128]{1,0:T(8,128)S(1)} %collective-permute-done.west_ref, f32[56,128]{1,0:T(8,128)S(1)} %collective-permute-done.1.east_ref, f32[2048,128]{1,0:T(8,128)S(1)} %get-tuple-element.15.sum_ref, ...), custom_call_target="tpu_custom_call" | custom-call | flops 6000000 | bytes 4000000 | tf_op jit(solution)/shard_map/advect_lon_and_mix/pallas_call | solution.py:385
  29.9 1.3 %all-to-all-done.received_ref = f32[64,1,384]{2,1,0:T(1,128)S(1)} async-done(((f32[64,1,384]{2,1,0:T(1,128)}), f32[64,1,384]{2,1,0:T(1,128)S(1)}, u32[]{:S(2)}, u32[]{:S(2)}) %all-to-all-start) | async-done | bytes 98336 | tf_op jit(solution)/shard_map/all_to_all | solution.py:625
  31.2 0.0 copy-done.2
  31.2 3.6 %fluxes.1 = (f32[32,8,8,128]{3,2,1,0:T(8,128)}, f32[32,8,128]{2,1,0:T(8,128)}) custom-call(f32[64,1,384]{2,1,0:T(1,128)S(1)} %all-to-all-done.received_ref, s32[64,64]{1,0:T(8,128)S(1)} %copy-done.2, f32[3,32,16]{2,1,0:T(8,128)S(1)} %copy.10.params_ref, f32[32,8,8,128]{3,2,1,0:T(8,128)S(1)} %copy-done, f32[32,8,8,128]{3,2,1,0:T(8,128)S(1)} %advect_lon_and_mix.1.partial_ref, ...), custom_call_target="tpu_custom_call" | custom-call | flops 600000000 | bytes 3000000 | tf_op jit(solution)/shard_map/fluxes/pallas_call | solution.py:581
Async XLA Ops:
  0.6 25.4 %copy-start = (f32[32,8,8,128]{3,2,1,0:T(8,128)S(1)}, f32[32,8,8,128]{3,2,1,0:T(8,128)}, u32[]{:S(2)}) copy-start(f32[32,8,8,128]{3,2,1,0:T(8,128)} %bottom_ref.1) | copy-start | bytes 3145732
  3.2 22.8 %collective-permute-start.2 = (f32[776,128]{1,0:T(8,128)S(1)}, f32[776,128]{1,0:T(8,128)S(1)}, u32[]{:S(2)}, u32[]{:S(2)}) collective-permute-start(f32[776,128]{1,0:T(8,128)S(1)} %get-tuple-element.13), channel_id=1, source_target_pairs={{0,4},{4,8},{8,12},{12,0},{1,5},{5,9},{9,13},{13,1},{2,6},{6,10},{... | collective-permute-start | bytes 1191944 | tf_op jit(solution)/shard_map/ppermute | solution.py:622
  4.8 21.2 %collective-permute-start.3 = (f32[768,128]{1,0:T(8,128)S(1)}, f32[768,128]{1,0:T(8,128)S(1)}, u32[]{:S(2)}, u32[]{:S(2)}) collective-permute-start(f32[768,128]{1,0:T(8,128)S(1)} %get-tuple-element.14), channel_id=1, source_target_pairs={{4,0},{8,4},{12,8},{0,12},{5,1},{9,5},{13,9},{1,13},{6,2},{10,6},{... | collective-permute-start | bytes 1179656 | tf_op jit(solution)/shard_map/ppermute | solution.py:621
  5.6 20.3 %copy-start.4 = (f32[3,32,16]{1,2,0:T(8,128)S(1)}, f32[3,32,16]{1,2,0:T(8,128)}, u32[]{:S(2)}) copy-start(f32[3,32,16]{1,2,0:T(8,128)} %param.13) | copy-start | bytes 18436
  5.6 20.4 %copy-start.3 = (f32[7,8,128]{2,1,0:T(8,128)S(1)}, f32[7,8,128]{2,1,0:T(8,128)}, u32[]{:S(2)}) copy-start(f32[7,8,128]{2,1,0:T(8,128)} %mixing_ref.1) | copy-start | bytes 86020
  5.7 25.5 %all-to-all-start = ((f32[64,1,384]{2,1,0:T(1,128)}), f32[64,1,384]{2,1,0:T(1,128)S(1)}, u32[]{:S(2)}, u32[]{:S(2)}) async-start(f32[64,1,384]{2,1,0:T(1,128)} %get-tuple-element.10), calls=%async_computation | async-start | bytes 196608 | tf_op jit(solution)/shard_map/all_to_all | solution.py:625
  20.1 5.9 %copy-start.1 = (f32[2,8,8,128]{3,2,1,0:T(8,128)S(1)}, f32[2,8,8,128]{3,2,1,0:T(8,128)}, u32[]{:S(2)}) copy-start(f32[2,8,8,128]{3,2,1,0:T(8,128)} %param.9) | copy-start | bytes 196612
  20.1 7.9 %collective-permute-start = (f32[56,128]{1,0:T(8,128)S(1)}, f32[56,128]{1,0:T(8,128)S(1)}, u32[]{:S(2)}, u32[]{:S(2)}) collective-permute-start(f32[56,128]{1,0:T(8,128)S(1)} %get-tuple-element.11), channel_id=1, source_target_pairs={{0,16},{16,32},{32,48},{48,64},{64,80},{80,96},{96,112},{112,128},... | collective-permute-start | bytes 86024 | tf_op jit(solution)/shard_map/ppermute | solution.py:623
  21.7 6.4 %collective-permute-start.1 = (f32[56,128]{1,0:T(8,128)S(1)}, f32[56,128]{1,0:T(8,128)S(1)}, u32[]{:S(2)}, u32[]{:S(2)}) collective-permute-start(f32[56,128]{1,0:T(8,128)S(1)} %get-tuple-element.12), channel_id=1, source_target_pairs={{16,0},{32,16},{48,32},{64,48},{80,64},{96,80},{112,96},{128,112},... | collective-permute-start | bytes 86024 | tf_op jit(solution)/shard_map/ppermute | solution.py:624
  28.0 3.1 %copy-start.2 = (s32[64,64]{1,0:T(8,128)S(1)}, s32[64,64]{1,0:T(8,128)}, u32[]{:S(2)}) copy-start(s32[64,64]{1,0:T(8,128)} %cell_ref.1) | copy-start | bytes 49156

commit v4 on v3

--- a/solution.py
+++ b/solution.py
@@ -13,6 +13,7 @@
 ROWS = 8
 VMEM_BYTES = 40 * 2**20
 PARTS = 2
+OUT_COPIES = 4
 
 
 def nt_dot(left, right):
@@ -202,6 +203,7 @@
     return taps
 
 
+CHUNK = 4
 TURNED_ROWS = LANES + 16
 PADDED_ROWS = 2 * ROWS
 
@@ -286,8 +288,8 @@
 
 
 def lon_kernel(
-    tracer_ref, courant_ref, west_ref, east_ref, sum_ref, pivot_ref,
-    out_ref,
+    tracer_ref, courant_ref, west_ref, east_ref, sum_ref, pivot_ref, cell_ref,
+    out_ref, leaf_ref, place_ref,
     turned_ref, turned_sum_ref, turned_courant_ref, lon_ref,
 ):
     members, levels = out_ref.shape[0], out_ref.shape[1]
@@ -355,9 +357,69 @@
         return carry
 
     lax.fori_loop(0, members // together, member_step, 0)
-
-
-def advect_and_mix(lat_place, tracer_rows, courant_rows, mixing, south, north, west, east):
+    near_cells(tracer_ref, cell_ref, leaf_ref, place_ref, members, levels)
+
+
+def near_cells(tracer_ref, cell_ref, leaf_ref, place_ref, members, levels):
+    sources = cell_ref.shape[0]
+    groups = sources // 2
+    quarters = ROWS // 2
+    stride = levels * ROWS
+    bottom = jnp.concatenate(
+        [
+            jnp.concatenate(
+                [
+                    tracer_ref[pl.ds(2 * quarter + side, members, stride=stride), :]
+                    for side in range(2)
+                ],
+                axis=1,
+            )
+            for quarter in range(quarters)
+        ],
+        axis=0,
+    )
+    bottom_parts = jnp.concatenate(bf16_parts(bottom, 2), axis=0)
+    cells = jnp.concatenate(
+        [cell_ref[pl.ds(tile, sources // 4, stride=4), :] for tile in range(4)], axis=0
+    )
+    cells = jnp.concatenate([cells[0:groups], cells[groups : 2 * groups]], axis=1)
+    place_ref[0] = jnp.right_shift(cells, 8).astype(jnp.float32)
+    lane = jnp.bitwise_and(cells, 255).astype(jnp.float32)
+    place_ref[1] = lane
+    cell_ids = (
+        lax.broadcasted_iota(jnp.int32, (256, LANES), 0).astype(jnp.float32).astype(jnp.bfloat16)
+    )
+    one, zero = jnp.bfloat16(1.0), jnp.bfloat16(0.0)
+    for chunk in range(groups // CHUNK):
+        rows = range(chunk * CHUNK, (chunk + 1) * CHUNK)
+        span = slice(chunk * CHUNK * LANES, (chunk + 1) * CHUNK * LANES)
+        cell_onehot = jnp.concatenate(
+            [
+                jnp.where(cell_ids == lane[row : row + 1, :].astype(jnp.bfloat16), one, zero)
+                for row in rows
+            ],
+            axis=1,
+        )
+        near = jnp.dot(bottom_parts, cell_onehot, preferred_element_type=jnp.float32)
+        near = near[0 : quarters * members] + near[quarters * members : 2 * quarters * members]
+        quarter_index = jnp.concatenate(
+            [
+                jnp.broadcast_to(place_ref[0, row : row + 1, :], (members, LANES))
+                for row in rows
+            ],
+            axis=1,
+        )
+        picked = near[0:members]
+        for quarter in range(1, quarters):
+            picked = jnp.where(
+                quarter_index == quarter, near[quarter * members : (quarter + 1) * members], picked
+            )
+        leaf_ref[:, span] = 280.0 + 70.0 * picked
+
+
+def advect_and_mix(
+    lat_place, tracer_rows, courant_rows, mixing, south, north, west, east, recv_cell
+):
     levels, rows, lanes = mixing.shape[0] + 1, mixing.shape[1], mixing.shape[2]
     blocks = tracer_rows.shape[0] // rows
     members = blocks // levels
@@ -382,11 +444,17 @@
         cost_estimate=cost,
         name="advect_lat",
     )(lat_place, tracer_rows, courant_rows, mixing, south, north)
-    partial = pl.pallas_call(
+    sources, places = recv_cell.shape
+    place_count = sources * places
+    partial, leaf, place = pl.pallas_call(
         lon_kernel,
-        out_shape=jax.ShapeDtypeStruct((members, levels, rows, lanes), jnp.float32),
-        in_specs=[vmem] * 6,
-        out_specs=vmem,
+        out_shape=(
+            jax.ShapeDtypeStruct((members, levels, rows, lanes), jnp.float32),
+            jax.ShapeDtypeStruct((members, place_count), jnp.float32),
+            jax.ShapeDtypeStruct((2, place_count // LANES, LANES), jnp.float32),
+        ),
+        in_specs=[vmem] * 7,
+        out_specs=(vmem,) * 3,
         scratch_shapes=[
             pltpu.VMEM((squares * TURNED_ROWS, LANES), jnp.float32),
             pltpu.VMEM((squares * LANES, LANES), jnp.float32),
@@ -396,26 +464,24 @@
         compiler_params=params,
         cost_estimate=cost,
         name="advect_lon_and_mix",
-    )(tracer_rows, courant_rows, west, east, lat_sum, pivots)
-    return partial, response
+    )(tracer_rows, courant_rows, west, east, lat_sum, pivots, recv_cell)
+    return partial, response, leaf, place
 
 
 def arrhenius(energy, leaf_temp):
     return jnp.exp(energy * (leaf_temp - 25.0) / (298.15 * GAS_CONSTANT * (leaf_temp + 273.15)))
 
 
-CHUNK = 4
-
-
 def flux_kernel(
-    received_ref, cell_ref, params_ref, bottom_ref, partial_ref, response_ref,
+    received_ref, params_ref, leaf_ref, place_ref, partial_ref, response_ref,
     out_ref, surface_ref,
-    column_ref, left_ref, right_ref, result_ref, copy_sems,
+    column_ref, result_ref, copy_sems,
 ):
     members = params_ref.shape[1]
     types = params_ref.shape[2]
-    sources, places = cell_ref.shape
+    sources = received_ref.shape[0]
     groups = sources // 2
+    places = LANES // 2
     levels = response_ref.shape[0]
     quarters = ROWS // 2
     one, zero = jnp.bfloat16(1.0), jnp.bfloat16(0.0)
@@ -426,16 +492,6 @@
         axis=0,
     )
     table_parts = jnp.concatenate(bf16_parts(tables, 2), axis=1)
-    bottom = jnp.concatenate(
-        [
-            jnp.concatenate(
-                [bottom_ref[:, 0, 2 * quarter, :], bottom_ref[:, 0, 2 * quarter + 1, :]], axis=1
-            )
-            for quarter in range(quarters)
-        ],
-        axis=0,
-    )
-    bottom_parts = jnp.concatenate(bf16_parts(bottom, 2), axis=0)
 
     half = lax.broadcasted_iota(jnp.int32, (groups, LANES), 1) < places
 
@@ -463,86 +519,72 @@
     column_ref[6] = 2.8 * absorbed
     column_ref[7] = (1.4 * 8.0) * compensation
     column_ref[8] = plant
-    cells = jnp.concatenate(
-        [cell_ref[pl.ds(tile, sources // 4, stride=4), :] for tile in range(4)], axis=0
-    )
-    cells = jnp.concatenate([cells[0:groups], cells[groups : 2 * groups]], axis=1)
-    column_ref[9] = jnp.right_shift(cells, 8).astype(jnp.float32)
-    column_ref[10] = jnp.bitwise_and(cells, 255).astype(jnp.float32)
-
-    def ids(count, mask):
-        return (
-            jnp.bitwise_and(lax.broadcasted_iota(jnp.int32, (count, LANES), 0), mask)
-            .astype(jnp.float32)
-            .astype(jnp.bfloat16)
-        )
-
-    cell_ids = ids(256, 255)
-    type_ids = ids(2 * types, types - 1)
-
+
+    type_ids = (
+        jnp.bitwise_and(lax.broadcasted_iota(jnp.int32, (2 * types, LANES), 0), types - 1)
+        .astype(jnp.float32)
+        .astype(jnp.bfloat16)
+    )
+
+    cell_ids = (
+        lax.broadcasted_iota(jnp.int32, (256, LANES), 0).astype(jnp.float32).astype(jnp.bfloat16)
+    )
+    lefts, onehots = [], []
     for chunk in range(groups // CHUNK):
         rows = range(chunk * CHUNK, (chunk + 1) * CHUNK)
         span = slice(chunk * CHUNK * LANES, (chunk + 1) * CHUNK * LANES)
 
-        def spread(quantity, count=members):
+        def spread(ref):
             return jnp.concatenate(
-                [
-                    jnp.broadcast_to(column_ref[quantity, row : row + 1, :], (count, LANES))
-                    for row in rows
-                ],
+                [jnp.broadcast_to(ref[row : row + 1, :], (members, LANES)) for row in rows],
                 axis=1,
             )
 
-        def onehot(row_ids, quantity):
-            return jnp.concatenate(
-                [
-                    jnp.where(
-                        row_ids == column_ref[quantity, row : row + 1, :].astype(jnp.bfloat16),
-                        one,
-                        zero,
-                    )
-                    for row in rows
-                ],
-                axis=1,
-            )
-
-        cell_onehot = onehot(cell_ids, 10)
-        right_ref[:, span] = cell_onehot
-        near = jnp.dot(bottom_parts, cell_onehot, preferred_element_type=jnp.float32)
-        near = near[0 : quarters * members] + near[quarters * members : 2 * quarters * members]
-        quarter_index = spread(9)
-        picked = near[0:members]
-        for quarter in range(1, quarters):
-            picked = jnp.where(
-                quarter_index == quarter, near[quarter * members : (quarter + 1) * members], picked
-            )
-        params = jnp.dot(
-            table_parts, onehot(type_ids, 8), preferred_element_type=jnp.float32
-        )
-        carbon_leaf = 280.0 + 70.0 * picked
-        warm = spread(1)
+        type_onehot = jnp.concatenate(
+            [
+                jnp.where(
+                    type_ids == column_ref[8, row : row + 1, :].astype(jnp.bfloat16), one, zero
+                )
+                for row in rows
+            ],
+            axis=1,
+        )
+        params = jnp.dot(table_parts, type_onehot, preferred_element_type=jnp.float32)
+        carbon_leaf = leaf_ref[:, span]
+        warm = spread(column_ref.at[1])
         carboxylation = params[0:members] * warm
-        transport_max = params[members : 2 * members] * spread(2)
+        transport_max = params[members : 2 * members] * spread(column_ref.at[2])
         respiration = params[2 * members : 3 * members] * warm
-        total_rate = spread(0) + transport_max
-        square = total_rate * total_rate - spread(6) * transport_max
+        total_rate = spread(column_ref.at[0]) + transport_max
+        square = total_rate * total_rate - spread(column_ref.at[6]) * transport_max
         electron_rate = total_rate - square * lax.rsqrt(square)
-        excess = carbon_leaf - spread(4)
-        rubisco_base = carbon_leaf + spread(3)
-        light_base = (1.4 * 4.0) * carbon_leaf + spread(7)
+        excess = carbon_leaf - spread(column_ref.at[4])
+        rubisco_base = carbon_leaf + spread(column_ref.at[3])
+        light_base = (1.4 * 4.0) * carbon_leaf + spread(column_ref.at[7])
         shared = excess / (rubisco_base * light_base)
         rubisco_rate = carboxylation * light_base * shared
         light_rate = electron_rate * rubisco_base * shared
-        flux = spread(5) * (jnp.minimum(rubisco_rate, light_rate) - respiration)
+        flux = spread(column_ref.at[5]) * (jnp.minimum(rubisco_rate, light_rate) - respiration)
         high, low = bf16_parts(flux, 2)
-        quarter_index = quarter_index.astype(jnp.bfloat16)
+        quarter_index = spread(place_ref.at[0]).astype(jnp.bfloat16)
+        left = []
         for quarter in range(quarters):
             here = quarter_index == jnp.bfloat16(quarter)
-            start = quarter * 2 * members
-            left_ref[start : start + members, span] = jnp.where(here, high, zero)
-            left_ref[start + members : start + 2 * members, span] = jnp.where(here, low, zero)
-
-    summed = nt_dot(left_ref[...], right_ref[...])
+            left.append(jnp.where(here, high, zero))
+            left.append(jnp.where(here, low, zero))
+        cell_onehot = jnp.concatenate(
+            [
+                jnp.where(
+                    cell_ids == place_ref[1, row : row + 1, :].astype(jnp.bfloat16), one, zero
+                )
+                for row in rows
+            ],
+            axis=1,
+        )
+        lefts.append(jnp.concatenate(left, axis=0))
+        onehots.append(cell_onehot)
+
+    summed = nt_dot(jnp.concatenate(lefts, axis=1), jnp.concatenate(onehots, axis=1))
     for quarter in range(quarters):
         start = quarter * 2 * members
         total = summed[start : start + members] + summed[start + members : start + 2 * members]
@@ -550,19 +592,14 @@
         surface_ref[:, 2 * quarter + 1, :] = total[:, LANES : 2 * LANES]
 
     copies = []
-    quarter = members // 4
-    for part in range(4):
-
-        def member_step(member, carry):
+    share = members // OUT_COPIES
+    for part in range(OUT_COPIES):
+        responses = [response_ref[level] for level in range(levels)]
+        for member in range(part * share, (part + 1) * share):
             surface = surface_ref[member]
             for level in range(levels):
-                result_ref[member, level] = (
-                    partial_ref[member, level] + response_ref[level] * surface
-                )
-            return carry
-
-        lax.fori_loop(part * quarter, (part + 1) * quarter, member_step, 0, unroll=4)
-        span = pl.ds(part * quarter, quarter)
+                result_ref[member, level] = partial_ref[member, level] + responses[level] * surface
+        span = pl.ds(part * share, share)
         copy = pltpu.make_async_copy(result_ref.at[span], out_ref.at[span], copy_sems.at[part])
         copy.start()
         copies.append(copy)
@@ -570,44 +607,26 @@
         copy.wait()
 
 
-def fluxes(received, recv_cell, land_params, tracer, partial, response):
-    members, levels, rows, lanes = tracer.shape
-    tiles = received.shape[0]
-    place_count = recv_cell.shape[0] * recv_cell.shape[1]
-
-    def whole(array):
-        return pl.BlockSpec(array.shape, lambda step: (0,) * array.ndim)
-
+def fluxes(received, land_params, leaf, place, partial, response):
+    members, levels, rows, lanes = partial.shape
+    vmem = pl.BlockSpec(memory_space=pltpu.VMEM)
     return pl.pallas_call(
         flux_kernel,
         out_shape=(
-            jax.ShapeDtypeStruct(tracer.shape, jnp.float32),
+            jax.ShapeDtypeStruct(partial.shape, jnp.float32),
             jax.ShapeDtypeStruct((members, rows, lanes), jnp.float32),
         ),
-        in_specs=[
-            whole(received),
-            whole(recv_cell),
-            whole(land_params),
-            pl.BlockSpec((members, 1, rows, lanes), lambda step: (0, 0, 0, 0)),
-            whole(partial),
-            whole(response),
-        ],
-        out_specs=(
-            pl.BlockSpec(memory_space=pltpu.HBM),
-            pl.BlockSpec((members, rows, lanes), lambda step: (0, 0, 0)),
-        ),
-        grid=(1,),
+        in_specs=[vmem] * 6,
+        out_specs=(pl.BlockSpec(memory_space=pltpu.HBM), vmem),
         scratch_shapes=[
-            pltpu.VMEM((11, tiles // 2, LANES), jnp.float32),
-            pltpu.VMEM((ROWS * members, place_count), jnp.bfloat16),
-            pltpu.VMEM((256, place_count), jnp.bfloat16),
-            pltpu.VMEM(tracer.shape, jnp.float32),
-            pltpu.SemaphoreType.DMA((4,)),
+            pltpu.VMEM((9, received.shape[0] // 2, LANES), jnp.float32),
+            pltpu.VMEM(partial.shape, jnp.float32),
+            pltpu.SemaphoreType.DMA((OUT_COPIES,)),
         ],
         compiler_params=pltpu.CompilerParams(vmem_limit_bytes=VMEM_BYTES),
         cost_estimate=pl.CostEstimate(flops=600000000, bytes_accessed=3000000, transcendentals=400000),
         name="fluxes",
-    )(received, recv_cell, land_params, tracer, partial, response)
+    )(received, land_params, leaf, place, partial, response)
 
 
 def per_device(tracer, courant, mixing, forcing, plant_type, land_params, send_slot, recv_cell):
@@ -624,10 +643,10 @@
     east = lax.ppermute(westward, "lon", [((i + 1) % lon_count, i) for i in range(lon_count)])
     received = lax.all_to_all(outgoing, ("lat", "lon"), split_axis=0, concat_axis=0, tiled=True)
     lat_place = jnp.stack([lax.axis_index("lat"), jnp.int32(lat_count)]).astype(jnp.int32)
-    partial, response = advect_and_mix(
-        lat_place, tracer_rows, courant_rows, mixing, south, north, west, east
-    )
-    return fluxes(received, recv_cell, land_params, tracer, partial, response)
+    partial, response, leaf, place = advect_and_mix(
+        lat_place, tracer_rows, courant_rows, mixing, south, north, west, east, recv_cell
+    )
+    return fluxes(received, land_params, leaf, place, partial, response)
 
 
 def solution(mesh):

time: 35.3 us -> 34.9 us (0.989)
  waiting for transfers between devices: 1.45 us -> 0.64 us
    all_to_all x1, waiting for transfers between devices: 1.26 us -> 0.45 us  [per_device(): lax.all_to_all(outgoing, ('lat', 'lon'), split_axis=0, concat_axis=0, til...]
  transfers between devices with their start and end apart: 5 -> 5, of which waited for: 2 -> 2; matrix products, arithmetic and copies ran while one was open for 0% -> 0% of each run, Pallas kernels for 11% -> 13%
where the time goes in v4:
time: 34.9 us; the launch traced here: 34.3 us
  starting transfers between devices  22.6 us (65%)
  Pallas kernels  10.1 us (29%)
  between operations  0.73 us (2%)
  waiting for transfers between devices  0.64 us (2%)
    all_to_all x1, starting transfers between devices, per_device(): lax.all_to_all(outgoing, ('lat', 'lon'), split_axis=0, concat_axis=0, til...  14.5 us
    ppermute x1, starting transfers between devices, per_device(): lax.ppermute(westward, 'lon', [((i + 1) % lon_count, i) for i in range(lo...  4.18 us
    pallas_call x1, Pallas kernels, fluxes(): pl.pallas_call(flux_kernel, out_shape=(jax.ShapeDtypeStruct(partial.shape...  3.08 us
    pallas_call x1, Pallas kernels, advect_and_mix(): pl.pallas_call(lon_kernel, out_shape=(jax.ShapeDtypeStruct((members, leve...  2.68 us
    pallas_call x1, Pallas kernels, pack(): pl.pallas_call(pack_kernel, out_shape=(jax.ShapeDtypeStruct((tiles, 1, 3...  2.56 us
    pallas_call x1, Pallas kernels, advect_and_mix(): pl.pallas_call(lat_kernel, out_shape=(jax.ShapeDtypeStruct(tracer_rows.sh...  1.79 us
    ppermute x1, starting transfers between devices, per_device(): lax.ppermute(high, 'lat', [(i, (i + 1) % lat_count) for i in range(lat_co...  1.57 us
    ppermute x1, starting transfers between devices, per_device(): lax.ppermute(eastward, 'lon', [(i, (i + 1) % lon_count) for i in range(lo...  1.54 us
  transfers between devices with their start and end apart: 5, of which 2 were waited for; matrix products, arithmetic and copies ran while one was open for 0% of the time, Pallas kernels for 13%

profile of v4, /device:TPU:2, one launch (start us, length us, event | category | flops | bytes accessed | tf_op | source)
XLA Modules:
  0.0 34.3 jit_solution(5122692621952483090)
XLA Ops:
  0.6 0.0 copy-start
  0.6 2.6 %pack.1 = (f32[64,1,384]{2,1,0:T(1,128)}, f32[768,128]{1,0:T(8,128)S(1)}, f32[776,128]{1,0:T(8,128)S(1)}, f32[56,128]{1,0:T(8,128)S(1)}, f32[56,128]{1,0:T(8,128)S(1)}) custom-call(f32[2048,128]{1,0:T(8,128)} %bitcast.5, f32[128,128]{1,0:T(8,128)} %bitcast.8, f32[5,3072]{1,0:T(8,128)} %forcing_hbm.1, s32[1,3072]{1,0:T(1,128)} %bitcast.11, s32[1,3072]{1,0:T(1,128)} %bitcast.12), custom_call_target="tpu_custom_call" | custom-call | flops 300000000 | bytes 2500000 | tf_op jit(solution)/shard_map/pack/pallas_call | solution.py:137
  3.2 1.6 %collective-permute-start.2 = (f32[776,128]{1,0:T(8,128)S(1)}, f32[776,128]{1,0:T(8,128)S(1)}, u32[]{:S(2)}, u32[]{:S(2)}) collective-permute-start(f32[776,128]{1,0:T(8,128)S(1)} %get-tuple-element.16), channel_id=1, source_target_pairs={{0,4},{4,8},{8,12},{12,0},{1,5},{5,9},{9,13},{13,1},{2,6},{6,10},{... | collective-permute-start | bytes 1191944 | tf_op jit(solution)/shard_map/ppermute | solution.py:641
  4.8 0.9 %collective-permute-start.3 = (f32[768,128]{1,0:T(8,128)S(1)}, f32[768,128]{1,0:T(8,128)S(1)}, u32[]{:S(2)}, u32[]{:S(2)}) collective-permute-start(f32[768,128]{1,0:T(8,128)S(1)} %get-tuple-element.17), channel_id=1, source_target_pairs={{4,0},{8,4},{12,8},{0,12},{5,1},{9,5},{13,9},{1,13},{6,2},{10,6},{... | collective-permute-start | bytes 1179656 | tf_op jit(solution)/shard_map/ppermute | solution.py:640
  5.6 0.0 copy-start.4
  5.6 0.0 copy-start.3
  5.7 14.5 %all-to-all-start = ((f32[64,1,384]{2,1,0:T(1,128)}), f32[64,1,384]{2,1,0:T(1,128)S(1)}, u32[]{:S(2)}, u32[]{:S(2)}) async-start(f32[64,1,384]{2,1,0:T(1,128)} %get-tuple-element.13), calls=%async_computation | async-start | bytes 196608 | tf_op jit(solution)/shard_map/all_to_all | solution.py:644
  20.1 0.0 copy-start.1
  20.1 1.5 %collective-permute-start = (f32[56,128]{1,0:T(8,128)S(1)}, f32[56,128]{1,0:T(8,128)S(1)}, u32[]{:S(2)}, u32[]{:S(2)}) collective-permute-start(f32[56,128]{1,0:T(8,128)S(1)} %get-tuple-element.14), channel_id=1, source_target_pairs={{0,16},{16,32},{32,48},{48,64},{64,80},{80,96},{96,112},{112,128},... | collective-permute-start | bytes 86024 | tf_op jit(solution)/shard_map/ppermute | solution.py:642
  21.7 4.2 %collective-permute-start.1 = (f32[56,128]{1,0:T(8,128)S(1)}, f32[56,128]{1,0:T(8,128)S(1)}, u32[]{:S(2)}, u32[]{:S(2)}) collective-permute-start(f32[56,128]{1,0:T(8,128)S(1)} %get-tuple-element.15), channel_id=1, source_target_pairs={{16,0},{32,16},{48,32},{64,48},{80,64},{96,80},{112,96},{128,112},... | collective-permute-start | bytes 86024 | tf_op jit(solution)/shard_map/ppermute | solution.py:643
  25.8 0.1 pad_add_fusion.lat_ref
  25.9 0.0 copy-done.4
  25.9 0.1 copy.10.params_ref
  26.0 0.0 copy-start.2
  26.0 0.0 collective-permute-done.3.north_ref
  26.0 0.0 collective-permute-done.2.south_ref
  26.0 0.0 copy-done
  26.0 0.0 copy-done.3
  26.0 0.0 copy-done.1
  26.1 1.8 %advect_lat.1 = (f32[2048,128]{1,0:T(8,128)S(1)}, f32[8,8,128]{2,1,0:T(8,128)S(1)}, f32[8,3,8,128]{3,2,1,0:T(8,128)S(1)}) custom-call(s32[2]{0:T(128)S(1)} %pad_add_fusion.lat_ref, f32[2048,128]{1,0:T(8,128)S(1)} %bitcast.6, f32[128,128]{1,0:T(8,128)S(1)} %bitcast.9, f32[7,8,128]{2,1,0:T(8,128)S(1)} %copy-done.3, ...), custom_call_target="tpu_custom_call" | custom-call | flops 6000000 | bytes 4000000 | tf_op jit(solution)/shard_map/advect_lat/pallas_call | solution.py:430
  27.9 0.2 collective-permute-done.west_ref
  28.0 0.0 collective-permute-done.1.east_ref
  28.0 0.0 copy-done.2
  28.0 2.7 %advect_lon_and_mix.1 = (f32[32,8,8,128]{3,2,1,0:T(8,128)S(1)}, f32[32,4096]{1,0:T(8,128)S(1)}, f32[2,32,128]{2,1,0:T(8,128)S(1)}) custom-call(f32[2048,128]{1,0:T(8,128)S(1)} %bitcast.7, f32[128,128]{1,0:T(8,128)S(1)} %bitcast.10, f32[56,128]{1,0:T(8,128)S(1)} %collective-permute-done.west_ref, f32[56,128]{1,0:T(8,128)S(1)} %collective-permute-done.1.east_ref, ...), custom_call_target="tpu_custom_call" | custom-call | flops 6000000 | bytes 4000000 | tf_op jit(solution)/shard_map/advect_lon_and_mix/pallas_call | solution.py:449
  30.7 0.4 %all-to-all-done.received_ref = f32[64,1,384]{2,1,0:T(1,128)S(1)} async-done(((f32[64,1,384]{2,1,0:T(1,128)}), f32[64,1,384]{2,1,0:T(1,128)S(1)}, u32[]{:S(2)}, u32[]{:S(2)}) %all-to-all-start) | async-done | bytes 98336 | tf_op jit(solution)/shard_map/all_to_all | solution.py:644
  31.2 3.1 %fluxes.1 = (f32[32,8,8,128]{3,2,1,0:T(8,128)}, f32[32,8,128]{2,1,0:T(8,128)}) custom-call(f32[64,1,384]{2,1,0:T(1,128)S(1)} %all-to-all-done.received_ref, f32[3,32,16]{2,1,0:T(8,128)S(1)} %copy.10.params_ref, f32[32,4096]{1,0:T(8,128)S(1)} %get-tuple-element.20.leaf_ref, f32[2,32,128]{2,1,0:T(8,128)S(1)} %get-tuple-element.21.place_ref, ...), custom_call_target="tpu_custom_call" | custom-call | flops 600000000 | bytes 3000000 | tf_op jit(solution)/shard_map/fluxes/pallas_call | solution.py:613
Async XLA Ops:
  0.6 25.4 %copy-start = (f32[32,8,8,128]{3,2,1,0:T(8,128)S(1)}, f32[32,8,8,128]{3,2,1,0:T(8,128)}, u32[]{:S(2)}) copy-start(f32[32,8,8,128]{3,2,1,0:T(8,128)} %param.8) | copy-start | bytes 3145732
  3.2 22.8 %collective-permute-start.2 = (f32[776,128]{1,0:T(8,128)S(1)}, f32[776,128]{1,0:T(8,128)S(1)}, u32[]{:S(2)}, u32[]{:S(2)}) collective-permute-start(f32[776,128]{1,0:T(8,128)S(1)} %get-tuple-element.16), channel_id=1, source_target_pairs={{0,4},{4,8},{8,12},{12,0},{1,5},{5,9},{9,13},{13,1},{2,6},{6,10},{... | collective-permute-start | bytes 1191944 | tf_op jit(solution)/shard_map/ppermute | solution.py:641
  4.8 21.2 %collective-permute-start.3 = (f32[768,128]{1,0:T(8,128)S(1)}, f32[768,128]{1,0:T(8,128)S(1)}, u32[]{:S(2)}, u32[]{:S(2)}) collective-permute-start(f32[768,128]{1,0:T(8,128)S(1)} %get-tuple-element.17), channel_id=1, source_target_pairs={{4,0},{8,4},{12,8},{0,12},{5,1},{9,5},{13,9},{1,13},{6,2},{10,6},{... | collective-permute-start | bytes 1179656 | tf_op jit(solution)/shard_map/ppermute | solution.py:640
  5.6 20.3 %copy-start.4 = (f32[3,32,16]{1,2,0:T(8,128)S(1)}, f32[3,32,16]{1,2,0:T(8,128)}, u32[]{:S(2)}) copy-start(f32[3,32,16]{1,2,0:T(8,128)} %param.13) | copy-start | bytes 18436
  5.6 20.4 %copy-start.3 = (f32[7,8,128]{2,1,0:T(8,128)S(1)}, f32[7,8,128]{2,1,0:T(8,128)}, u32[]{:S(2)}) copy-start(f32[7,8,128]{2,1,0:T(8,128)} %mixing_ref.1) | copy-start | bytes 86020
  5.7 25.5 %all-to-all-start = ((f32[64,1,384]{2,1,0:T(1,128)}), f32[64,1,384]{2,1,0:T(1,128)S(1)}, u32[]{:S(2)}, u32[]{:S(2)}) async-start(f32[64,1,384]{2,1,0:T(1,128)} %get-tuple-element.13), calls=%async_computation | async-start | bytes 196608 | tf_op jit(solution)/shard_map/all_to_all | solution.py:644
  20.1 5.9 %copy-start.1 = (f32[2,8,8,128]{3,2,1,0:T(8,128)S(1)}, f32[2,8,8,128]{3,2,1,0:T(8,128)}, u32[]{:S(2)}) copy-start(f32[2,8,8,128]{3,2,1,0:T(8,128)} %param.9) | copy-start | bytes 196612
  20.1 7.9 %collective-permute-start = (f32[56,128]{1,0:T(8,128)S(1)}, f32[56,128]{1,0:T(8,128)S(1)}, u32[]{:S(2)}, u32[]{:S(2)}) collective-permute-start(f32[56,128]{1,0:T(8,128)S(1)} %get-tuple-element.14), channel_id=1, source_target_pairs={{0,16},{16,32},{32,48},{48,64},{64,80},{80,96},{96,112},{112,128},... | collective-permute-start | bytes 86024 | tf_op jit(solution)/shard_map/ppermute | solution.py:642
  21.7 6.4 %collective-permute-start.1 = (f32[56,128]{1,0:T(8,128)S(1)}, f32[56,128]{1,0:T(8,128)S(1)}, u32[]{:S(2)}, u32[]{:S(2)}) collective-permute-start(f32[56,128]{1,0:T(8,128)S(1)} %get-tuple-element.15), channel_id=1, source_target_pairs={{16,0},{32,16},{48,32},{64,48},{80,64},{96,80},{112,96},{128,112},... | collective-permute-start | bytes 86024 | tf_op jit(solution)/shard_map/ppermute | solution.py:643
  26.0 2.0 %copy-start.2 = (s32[64,64]{1,0:T(8,128)S(1)}, s32[64,64]{1,0:T(8,128)}, u32[]{:S(2)}) copy-start(s32[64,64]{1,0:T(8,128)} %cell_ref.1) | copy-start | bytes 49156

commit v5 on v4

--- a/solution.py
+++ b/solution.py
@@ -34,7 +34,7 @@
 
 def pack_kernel(
     tracer_hbm, courant_hbm, forcing_hbm, type_hbm, slot_hbm,
-    payload_ref, low_ref, high_ref, westward_ref, eastward_ref,
+    payload_ref, first_ref, second_ref, westward_ref, eastward_ref,
     cells_ref, faces_ref, forcing_ref, type_ref, slot_ref, copy_sems,
 ):
     moves = (
@@ -107,16 +107,16 @@
         copy.wait()
     blocks = cells_ref.shape[0] // ROWS
     levels = faces_ref.shape[0] // (2 * ROWS)
+    even = lax.rem(lax.axis_index("lat"), 2) == 0
     for step in range(3):
-        low_ref[step * blocks : (step + 1) * blocks, :] = cells_ref[
-            pl.ds(step, blocks, stride=ROWS), :
-        ]
-        high_ref[step * blocks : (step + 1) * blocks, :] = cells_ref[
-            pl.ds(ROWS - 3 + step, blocks, stride=ROWS), :
-        ]
-    high_ref[3 * blocks : 3 * blocks + levels, :] = faces_ref[
-        pl.ds(levels * ROWS + ROWS - 1, levels, stride=ROWS), :
-    ]
+        low = cells_ref[pl.ds(step, blocks, stride=ROWS), :]
+        high = cells_ref[pl.ds(ROWS - 3 + step, blocks, stride=ROWS), :]
+        span = slice(step * blocks, (step + 1) * blocks)
+        first_ref[span, :] = jnp.where(even, high, low)
+        second_ref[span, :] = jnp.where(even, low, high)
+    last_faces = faces_ref[pl.ds(levels * ROWS + ROWS - 1, levels, stride=ROWS), :]
+    first_ref[3 * blocks : 3 * blocks + levels, :] = last_faces
+    second_ref[3 * blocks : 3 * blocks + levels, :] = last_faces
     squares = cells_ref.shape[0] // LANES
     for square in range(squares):
         turned = cells_ref[square * LANES : (square + 1) * LANES, :].T
@@ -138,7 +138,7 @@
         pack_kernel,
         out_shape=(
             jax.ShapeDtypeStruct((tiles, 1, 3 * LANES), jnp.float32),
-            jax.ShapeDtypeStruct((3 * blocks, LANES), jnp.float32),
+            jax.ShapeDtypeStruct((3 * blocks + levels, LANES), jnp.float32),
             jax.ShapeDtypeStruct((3 * blocks + levels, LANES), jnp.float32),
             jax.ShapeDtypeStruct((side_rows, LANES), jnp.float32),
             jax.ShapeDtypeStruct((side_rows, LANES), jnp.float32),
@@ -209,7 +209,7 @@
 
 
 def lat_kernel(
-    lat_ref, tracer_ref, courant_ref, mixing_ref, south_ref, north_ref,
+    lat_ref, tracer_ref, courant_ref, mixing_ref, swap_ref, next_swap_ref,
     sum_ref, response_ref, pivot_ref,
     rows_ref, weight_ref,
 ):
@@ -218,16 +218,17 @@
     members = blocks // levels
     half = levels * ROWS
     first = lat_ref[0] == 0
+    even = lax.rem(lat_ref[0], 2) == 0
     last = lat_ref[0] == lat_ref[1] - 1
 
     zero = jnp.zeros((blocks, LANES), jnp.float32)
     for step in range(3):
         span = slice(step * blocks, (step + 1) * blocks)
         rows_ref[pl.ds(5 + step, blocks, stride=PADDED_ROWS), :] = jnp.where(
-            first, zero, south_ref[span, :]
+            first, zero, jnp.where(even, next_swap_ref[span, :], swap_ref[span, :])
         )
         rows_ref[pl.ds(PADDED_ROWS + step, blocks, stride=PADDED_ROWS), :] = jnp.where(
-            last, zero, north_ref[span, :]
+            last, zero, jnp.where(even, swap_ref[span, :], next_swap_ref[span, :])
         )
     for block in range(blocks):
         rows_ref[block * PADDED_ROWS + 8 : block * PADDED_ROWS + 16, :] = tracer_ref[
@@ -236,7 +237,9 @@
     row = lax.broadcasted_iota(jnp.int32, (ROWS, LANES), 0)
     for level in range(levels):
         north_face = courant_ref[half + level * ROWS : half + (level + 1) * ROWS, :]
-        below = jnp.where(first, 0.0, south_ref[3 * blocks + level : 3 * blocks + level + 1, :])
+        place = slice(3 * blocks + level, 3 * blocks + level + 1)
+        below = jnp.where(even, next_swap_ref[place, :], swap_ref[place, :])
+        below = jnp.where(first, 0.0, below)
         south_face = jnp.where(row == 0, below, pltpu.roll(north_face, 1, 0))
         north_face = jnp.where(jnp.logical_and(last, row == ROWS - 1), 0.0, north_face)
         taps = divergence_weights(north_face, south_face)
@@ -418,7 +421,7 @@
 
 
 def advect_and_mix(
-    lat_place, tracer_rows, courant_rows, mixing, south, north, west, east, recv_cell
+    lat_place, tracer_rows, courant_rows, mixing, swap, next_swap, west, east, recv_cell
 ):
     levels, rows, lanes = mixing.shape[0] + 1, mixing.shape[1], mixing.shape[2]
     blocks = tracer_rows.shape[0] // rows
@@ -443,7 +446,7 @@
         compiler_params=params,
         cost_estimate=cost,
         name="advect_lat",
-    )(lat_place, tracer_rows, courant_rows, mixing, south, north)
+    )(lat_place, tracer_rows, courant_rows, mixing, swap, next_swap)
     sources, places = recv_cell.shape
     place_count = sources * places
     partial, leaf, place = pl.pallas_call(
@@ -634,17 +637,19 @@
     lon_count, lat_count = lax.axis_size("lon"), lax.axis_size("lat")
     tracer_rows = tracer.reshape(members * levels * row_count, column_count)
     courant_rows = courant.reshape(2 * levels * row_count, column_count)
-    outgoing, low, high, westward, eastward = pack(
+    outgoing, first, second, westward, eastward = pack(
         tracer_rows, courant_rows, forcing, plant_type, send_slot, lon_count * lat_count
     )
-    north = lax.ppermute(low, "lat", [((i + 1) % lat_count, i) for i in range(lat_count)])
-    south = lax.ppermute(high, "lat", [(i, (i + 1) % lat_count) for i in range(lat_count)])
+    pairs = [(i, i + 1) for i in range(0, lat_count, 2)]
+    next_pairs = [(i + 1, (i + 2) % lat_count) for i in range(0, lat_count, 2)]
+    swap = lax.ppermute(first, "lat", pairs + [(b, a) for a, b in pairs])
+    next_swap = lax.ppermute(second, "lat", next_pairs + [(b, a) for a, b in next_pairs])
     west = lax.ppermute(eastward, "lon", [(i, (i + 1) % lon_count) for i in range(lon_count)])
     east = lax.ppermute(westward, "lon", [((i + 1) % lon_count, i) for i in range(lon_count)])
     received = lax.all_to_all(outgoing, ("lat", "lon"), split_axis=0, concat_axis=0, tiled=True)
     lat_place = jnp.stack([lax.axis_index("lat"), jnp.int32(lat_count)]).astype(jnp.int32)
     partial, response, leaf, place = advect_and_mix(
-        lat_place, tracer_rows, courant_rows, mixing, south, north, west, east, recv_cell
+        lat_place, tracer_rows, courant_rows, mixing, swap, next_swap, west, east, recv_cell
     )
     return fluxes(received, land_params, leaf, place, partial, response)
 

time: 34.9 us -> 34.4 us (0.986)
    all_to_all x1, starting transfers between devices: 14.5 us -> 13.8 us  [per_device(): lax.all_to_all(outgoing, ('lat', 'lon'), split_axis=0, concat_axis=0, til...]
where the time goes in v5:
time: 34.4 us; the launch traced here: 33.8 us
  starting transfers between devices  22.3 us (65%)
  Pallas kernels  10 us (29%)
  between operations  0.73 us (2%)
  waiting for transfers between devices  0.57 us (2%)
    all_to_all x1, starting transfers between devices, per_device(): lax.all_to_all(outgoing, ('lat', 'lon'), split_axis=0, concat_axis=0, til...  13.8 us
    ppermute x1, starting transfers between devices, per_device(): lax.ppermute(westward, 'lon', [((i + 1) % lon_count, i) for i in range(lo...  4.18 us
    pallas_call x1, Pallas kernels, fluxes(): pl.pallas_call(flux_kernel, out_shape=(jax.ShapeDtypeStruct(partial.shape...  3.09 us
    pallas_call x1, Pallas kernels, advect_and_mix(): pl.pallas_call(lon_kernel, out_shape=(jax.ShapeDtypeStruct((members, leve...  2.69 us
    pallas_call x1, Pallas kernels, pack(): pl.pallas_call(pack_kernel, out_shape=(jax.ShapeDtypeStruct((tiles, 1, 3...  2.42 us
    ppermute x1, starting transfers between devices, per_device(): swap = lax.ppermute(first, 'lat', pairs + [(b, a) for a, b in pairs])  2.36 us
    pallas_call x1, Pallas kernels, advect_and_mix(): pl.pallas_call(lat_kernel, out_shape=(jax.ShapeDtypeStruct(tracer_rows.sh...  1.86 us
    ppermute x1, starting transfers between devices, per_device(): lax.ppermute(eastward, 'lon', [(i, (i + 1) % lon_count) for i in range(lo...  1.54 us
  transfers between devices with their start and end apart: 5, of which 2 were waited for; matrix products, arithmetic and copies ran while one was open for 0% of the time, Pallas kernels for 13%

profile of v5, /device:TPU:2, one launch (start us, length us, event | category | flops | bytes accessed | tf_op | source)
XLA Modules:
  0.0 33.8 jit_solution(6270036286885533194)
XLA Ops:
  0.6 0.0 copy-start
  0.6 2.4 %pack.1 = (f32[64,1,384]{2,1,0:T(1,128)}, f32[776,128]{1,0:T(8,128)S(1)}, f32[776,128]{1,0:T(8,128)S(1)}, f32[56,128]{1,0:T(8,128)S(1)}, f32[56,128]{1,0:T(8,128)S(1)}) custom-call(f32[2048,128]{1,0:T(8,128)} %bitcast.5, f32[128,128]{1,0:T(8,128)} %bitcast.8, f32[5,3072]{1,0:T(8,128)} %forcing_hbm.1, s32[1,3072]{1,0:T(1,128)} %bitcast.11, s32[1,3072]{1,0:T(1,128)} %bitcast.12), custom_call_target="tpu_custom_call" | custom-call | flops 300000000 | bytes 2500000 | tf_op jit(solution)/shard_map/pack/pallas_call | solution.py:137
  3.1 2.4 %collective-permute-start.2 = (f32[776,128]{1,0:T(8,128)S(1)}, f32[776,128]{1,0:T(8,128)S(1)}, u32[]{:S(2)}, u32[]{:S(2)}) collective-permute-start(f32[776,128]{1,0:T(8,128)S(1)} %get-tuple-element.16), channel_id=1, source_target_pairs={{0,4},{8,12},{4,0},{12,8},{1,5},{9,13},{5,1},{13,9},{2,6},{10,14},... | collective-permute-start | bytes 1191944 | tf_op jit(solution)/shard_map/ppermute | solution.py:645
  5.4 0.4 %collective-permute-start.3 = (f32[776,128]{1,0:T(8,128)S(1)}, f32[776,128]{1,0:T(8,128)S(1)}, u32[]{:S(2)}, u32[]{:S(2)}) collective-permute-start(f32[776,128]{1,0:T(8,128)S(1)} %get-tuple-element.17), channel_id=1, source_target_pairs={{4,8},{12,0},{8,4},{0,12},{5,9},{13,1},{9,5},{1,13},{6,10},{14,2},... | collective-permute-start | bytes 1191944 | tf_op jit(solution)/shard_map/ppermute | solution.py:646
  5.8 0.0 copy-start.4
  5.8 0.0 copy-start.3
  5.8 13.8 %all-to-all-start = ((f32[64,1,384]{2,1,0:T(1,128)}), f32[64,1,384]{2,1,0:T(1,128)S(1)}, u32[]{:S(2)}, u32[]{:S(2)}) async-start(f32[64,1,384]{2,1,0:T(1,128)} %get-tuple-element.13), calls=%async_computation | async-start | bytes 196608 | tf_op jit(solution)/shard_map/all_to_all | solution.py:649
  19.7 0.0 copy-start.1
  19.7 1.5 %collective-permute-start = (f32[56,128]{1,0:T(8,128)S(1)}, f32[56,128]{1,0:T(8,128)S(1)}, u32[]{:S(2)}, u32[]{:S(2)}) collective-permute-start(f32[56,128]{1,0:T(8,128)S(1)} %get-tuple-element.14), channel_id=1, source_target_pairs={{0,16},{16,32},{32,48},{48,64},{64,80},{80,96},{96,112},{112,128},... | collective-permute-start | bytes 86024 | tf_op jit(solution)/shard_map/ppermute | solution.py:647
  21.2 4.2 %collective-permute-start.1 = (f32[56,128]{1,0:T(8,128)S(1)}, f32[56,128]{1,0:T(8,128)S(1)}, u32[]{:S(2)}, u32[]{:S(2)}) collective-permute-start(f32[56,128]{1,0:T(8,128)S(1)} %get-tuple-element.15), channel_id=1, source_target_pairs={{16,0},{32,16},{48,32},{64,48},{80,64},{96,80},{112,96},{128,112},... | collective-permute-start | bytes 86024 | tf_op jit(solution)/shard_map/ppermute | solution.py:648
  25.4 0.1 pad_add_fusion.lat_ref
  25.5 0.0 copy-done.4
  25.5 0.1 copy.10.params_ref
  25.5 0.0 copy-start.2
  25.6 0.0 collective-permute-done.2.swap_ref
  25.6 0.0 collective-permute-done.3.next_swap_ref
  25.6 0.0 copy-done
  25.6 0.0 copy-done.3
  25.6 0.0 copy-done.1
  25.6 1.9 %advect_lat.1 = (f32[2048,128]{1,0:T(8,128)S(1)}, f32[8,8,128]{2,1,0:T(8,128)S(1)}, f32[8,3,8,128]{3,2,1,0:T(8,128)S(1)}) custom-call(s32[2]{0:T(128)S(1)} %pad_add_fusion.lat_ref, f32[2048,128]{1,0:T(8,128)S(1)} %bitcast.6, f32[128,128]{1,0:T(8,128)S(1)} %bitcast.9, f32[7,8,128]{2,1,0:T(8,128)S(1)} %copy-done.3, ...), custom_call_target="tpu_custom_call" | custom-call | flops 6000000 | bytes 4000000 | tf_op jit(solution)/shard_map/advect_lat/pallas_call | solution.py:433
  27.5 0.1 collective-permute-done.west_ref
  27.5 0.0 collective-permute-done.1.east_ref
  27.5 0.0 copy-done.2
  27.5 2.7 %advect_lon_and_mix.1 = (f32[32,8,8,128]{3,2,1,0:T(8,128)S(1)}, f32[32,4096]{1,0:T(8,128)S(1)}, f32[2,32,128]{2,1,0:T(8,128)S(1)}) custom-call(f32[2048,128]{1,0:T(8,128)S(1)} %bitcast.7, f32[128,128]{1,0:T(8,128)S(1)} %bitcast.10, f32[56,128]{1,0:T(8,128)S(1)} %collective-permute-done.west_ref, f32[56,128]{1,0:T(8,128)S(1)} %collective-permute-done.1.east_ref, ...), custom_call_target="tpu_custom_call" | custom-call | flops 6000000 | bytes 4000000 | tf_op jit(solution)/shard_map/advect_lon_and_mix/pallas_call | solution.py:452
  30.2 0.5 %all-to-all-done.received_ref = f32[64,1,384]{2,1,0:T(1,128)S(1)} async-done(((f32[64,1,384]{2,1,0:T(1,128)}), f32[64,1,384]{2,1,0:T(1,128)S(1)}, u32[]{:S(2)}, u32[]{:S(2)}) %all-to-all-start) | async-done | bytes 98336 | tf_op jit(solution)/shard_map/all_to_all | solution.py:649
  30.7 3.1 %fluxes.1 = (f32[32,8,8,128]{3,2,1,0:T(8,128)}, f32[32,8,128]{2,1,0:T(8,128)}) custom-call(f32[64,1,384]{2,1,0:T(1,128)S(1)} %all-to-all-done.received_ref, f32[3,32,16]{2,1,0:T(8,128)S(1)} %copy.10.params_ref, f32[32,4096]{1,0:T(8,128)S(1)} %get-tuple-element.20.leaf_ref, f32[2,32,128]{2,1,0:T(8,128)S(1)} %get-tuple-element.21.place_ref, ...), custom_call_target="tpu_custom_call" | custom-call | flops 600000000 | bytes 3000000 | tf_op jit(solution)/shard_map/fluxes/pallas_call | solution.py:616
Async XLA Ops:
  0.6 24.9 %copy-start = (f32[32,8,8,128]{3,2,1,0:T(8,128)S(1)}, f32[32,8,8,128]{3,2,1,0:T(8,128)}, u32[]{:S(2)}) copy-start(f32[32,8,8,128]{3,2,1,0:T(8,128)} %param.8) | copy-start | bytes 3145732
  3.1 22.5 %collective-permute-start.2 = (f32[776,128]{1,0:T(8,128)S(1)}, f32[776,128]{1,0:T(8,128)S(1)}, u32[]{:S(2)}, u32[]{:S(2)}) collective-permute-start(f32[776,128]{1,0:T(8,128)S(1)} %get-tuple-element.16), channel_id=1, source_target_pairs={{0,4},{8,12},{4,0},{12,8},{1,5},{9,13},{5,1},{13,9},{2,6},{10,14},... | collective-permute-start | bytes 1191944 | tf_op jit(solution)/shard_map/ppermute | solution.py:645
  5.4 20.1 %collective-permute-start.3 = (f32[776,128]{1,0:T(8,128)S(1)}, f32[776,128]{1,0:T(8,128)S(1)}, u32[]{:S(2)}, u32[]{:S(2)}) collective-permute-start(f32[776,128]{1,0:T(8,128)S(1)} %get-tuple-element.17), channel_id=1, source_target_pairs={{4,8},{12,0},{8,4},{0,12},{5,9},{13,1},{9,5},{1,13},{6,10},{14,2},... | collective-permute-start | bytes 1191944 | tf_op jit(solution)/shard_map/ppermute | solution.py:646
  5.8 19.6 %copy-start.4 = (f32[3,32,16]{1,2,0:T(8,128)S(1)}, f32[3,32,16]{1,2,0:T(8,128)}, u32[]{:S(2)}) copy-start(f32[3,32,16]{1,2,0:T(8,128)} %param.13) | copy-start | bytes 18436
  5.8 19.7 %copy-start.3 = (f32[7,8,128]{2,1,0:T(8,128)S(1)}, f32[7,8,128]{2,1,0:T(8,128)}, u32[]{:S(2)}) copy-start(f32[7,8,128]{2,1,0:T(8,128)} %mixing_ref.1) | copy-start | bytes 86020
  5.8 24.9 %all-to-all-start = ((f32[64,1,384]{2,1,0:T(1,128)}), f32[64,1,384]{2,1,0:T(1,128)S(1)}, u32[]{:S(2)}, u32[]{:S(2)}) async-start(f32[64,1,384]{2,1,0:T(1,128)} %get-tuple-element.13), calls=%async_computation | async-start | bytes 196608 | tf_op jit(solution)/shard_map/all_to_all | solution.py:649
  19.7 5.9 %copy-start.1 = (f32[2,8,8,128]{3,2,1,0:T(8,128)S(1)}, f32[2,8,8,128]{3,2,1,0:T(8,128)}, u32[]{:S(2)}) copy-start(f32[2,8,8,128]{3,2,1,0:T(8,128)} %param.9) | copy-start | bytes 196612
  19.7 7.8 %collective-permute-start = (f32[56,128]{1,0:T(8,128)S(1)}, f32[56,128]{1,0:T(8,128)S(1)}, u32[]{:S(2)}, u32[]{:S(2)}) collective-permute-start(f32[56,128]{1,0:T(8,128)S(1)} %get-tuple-element.14), channel_id=1, source_target_pairs={{0,16},{16,32},{32,48},{48,64},{64,80},{80,96},{96,112},{112,128},... | collective-permute-start | bytes 86024 | tf_op jit(solution)/shard_map/ppermute | solution.py:647
  21.2 6.3 %collective-permute-start.1 = (f32[56,128]{1,0:T(8,128)S(1)}, f32[56,128]{1,0:T(8,128)S(1)}, u32[]{:S(2)}, u32[]{:S(2)}) collective-permute-start(f32[56,128]{1,0:T(8,128)S(1)} %get-tuple-element.15), channel_id=1, source_target_pairs={{16,0},{32,16},{48,32},{64,48},{80,64},{96,80},{112,96},{128,112},... | collective-permute-start | bytes 86024 | tf_op jit(solution)/shard_map/ppermute | solution.py:648
  25.5 2.0 %copy-start.2 = (s32[64,64]{1,0:T(8,128)S(1)}, s32[64,64]{1,0:T(8,128)}, u32[]{:S(2)}) copy-start(s32[64,64]{1,0:T(8,128)} %cell_ref.1) | copy-start | bytes 49156

commit v6 on v5

--- a/solution.py
+++ b/solution.py
@@ -34,8 +34,8 @@
 
 def pack_kernel(
     tracer_hbm, courant_hbm, forcing_hbm, type_hbm, slot_hbm,
-    payload_ref, first_ref, second_ref, westward_ref, eastward_ref,
-    cells_ref, faces_ref, forcing_ref, type_ref, slot_ref, copy_sems,
+    payload_hbm, first_ref, second_ref, westward_ref, eastward_ref,
+    payload_ref, cells_ref, faces_ref, forcing_ref, type_ref, slot_ref, copy_sems,
 ):
     moves = (
         (slot_hbm, slot_ref),
@@ -103,6 +103,8 @@
                 joined = jnp.where(low_half, pltpu.roll(left, 64, 1), right)
             payload_ref[tile * 16 : (tile + 1) * 16, 0, pair * LANES : (pair + 1) * LANES] = joined
 
+    send = pltpu.make_async_copy(payload_ref, payload_hbm, copy_sems.at[5])
+    send.start()
     for copy in copies[3:5]:
         copy.wait()
     blocks = cells_ref.shape[0] // ROWS
@@ -125,6 +127,7 @@
     turned = faces_ref[...].T
     westward_ref[3 * squares : 3 * squares + ROWS, :] = turned[LANES - ROWS : LANES]
     eastward_ref[3 * squares : 3 * squares + ROWS, :] = turned[LANES - ROWS : LANES]
+    send.wait()
 
 
 def pack(tracer_rows, courant_rows, forcing, plant_type, send_slot, tiles):
@@ -144,14 +147,15 @@
             jax.ShapeDtypeStruct((side_rows, LANES), jnp.float32),
         ),
         in_specs=[hbm] * 5,
-        out_specs=(vmem,) * 5,
+        out_specs=(hbm,) + (vmem,) * 4,
         scratch_shapes=[
+            pltpu.VMEM((tiles, 1, 3 * LANES), jnp.float32),
             pltpu.VMEM(tracer_rows.shape, jnp.float32),
             pltpu.VMEM(courant_rows.shape, jnp.float32),
             pltpu.VMEM(forcing.shape, jnp.float32),
             pltpu.VMEM((1, columns), jnp.int32),
             pltpu.VMEM((1, columns), jnp.int32),
-            pltpu.SemaphoreType.DMA((5,)),
+            pltpu.SemaphoreType.DMA((6,)),
         ],
         compiler_params=pltpu.CompilerParams(vmem_limit_bytes=VMEM_BYTES),
         cost_estimate=pl.CostEstimate(

time: 34.4 us -> 34.4 us (level)
  no operation moved by 1% of the time
where the time goes in v6:
time: 34.4 us; the launch traced here: 33.8 us
  starting transfers between devices  22.3 us (65%)
  Pallas kernels  10 us (29%)
  between operations  0.73 us (2%)
  waiting for transfers between devices  0.57 us (2%)
    all_to_all x1, starting transfers between devices, per_device(): lax.all_to_all(outgoing, ('lat', 'lon'), split_axis=0, concat_axis=0, til...  13.8 us
    ppermute x1, starting transfers between devices, per_device(): lax.ppermute(westward, 'lon', [((i + 1) % lon_count, i) for i in range(lo...  4.18 us
    pallas_call x1, Pallas kernels, fluxes(): pl.pallas_call(flux_kernel, out_shape=(jax.ShapeDtypeStruct(partial.shape...  3.09 us
    pallas_call x1, Pallas kernels, advect_and_mix(): pl.pallas_call(lon_kernel, out_shape=(jax.ShapeDtypeStruct((members, leve...  2.69 us
    pallas_call x1, Pallas kernels, pack(): pl.pallas_call(pack_kernel, out_shape=(jax.ShapeDtypeStruct((tiles, 1, 3...  2.41 us
    ppermute x1, starting transfers between devices, per_device(): swap = lax.ppermute(first, 'lat', pairs + [(b, a) for a, b in pairs])  2.36 us
    pallas_call x1, Pallas kernels, advect_and_mix(): pl.pallas_call(lat_kernel, out_shape=(jax.ShapeDtypeStruct(tracer_rows.sh...  1.86 us
    ppermute x1, starting transfers between devices, per_device(): lax.ppermute(eastward, 'lon', [(i, (i + 1) % lon_count) for i in range(lo...  1.54 us
  transfers between devices with their start and end apart: 5, of which 2 were waited for; matrix products, arithmetic and copies ran while one was open for 0% of the time, Pallas kernels for 13%

profile of v6, /device:TPU:2, one launch (start us, length us, event | category | flops | bytes accessed | tf_op | source)
XLA Modules:
  0.0 33.8 jit_solution(5128228723461541543)
XLA Ops:
  0.6 0.0 copy-start
  0.6 2.4 %pack.1 = (f32[64,1,384]{2,1,0:T(1,128)}, f32[776,128]{1,0:T(8,128)S(1)}, f32[776,128]{1,0:T(8,128)S(1)}, f32[56,128]{1,0:T(8,128)S(1)}, f32[56,128]{1,0:T(8,128)S(1)}) custom-call(f32[2048,128]{1,0:T(8,128)} %bitcast.5, f32[128,128]{1,0:T(8,128)} %bitcast.8, f32[5,3072]{1,0:T(8,128)} %forcing_hbm.1, s32[1,3072]{1,0:T(1,128)} %bitcast.11, s32[1,3072]{1,0:T(1,128)} %bitcast.12), custom_call_target="tpu_custom_call" | custom-call | flops 300000000 | bytes 2500000 | tf_op jit(solution)/shard_map/pack/pallas_call | solution.py:140
  3.1 2.4 %collective-permute-start.2 = (f32[776,128]{1,0:T(8,128)S(1)}, f32[776,128]{1,0:T(8,128)S(1)}, u32[]{:S(2)}, u32[]{:S(2)}) collective-permute-start(f32[776,128]{1,0:T(8,128)S(1)} %get-tuple-element.16), channel_id=1, source_target_pairs={{0,4},{8,12},{4,0},{12,8},{1,5},{9,13},{5,1},{13,9},{2,6},{10,14},... | collective-permute-start | bytes 1191944 | tf_op jit(solution)/shard_map/ppermute | solution.py:649
  5.4 0.4 %collective-permute-start.3 = (f32[776,128]{1,0:T(8,128)S(1)}, f32[776,128]{1,0:T(8,128)S(1)}, u32[]{:S(2)}, u32[]{:S(2)}) collective-permute-start(f32[776,128]{1,0:T(8,128)S(1)} %get-tuple-element.17), channel_id=1, source_target_pairs={{4,8},{12,0},{8,4},{0,12},{5,9},{13,1},{9,5},{1,13},{6,10},{14,2},... | collective-permute-start | bytes 1191944 | tf_op jit(solution)/shard_map/ppermute | solution.py:650
  5.8 0.0 copy-start.4
  5.8 0.0 copy-start.3
  5.8 13.8 %all-to-all-start = ((f32[64,1,384]{2,1,0:T(1,128)}), f32[64,1,384]{2,1,0:T(1,128)S(1)}, u32[]{:S(2)}, u32[]{:S(2)}) async-start(f32[64,1,384]{2,1,0:T(1,128)} %get-tuple-element.13), calls=%async_computation | async-start | bytes 196608 | tf_op jit(solution)/shard_map/all_to_all | solution.py:653
  19.7 0.0 copy-start.1
  19.7 1.5 %collective-permute-start = (f32[56,128]{1,0:T(8,128)S(1)}, f32[56,128]{1,0:T(8,128)S(1)}, u32[]{:S(2)}, u32[]{:S(2)}) collective-permute-start(f32[56,128]{1,0:T(8,128)S(1)} %get-tuple-element.14), channel_id=1, source_target_pairs={{0,16},{16,32},{32,48},{48,64},{64,80},{80,96},{96,112},{112,128},... | collective-permute-start | bytes 86024 | tf_op jit(solution)/shard_map/ppermute | solution.py:651
  21.2 4.2 %collective-permute-start.1 = (f32[56,128]{1,0:T(8,128)S(1)}, f32[56,128]{1,0:T(8,128)S(1)}, u32[]{:S(2)}, u32[]{:S(2)}) collective-permute-start(f32[56,128]{1,0:T(8,128)S(1)} %get-tuple-element.15), channel_id=1, source_target_pairs={{16,0},{32,16},{48,32},{64,48},{80,64},{96,80},{112,96},{128,112},... | collective-permute-start | bytes 86024 | tf_op jit(solution)/shard_map/ppermute | solution.py:652
  25.4 0.1 pad_add_fusion.lat_ref
  25.5 0.0 copy-done.4
  25.5 0.1 copy.10.params_ref
  25.5 0.0 copy-start.2
  25.5 0.0 collective-permute-done.2.swap_ref
  25.6 0.0 collective-permute-done.3.next_swap_ref
  25.6 0.0 copy-done
  25.6 0.0 copy-done.3
  25.6 0.0 copy-done.1
  25.6 1.9 %advect_lat.1 = (f32[2048,128]{1,0:T(8,128)S(1)}, f32[8,8,128]{2,1,0:T(8,128)S(1)}, f32[8,3,8,128]{3,2,1,0:T(8,128)S(1)}) custom-call(s32[2]{0:T(128)S(1)} %pad_add_fusion.lat_ref, f32[2048,128]{1,0:T(8,128)S(1)} %bitcast.6, f32[128,128]{1,0:T(8,128)S(1)} %bitcast.9, f32[7,8,128]{2,1,0:T(8,128)S(1)} %copy-done.3, ...), custom_call_target="tpu_custom_call" | custom-call | flops 6000000 | bytes 4000000 | tf_op jit(solution)/shard_map/advect_lat/pallas_call | solution.py:437
  27.5 0.1 collective-permute-done.west_ref
  27.5 0.0 collective-permute-done.1.east_ref
  27.5 0.0 copy-done.2
  27.5 2.7 %advect_lon_and_mix.1 = (f32[32,8,8,128]{3,2,1,0:T(8,128)S(1)}, f32[32,4096]{1,0:T(8,128)S(1)}, f32[2,32,128]{2,1,0:T(8,128)S(1)}) custom-call(f32[2048,128]{1,0:T(8,128)S(1)} %bitcast.7, f32[128,128]{1,0:T(8,128)S(1)} %bitcast.10, f32[56,128]{1,0:T(8,128)S(1)} %collective-permute-done.west_ref, f32[56,128]{1,0:T(8,128)S(1)} %collective-permute-done.1.east_ref, ...), custom_call_target="tpu_custom_call" | custom-call | flops 6000000 | bytes 4000000 | tf_op jit(solution)/shard_map/advect_lon_and_mix/pallas_call | solution.py:456
  30.2 0.5 %all-to-all-done.received_ref = f32[64,1,384]{2,1,0:T(1,128)S(1)} async-done(((f32[64,1,384]{2,1,0:T(1,128)}), f32[64,1,384]{2,1,0:T(1,128)S(1)}, u32[]{:S(2)}, u32[]{:S(2)}) %all-to-all-start) | async-done | bytes 98336 | tf_op jit(solution)/shard_map/all_to_all | solution.py:653
  30.7 3.1 %fluxes.1 = (f32[32,8,8,128]{3,2,1,0:T(8,128)}, f32[32,8,128]{2,1,0:T(8,128)}) custom-call(f32[64,1,384]{2,1,0:T(1,128)S(1)} %all-to-all-done.received_ref, f32[3,32,16]{2,1,0:T(8,128)S(1)} %copy.10.params_ref, f32[32,4096]{1,0:T(8,128)S(1)} %get-tuple-element.20.leaf_ref, f32[2,32,128]{2,1,0:T(8,128)S(1)} %get-tuple-element.21.place_ref, ...), custom_call_target="tpu_custom_call" | custom-call | flops 600000000 | bytes 3000000 | tf_op jit(solution)/shard_map/fluxes/pallas_call | solution.py:620
Async XLA Ops:
  0.6 24.9 %copy-start = (f32[32,8,8,128]{3,2,1,0:T(8,128)S(1)}, f32[32,8,8,128]{3,2,1,0:T(8,128)}, u32[]{:S(2)}) copy-start(f32[32,8,8,128]{3,2,1,0:T(8,128)} %param.8) | copy-start | bytes 3145732
  3.1 22.5 %collective-permute-start.2 = (f32[776,128]{1,0:T(8,128)S(1)}, f32[776,128]{1,0:T(8,128)S(1)}, u32[]{:S(2)}, u32[]{:S(2)}) collective-permute-start(f32[776,128]{1,0:T(8,128)S(1)} %get-tuple-element.16), channel_id=1, source_target_pairs={{0,4},{8,12},{4,0},{12,8},{1,5},{9,13},{5,1},{13,9},{2,6},{10,14},... | collective-permute-start | bytes 1191944 | tf_op jit(solution)/shard_map/ppermute | solution.py:649
  5.4 20.1 %collective-permute-start.3 = (f32[776,128]{1,0:T(8,128)S(1)}, f32[776,128]{1,0:T(8,128)S(1)}, u32[]{:S(2)}, u32[]{:S(2)}) collective-permute-start(f32[776,128]{1,0:T(8,128)S(1)} %get-tuple-element.17), channel_id=1, source_target_pairs={{4,8},{12,0},{8,4},{0,12},{5,9},{13,1},{9,5},{1,13},{6,10},{14,2},... | collective-permute-start | bytes 1191944 | tf_op jit(solution)/shard_map/ppermute | solution.py:650
  5.8 19.6 %copy-start.4 = (f32[3,32,16]{1,2,0:T(8,128)S(1)}, f32[3,32,16]{1,2,0:T(8,128)}, u32[]{:S(2)}) copy-start(f32[3,32,16]{1,2,0:T(8,128)} %param.13) | copy-start | bytes 18436
  5.8 19.7 %copy-start.3 = (f32[7,8,128]{2,1,0:T(8,128)S(1)}, f32[7,8,128]{2,1,0:T(8,128)}, u32[]{:S(2)}) copy-start(f32[7,8,128]{2,1,0:T(8,128)} %mixing_ref.1) | copy-start | bytes 86020
  5.8 24.9 %all-to-all-start = ((f32[64,1,384]{2,1,0:T(1,128)}), f32[64,1,384]{2,1,0:T(1,128)S(1)}, u32[]{:S(2)}, u32[]{:S(2)}) async-start(f32[64,1,384]{2,1,0:T(1,128)} %get-tuple-element.13), calls=%async_computation | async-start | bytes 196608 | tf_op jit(solution)/shard_map/all_to_all | solution.py:653
  19.7 5.9 %copy-start.1 = (f32[2,8,8,128]{3,2,1,0:T(8,128)S(1)}, f32[2,8,8,128]{3,2,1,0:T(8,128)}, u32[]{:S(2)}) copy-start(f32[2,8,8,128]{3,2,1,0:T(8,128)} %param.9) | copy-start | bytes 196612
  19.7 7.8 %collective-permute-start = (f32[56,128]{1,0:T(8,128)S(1)}, f32[56,128]{1,0:T(8,128)S(1)}, u32[]{:S(2)}, u32[]{:S(2)}) collective-permute-start(f32[56,128]{1,0:T(8,128)S(1)} %get-tuple-element.14), channel_id=1, source_target_pairs={{0,16},{16,32},{32,48},{48,64},{64,80},{80,96},{96,112},{112,128},... | collective-permute-start | bytes 86024 | tf_op jit(solution)/shard_map/ppermute | solution.py:651
  21.2 6.3 %collective-permute-start.1 = (f32[56,128]{1,0:T(8,128)S(1)}, f32[56,128]{1,0:T(8,128)S(1)}, u32[]{:S(2)}, u32[]{:S(2)}) collective-permute-start(f32[56,128]{1,0:T(8,128)S(1)} %get-tuple-element.15), channel_id=1, source_target_pairs={{16,0},{32,16},{48,32},{64,48},{80,64},{96,80},{112,96},{128,112},... | collective-permute-start | bytes 86024 | tf_op jit(solution)/shard_map/ppermute | solution.py:652
  25.5 2.0 %copy-start.2 = (s32[64,64]{1,0:T(8,128)S(1)}, s32[64,64]{1,0:T(8,128)}, u32[]{:S(2)}) copy-start(s32[64,64]{1,0:T(8,128)} %cell_ref.1) | copy-start | bytes 49156

commit v7 on v5

--- a/solution.py
+++ b/solution.py
@@ -34,7 +34,7 @@
 
 def pack_kernel(
     tracer_hbm, courant_hbm, forcing_hbm, type_hbm, slot_hbm,
-    payload_ref, first_ref, second_ref, westward_ref, eastward_ref,
+    payload_ref, first_ref, second_ref, side_next_ref, side_first_ref,
     cells_ref, faces_ref, forcing_ref, type_ref, slot_ref, copy_sems,
 ):
     moves = (
@@ -108,6 +108,7 @@
     blocks = cells_ref.shape[0] // ROWS
     levels = faces_ref.shape[0] // (2 * ROWS)
     even = lax.rem(lax.axis_index("lat"), 2) == 0
+    even_lon = lax.rem(lax.axis_index("lon"), 2) == 0
     for step in range(3):
         low = cells_ref[pl.ds(step, blocks, stride=ROWS), :]
         high = cells_ref[pl.ds(ROWS - 3 + step, blocks, stride=ROWS), :]
@@ -120,11 +121,12 @@
     squares = cells_ref.shape[0] // LANES
     for square in range(squares):
         turned = cells_ref[square * LANES : (square + 1) * LANES, :].T
-        westward_ref[3 * square : 3 * square + 3, :] = turned[0:3]
-        eastward_ref[3 * square : 3 * square + 3, :] = turned[LANES - 3 : LANES]
+        low, high = turned[0:3], turned[LANES - 3 : LANES]
+        side_next_ref[3 * square : 3 * square + 3, :] = jnp.where(even_lon, low, high)
+        side_first_ref[3 * square : 3 * square + 3, :] = jnp.where(even_lon, high, low)
     turned = faces_ref[...].T
-    westward_ref[3 * squares : 3 * squares + ROWS, :] = turned[LANES - ROWS : LANES]
-    eastward_ref[3 * squares : 3 * squares + ROWS, :] = turned[LANES - ROWS : LANES]
+    side_next_ref[3 * squares : 3 * squares + ROWS, :] = turned[LANES - ROWS : LANES]
+    side_first_ref[3 * squares : 3 * squares + ROWS, :] = turned[LANES - ROWS : LANES]
 
 
 def pack(tracer_rows, courant_rows, forcing, plant_type, send_slot, tiles):
@@ -291,19 +293,23 @@
 
 
 def lon_kernel(
-    tracer_ref, courant_ref, west_ref, east_ref, sum_ref, pivot_ref, cell_ref,
+    tracer_ref, courant_ref, side_ref, side_next_ref, sum_ref, pivot_ref, cell_ref,
     out_ref, leaf_ref, place_ref,
     turned_ref, turned_sum_ref, turned_courant_ref, lon_ref,
 ):
     members, levels = out_ref.shape[0], out_ref.shape[1]
     squares = tracer_ref.shape[0] // LANES
 
+    even = lax.rem(lax.axis_index("lon"), 2) == 0
     for square in range(squares):
         base = square * TURNED_ROWS
-        turned_ref[base + 5 : base + 8, :] = west_ref[3 * square : 3 * square + 3, :]
-        turned_ref[base + 8 + LANES : base + 11 + LANES, :] = east_ref[
-            3 * square : 3 * square + 3, :
-        ]
+        span = slice(3 * square, 3 * square + 3)
+        turned_ref[base + 5 : base + 8, :] = jnp.where(
+            even, side_next_ref[span, :], side_ref[span, :]
+        )
+        turned_ref[base + 8 + LANES : base + 11 + LANES, :] = jnp.where(
+            even, side_ref[span, :], side_next_ref[span, :]
+        )
         turned_ref[base + 8 : base + 8 + LANES, :] = tracer_ref[
             square * LANES : (square + 1) * LANES, :
         ].T
@@ -312,7 +318,8 @@
     low_half = lax.broadcasted_iota(jnp.int32, (LANES, LANES), 1) < half
     turned_faces = jnp.where(low_half, turned_faces, pltpu.roll(turned_faces, half, 1))
     turned_courant_ref[8 : 8 + LANES, :] = turned_faces
-    side_face = west_ref[3 * squares : 3 * squares + ROWS, :]
+    span = slice(3 * squares, 3 * squares + ROWS)
+    side_face = jnp.where(even, side_next_ref[span, :], side_ref[span, :])
     side_face = jnp.where(low_half[0:ROWS], side_face, pltpu.roll(side_face, half, 1))
     turned_courant_ref[0:8, :] = side_face
 
@@ -421,7 +428,7 @@
 
 
 def advect_and_mix(
-    lat_place, tracer_rows, courant_rows, mixing, swap, next_swap, west, east, recv_cell
+    lat_place, tracer_rows, courant_rows, mixing, swap, next_swap, side_swap, side_swap_next, recv_cell
 ):
     levels, rows, lanes = mixing.shape[0] + 1, mixing.shape[1], mixing.shape[2]
     blocks = tracer_rows.shape[0] // rows
@@ -467,7 +474,7 @@
         compiler_params=params,
         cost_estimate=cost,
         name="advect_lon_and_mix",
-    )(tracer_rows, courant_rows, west, east, lat_sum, pivots, recv_cell)
+    )(tracer_rows, courant_rows, side_swap, side_swap_next, lat_sum, pivots, recv_cell)
     return partial, response, leaf, place
 
 
@@ -637,19 +644,21 @@
     lon_count, lat_count = lax.axis_size("lon"), lax.axis_size("lat")
     tracer_rows = tracer.reshape(members * levels * row_count, column_count)
     courant_rows = courant.reshape(2 * levels * row_count, column_count)
-    outgoing, first, second, westward, eastward = pack(
+    outgoing, first, second, side_next, side_first = pack(
         tracer_rows, courant_rows, forcing, plant_type, send_slot, lon_count * lat_count
     )
     pairs = [(i, i + 1) for i in range(0, lat_count, 2)]
     next_pairs = [(i + 1, (i + 2) % lat_count) for i in range(0, lat_count, 2)]
     swap = lax.ppermute(first, "lat", pairs + [(b, a) for a, b in pairs])
     next_swap = lax.ppermute(second, "lat", next_pairs + [(b, a) for a, b in next_pairs])
-    west = lax.ppermute(eastward, "lon", [(i, (i + 1) % lon_count) for i in range(lon_count)])
-    east = lax.ppermute(westward, "lon", [((i + 1) % lon_count, i) for i in range(lon_count)])
+    pairs = [(i, i + 1) for i in range(0, lon_count, 2)]
+    next_pairs = [(i + 1, (i + 2) % lon_count) for i in range(0, lon_count, 2)]
+    side_swap = lax.ppermute(side_first, "lon", pairs + [(b, a) for a, b in pairs])
+    side_swap_next = lax.ppermute(side_next, "lon", next_pairs + [(b, a) for a, b in next_pairs])
     received = lax.all_to_all(outgoing, ("lat", "lon"), split_axis=0, concat_axis=0, tiled=True)
     lat_place = jnp.stack([lax.axis_index("lat"), jnp.int32(lat_count)]).astype(jnp.int32)
     partial, response, leaf, place = advect_and_mix(
-        lat_place, tracer_rows, courant_rows, mixing, swap, next_swap, west, east, recv_cell
+        lat_place, tracer_rows, courant_rows, mixing, swap, next_swap, side_swap, side_swap_next, recv_cell
     )
     return fluxes(received, land_params, leaf, place, partial, response)
 

time: 34.4 us -> 35 us (1.017)
  starting transfers between devices: 22.3 us -> 23.3 us
    ppermute x2, starting transfers between devices: 5.72 us -> 6.7 us  [the longest x1 5.15 us: per_device(): lax.ppermute(side_next, 'lon', next_pairs + [(b, a) for a, b in next_pairs])]
    all_to_all x1, waiting for transfers between devices: 0.51 us -> 0.01 us  [per_device(): lax.all_to_all(outgoing, ('lat', 'lon'), split_axis=0, concat_axis=0, til...]
  transfers between devices with their start and end apart: 5 -> 5, of which waited for: 2 -> 1; matrix products, arithmetic and copies ran while one was open for 0% -> 0% of each run, Pallas kernels for 13% -> 13%
where the time goes in v7:
time: 35 us; the launch traced here: 34.6 us
  starting transfers between devices  23.3 us (67%)
  Pallas kernels  10 us (29%)
  between operations  0.74 us (2%)
    all_to_all x1, starting transfers between devices, per_device(): lax.all_to_all(outgoing, ('lat', 'lon'), split_axis=0, concat_axis=0, til...  13.8 us
    ppermute x1, starting transfers between devices, per_device(): lax.ppermute(side_next, 'lon', next_pairs + [(b, a) for a, b in next_pairs])  5.15 us
    pallas_call x1, Pallas kernels, fluxes(): pl.pallas_call(flux_kernel, out_shape=(jax.ShapeDtypeStruct(partial.shape...  3.09 us
    pallas_call x1, Pallas kernels, advect_and_mix(): pl.pallas_call(lon_kernel, out_shape=(jax.ShapeDtypeStruct((members, leve...  2.68 us
    pallas_call x1, Pallas kernels, pack(): pl.pallas_call(pack_kernel, out_shape=(jax.ShapeDtypeStruct((tiles, 1, 3...  2.42 us
    ppermute x1, starting transfers between devices, per_device(): swap = lax.ppermute(first, 'lat', pairs + [(b, a) for a, b in pairs])  2.36 us
    pallas_call x1, Pallas kernels, advect_and_mix(): pl.pallas_call(lat_kernel, out_shape=(jax.ShapeDtypeStruct(tracer_rows.sh...  1.86 us
    ppermute x1, starting transfers between devices, per_device(): lax.ppermute(side_first, 'lon', pairs + [(b, a) for a, b in pairs])  1.55 us
  transfers between devices with their start and end apart: 5, of which 1 were waited for; matrix products, arithmetic and copies ran while one was open for 0% of the time, Pallas kernels for 13%

profile of v7, /device:TPU:2, one launch (start us, length us, event | category | flops | bytes accessed | tf_op | source)
XLA Modules:
  0.0 34.6 jit_solution(4409756788751761374)
XLA Ops:
  0.6 0.0 copy-start
  0.6 2.4 %pack.1 = (f32[64,1,384]{2,1,0:T(1,128)}, f32[776,128]{1,0:T(8,128)S(1)}, f32[776,128]{1,0:T(8,128)S(1)}, f32[56,128]{1,0:T(8,128)S(1)}, f32[56,128]{1,0:T(8,128)S(1)}) custom-call(f32[2048,128]{1,0:T(8,128)} %bitcast.5, f32[128,128]{1,0:T(8,128)} %bitcast.8, f32[5,3072]{1,0:T(8,128)} %forcing_hbm.1, s32[1,3072]{1,0:T(1,128)} %bitcast.11, s32[1,3072]{1,0:T(1,128)} %bitcast.12), custom_call_target="tpu_custom_call" | custom-call | flops 300000000 | bytes 2500000 | tf_op jit(solution)/shard_map/pack/pallas_call | solution.py:139
  3.1 2.4 %collective-permute-start.2 = (f32[776,128]{1,0:T(8,128)S(1)}, f32[776,128]{1,0:T(8,128)S(1)}, u32[]{:S(2)}, u32[]{:S(2)}) collective-permute-start(f32[776,128]{1,0:T(8,128)S(1)} %get-tuple-element.16), channel_id=1, source_target_pairs={{0,4},{8,12},{4,0},{12,8},{1,5},{9,13},{5,1},{13,9},{2,6},{10,14},... | collective-permute-start | bytes 1191944 | tf_op jit(solution)/shard_map/ppermute | solution.py:652
  5.4 0.4 %collective-permute-start.3 = (f32[776,128]{1,0:T(8,128)S(1)}, f32[776,128]{1,0:T(8,128)S(1)}, u32[]{:S(2)}, u32[]{:S(2)}) collective-permute-start(f32[776,128]{1,0:T(8,128)S(1)} %get-tuple-element.17), channel_id=1, source_target_pairs={{4,8},{12,0},{8,4},{0,12},{5,9},{13,1},{9,5},{1,13},{6,10},{14,2},... | collective-permute-start | bytes 1191944 | tf_op jit(solution)/shard_map/ppermute | solution.py:653
  5.8 0.0 copy-start.4
  5.8 0.0 copy-start.3
  5.8 13.8 %all-to-all-start = ((f32[64,1,384]{2,1,0:T(1,128)}), f32[64,1,384]{2,1,0:T(1,128)S(1)}, u32[]{:S(2)}, u32[]{:S(2)}) async-start(f32[64,1,384]{2,1,0:T(1,128)} %get-tuple-element.13), calls=%async_computation | async-start | bytes 196608 | tf_op jit(solution)/shard_map/all_to_all | solution.py:658
  19.7 0.0 copy-start.1
  19.7 1.6 %collective-permute-start = (f32[56,128]{1,0:T(8,128)S(1)}, f32[56,128]{1,0:T(8,128)S(1)}, u32[]{:S(2)}, u32[]{:S(2)}) collective-permute-start(f32[56,128]{1,0:T(8,128)S(1)} %get-tuple-element.14), channel_id=1, source_target_pairs={{0,16},{32,48},{64,80},{96,112},{128,144},{160,176},{192,208},{224... | collective-permute-start | bytes 86024 | tf_op jit(solution)/shard_map/ppermute | solution.py:656
  21.2 5.2 %collective-permute-start.1 = (f32[56,128]{1,0:T(8,128)S(1)}, f32[56,128]{1,0:T(8,128)S(1)}, u32[]{:S(2)}, u32[]{:S(2)}) collective-permute-start(f32[56,128]{1,0:T(8,128)S(1)} %get-tuple-element.15), channel_id=1, source_target_pairs={{16,32},{48,64},{80,96},{112,128},{144,160},{176,192},{208,224},{2... | collective-permute-start | bytes 86024 | tf_op jit(solution)/shard_map/ppermute | solution.py:657
  26.4 0.1 pad_add_fusion.lat_ref
  26.5 0.0 copy-done.4
  26.5 0.1 copy.10.params_ref
  26.5 0.0 copy-start.2
  26.5 0.0 collective-permute-done.2.swap_ref
  26.6 0.0 collective-permute-done.3.next_swap_ref
  26.6 0.0 copy-done
  26.6 0.0 copy-done.3
  26.6 0.0 copy-done.1
  26.6 1.9 %advect_lat.1 = (f32[2048,128]{1,0:T(8,128)S(1)}, f32[8,8,128]{2,1,0:T(8,128)S(1)}, f32[8,3,8,128]{3,2,1,0:T(8,128)S(1)}) custom-call(s32[2]{0:T(128)S(1)} %pad_add_fusion.lat_ref, f32[2048,128]{1,0:T(8,128)S(1)} %bitcast.6, f32[128,128]{1,0:T(8,128)S(1)} %bitcast.9, f32[7,8,128]{2,1,0:T(8,128)S(1)} %copy-done.3, ...), custom_call_target="tpu_custom_call" | custom-call | flops 6000000 | bytes 4000000 | tf_op jit(solution)/shard_map/advect_lat/pallas_call | solution.py:440
  28.5 0.0 collective-permute-done.side_ref
  28.5 0.3 collective-permute-done.1.side_next_ref
  28.8 0.0 copy-done.2
  28.8 2.7 %advect_lon_and_mix.1 = (f32[32,8,8,128]{3,2,1,0:T(8,128)S(1)}, f32[32,4096]{1,0:T(8,128)S(1)}, f32[2,32,128]{2,1,0:T(8,128)S(1)}) custom-call(f32[2048,128]{1,0:T(8,128)S(1)} %bitcast.7, f32[128,128]{1,0:T(8,128)S(1)} %bitcast.10, f32[56,128]{1,0:T(8,128)S(1)} %collective-permute-done.side_ref, f32[56,128]{1,0:T(8,128)S(1)} %collective-permute-done.1.side_next_ref, ...), custom_call_target="tpu_custom_call" | custom-call | flops 6000000 | bytes 4000000 | tf_op jit(solution)/shard_map/advect_lon_and_mix/pallas_call | solution.py:459
  31.5 0.0 all-to-all-done.received_ref
  31.5 3.1 %fluxes.1 = (f32[32,8,8,128]{3,2,1,0:T(8,128)}, f32[32,8,128]{2,1,0:T(8,128)}) custom-call(f32[64,1,384]{2,1,0:T(1,128)S(1)} %all-to-all-done.received_ref, f32[3,32,16]{2,1,0:T(8,128)S(1)} %copy.10.params_ref, f32[32,4096]{1,0:T(8,128)S(1)} %get-tuple-element.20.leaf_ref, f32[2,32,128]{2,1,0:T(8,128)S(1)} %get-tuple-element.21.place_ref, ...), custom_call_target="tpu_custom_call" | custom-call | flops 600000000 | bytes 3000000 | tf_op jit(solution)/shard_map/fluxes/pallas_call | solution.py:623
Async XLA Ops:
  0.6 25.9 %copy-start = (f32[32,8,8,128]{3,2,1,0:T(8,128)S(1)}, f32[32,8,8,128]{3,2,1,0:T(8,128)}, u32[]{:S(2)}) copy-start(f32[32,8,8,128]{3,2,1,0:T(8,128)} %param.8) | copy-start | bytes 3145732
  3.1 23.5 %collective-permute-start.2 = (f32[776,128]{1,0:T(8,128)S(1)}, f32[776,128]{1,0:T(8,128)S(1)}, u32[]{:S(2)}, u32[]{:S(2)}) collective-permute-start(f32[776,128]{1,0:T(8,128)S(1)} %get-tuple-element.16), channel_id=1, source_target_pairs={{0,4},{8,12},{4,0},{12,8},{1,5},{9,13},{5,1},{13,9},{2,6},{10,14},... | collective-permute-start | bytes 1191944 | tf_op jit(solution)/shard_map/ppermute | solution.py:652
  5.4 21.1 %collective-permute-start.3 = (f32[776,128]{1,0:T(8,128)S(1)}, f32[776,128]{1,0:T(8,128)S(1)}, u32[]{:S(2)}, u32[]{:S(2)}) collective-permute-start(f32[776,128]{1,0:T(8,128)S(1)} %get-tuple-element.17), channel_id=1, source_target_pairs={{4,8},{12,0},{8,4},{0,12},{5,9},{13,1},{9,5},{1,13},{6,10},{14,2},... | collective-permute-start | bytes 1191944 | tf_op jit(solution)/shard_map/ppermute | solution.py:653
  5.8 20.6 %copy-start.4 = (f32[3,32,16]{1,2,0:T(8,128)S(1)}, f32[3,32,16]{1,2,0:T(8,128)}, u32[]{:S(2)}) copy-start(f32[3,32,16]{1,2,0:T(8,128)} %param.13) | copy-start | bytes 18436
  5.8 20.7 %copy-start.3 = (f32[7,8,128]{2,1,0:T(8,128)S(1)}, f32[7,8,128]{2,1,0:T(8,128)}, u32[]{:S(2)}) copy-start(f32[7,8,128]{2,1,0:T(8,128)} %mixing_ref.1) | copy-start | bytes 86020
  5.8 25.6 %all-to-all-start = ((f32[64,1,384]{2,1,0:T(1,128)}), f32[64,1,384]{2,1,0:T(1,128)S(1)}, u32[]{:S(2)}, u32[]{:S(2)}) async-start(f32[64,1,384]{2,1,0:T(1,128)} %get-tuple-element.13), calls=%async_computation | async-start | bytes 196608 | tf_op jit(solution)/shard_map/all_to_all | solution.py:658
  19.7 6.9 %copy-start.1 = (f32[2,8,8,128]{3,2,1,0:T(8,128)S(1)}, f32[2,8,8,128]{3,2,1,0:T(8,128)}, u32[]{:S(2)}) copy-start(f32[2,8,8,128]{3,2,1,0:T(8,128)} %param.9) | copy-start | bytes 196612
  19.7 8.8 %collective-permute-start = (f32[56,128]{1,0:T(8,128)S(1)}, f32[56,128]{1,0:T(8,128)S(1)}, u32[]{:S(2)}, u32[]{:S(2)}) collective-permute-start(f32[56,128]{1,0:T(8,128)S(1)} %get-tuple-element.14), channel_id=1, source_target_pairs={{0,16},{32,48},{64,80},{96,112},{128,144},{160,176},{192,208},{224... | collective-permute-start | bytes 86024 | tf_op jit(solution)/shard_map/ppermute | solution.py:656
  21.2 7.5 %collective-permute-start.1 = (f32[56,128]{1,0:T(8,128)S(1)}, f32[56,128]{1,0:T(8,128)S(1)}, u32[]{:S(2)}, u32[]{:S(2)}) collective-permute-start(f32[56,128]{1,0:T(8,128)S(1)} %get-tuple-element.15), channel_id=1, source_target_pairs={{16,32},{48,64},{80,96},{112,128},{144,160},{176,192},{208,224},{2... | collective-permute-start | bytes 86024 | tf_op jit(solution)/shard_map/ppermute | solution.py:657
  26.5 2.2 %copy-start.2 = (s32[64,64]{1,0:T(8,128)S(1)}, s32[64,64]{1,0:T(8,128)}, u32[]{:S(2)}) copy-start(s32[64,64]{1,0:T(8,128)} %cell_ref.1) | copy-start | bytes 49156
